TPU v7x, 32 devices: a whole 2x2x4 slice. The times are simulated.
32 devices in a mesh: seq: 8 (over z, x), group: 4 (over y, core).
Axes of the slice: x: 2, y: 2, z: 4, core: 2. Of those that a mesh axis runs over, the one named last changes fastest.
Arguments:
- tokens: bfloat16 [4, 4096, 768], P('group', 'seq'), may hold values from -6 to 6
- cotangent: bfloat16 [4, 4096, 768], P('group', 'seq'), may hold values from -6 to 6
- skip_table: int32 [4, 16, 16], P('group'), may hold values from 0 to 1, as said below
- gain_attn: float32 [768], replicated, may hold values from 0.5 to 1.5
- w_attn: bfloat16 [768, 3072], replicated, may hold values from -0.21875 to 0.21875
- w_heads: bfloat16 [768, 36], replicated, may hold values from -0.21875 to 0.21875
- forget_bias: float32 [12], replicated, may hold values from 3 to 10
- query_gain: float32 [768], replicated, may hold values from 0.1 to 1.9
- key_gain: float32 [768], replicated, may hold values from 0.1 to 1.9
- w_out: bfloat16 [768, 768], replicated, may hold values from -0.875 to 0.875
- gain_ffn: float32 [768], replicated, may hold values from 0.4 to 1.6
- w_gate_up: bfloat16 [768, 4096], replicated, may hold values from -0.21875 to 0.21875
- w_down: bfloat16 [2048, 768], replicated, may hold values from -0.125 to 0.125
Outputs:
- activations: bfloat16 [4, 4096, 768], P('group', 'seq')
- grad_tokens: float32 [4, 4096, 768], P('group', 'seq')
- grad_gain_attn: float32 [768], replicated
- grad_w_attn: float32 [768, 3072], replicated
- grad_w_heads: float32 [768, 36], replicated
- grad_forget_bias: float32 [12], replicated
- grad_query_gain: float32 [768], replicated
- grad_key_gain: float32 [768], replicated
- grad_w_out: float32 [768, 768], replicated
- grad_gain_ffn: float32 [768], replicated
- grad_w_gate_up: float32 [768, 4096], replicated
- grad_w_down: float32 [2048, 768], replicated
Inputs may be any that keep to these rules, and one draw needn't show every extreme that they name: `skip_table`: 1 marks a key block that a query block drops; only key blocks two or more before the query block are dropped, and the last query block of every group drops none.
All inputs are finite; a program needn't handle non-finite values.
Results may differ from a plain program's by a relative error of at most 0.019.
Values may be sent and summed in bfloat16 or wider, within the bound.
A program may use at most 384 MiB of HBM per device.

v0:
```python
import jax
import jax.numpy as jnp
from jax import lax
from jax.sharding import PartitionSpec as P

D = 768
HEADS = 12
HDIM = 64
FF = 2048


NEG = -1e30
EPS = 1e-06


def padded_2(block, sides, width):
    for axis, dim in sides:
        count = lax.axis_size(axis)
        forward = [(i, i + 1) for i in range(count - 1)]
        backward = [(target, source) for source, target in forward]
        low = lax.ppermute(
            lax.slice_in_dim(block, block.shape[dim] - width, None, axis=dim), axis, forward
        )
        high = lax.ppermute(lax.slice_in_dim(block, 0, width, axis=dim), axis, backward)
        block = jnp.concatenate([low, block, high], axis=dim)
    return block


def rms_scale(values, gains):
    inverse = lax.rsqrt(jnp.mean(values * values, axis=-1, keepdims=True) + EPS)
    return values * inverse * gains


def head_scale(values, gains):
    shaped = values.reshape(values.shape[0], HEADS, HDIM)
    inverse = lax.rsqrt(jnp.mean(shaped * shaped, axis=-1, keepdims=True) + EPS)
    return (shaped * inverse).reshape(values.shape) * gains


def mixing(raw_rows, previous, shift_logits):
    block_rows = raw_rows.shape[0] // 2
    before = jnp.concatenate(
        [previous[0:1], raw_rows[: block_rows - 1], previous[1:2], raw_rows[block_rows:-1]], 0
    )
    shift_rate = jnp.repeat(jax.nn.sigmoid(shift_logits), HDIM, axis=1)
    return raw_rows + shift_rate * (before - raw_rows)


def swiglu(gate_up):
    return jax.nn.silu(gate_up[:, :FF]) * gate_up[:, FF:]


def to_group(values, seq_count):
    shaped = values.reshape((seq_count, 2, -1) + values.shape[1:])
    joined = jnp.concatenate([shaped[:, 0], shaped[::-1, 1]], 0)
    return joined.reshape(values.shape)


def to_device(values, seq_count):
    middle = values.shape[0] // 2
    front = values[:middle].reshape((seq_count, -1) + values.shape[1:])
    back_part = values[middle:].reshape((seq_count, -1) + values.shape[1:])[::-1]
    return jnp.stack([front, back_part], 1).reshape(values.shape)


def keep_same(carried):
    return carried


def local(
    tokens,
    cotangent,
    skip_table,
    gain_attn,
    w_attn,
    w_heads,
    forget_bias,
    query_gain,
    key_gain,
    w_out,
    gain_ffn,
    w_gate_up,
    w_down,
):
    seq_count = lax.axis_size("seq")
    my_place = lax.axis_index("seq")
    rows_here = tokens.shape[1]
    block_rows = rows_here // 2
    blocks = 2 * seq_count
    seq_total = blocks * block_rows
    score_scale = HDIM ** (-0.5)
    f32 = jnp.float32
    bf16 = jnp.bfloat16
    inputs = tokens[0].astype(f32)
    pruning = skip_table[0]
    last_block = blocks - 1 - my_place
    row_first = lax.dynamic_index_in_dim(pruning, my_place, 0, keepdims=False)
    row_last = lax.dynamic_index_in_dim(pruning, last_block, 0, keepdims=False)
    local_rows = jnp.arange(rows_here, dtype=jnp.int32)
    in_first = local_rows < block_rows
    own_blocks = jnp.where(in_first, my_place, last_block)
    query_pos = own_blocks * block_rows + local_rows % block_rows
    normed_attn, norm_back_attn = jax.vjp(rms_scale, inputs, gain_attn)
    h_first = normed_attn.astype(bf16)
    projected = jnp.dot(h_first, w_attn, preferred_element_type=f32)
    head_logits = jnp.dot(h_first, w_heads, preferred_element_type=f32)
    kv_raw = projected[:, D : 3 * D]
    seam_rows = jnp.stack([kv_raw[rows_here - 1], kv_raw[block_rows - 1]])
    padded = padded_2(seam_rows, (("seq", 0),), 1)
    previous = jnp.stack([padded[0], jnp.where(my_place == seq_count - 1, seam_rows[1], padded[3])])
    kv_mixed, mix_back = jax.vjp(mixing, kv_raw, previous, head_logits[:, HEADS:])
    query_norm, query_back = jax.vjp(head_scale, projected[:, :D], query_gain)
    key_norm, key_back = jax.vjp(head_scale, kv_mixed[:, :D], key_gain)
    query_low = query_norm.astype(bf16)
    key_low = key_norm.astype(bf16)
    value_low = kv_mixed[:, D:].astype(bf16)
    forget_in = head_logits[:, :HEADS] + forget_bias
    log_forget = jax.nn.log_sigmoid(forget_in)
    all_logs = lax.all_gather(log_forget, "seq", axis=0, tiled=True)
    cum_all = to_device(jnp.cumsum(to_group(all_logs, seq_count), axis=0), seq_count)
    cum_own = lax.dynamic_slice_in_dim(cum_all, my_place * rows_here, rows_here, 0)
    keys_all, values_all = (
        lax.all_gather(key_low, "seq", axis=0, tiled=True),
        lax.all_gather(value_low, "seq", axis=0, tiled=True),
    )
    query_heads = query_low.reshape(rows_here, HEADS, HDIM)
    cum_blocks = cum_all.reshape(blocks, block_rows, HEADS)
    numbers = jnp.arange(blocks, dtype=jnp.int32)

    def locate(number):
        device = number // 2
        return jnp.where(number % 2 == 0, device, blocks - 1 - device)

    def needed(number):
        block = locate(number)
        want_first = (block <= my_place) & (row_first[block] == 0)
        want_last = (block <= last_block) & (row_last[block] == 0)
        return want_first | want_last

    def scores(key_tile, cum_tile, number):
        block = locate(number)
        key_pos = block * block_rows + jnp.arange(block_rows, dtype=jnp.int32)
        raw_scores = (
            jnp.einsum("qhd,khd->hqk", query_heads, key_tile, preferred_element_type=f32)
            * score_scale
        )
        raw_scores = raw_scores + cum_own.T[:, :, None] - cum_tile.T[:, None, :]
        dropped = jnp.where(in_first, row_first[block], row_last[block])
        allowed = (key_pos[None, :] <= query_pos[:, None]) & (dropped[:, None] == 0)
        return (raw_scores, allowed)

    key_blocks = keys_all.reshape(blocks, block_rows, HEADS, HDIM)
    value_blocks = values_all.reshape(blocks, block_rows, HEADS, HDIM)

    def stats_step(carried, block_item):
        key_tile, cum_tile, number = block_item

        def stats_live(running):
            row_top, exp_total = running
            raw_scores, allowed = scores(key_tile, cum_tile, number)
            raw_scores = jnp.where(allowed[None], raw_scores, NEG)
            new_top = jnp.maximum(row_top, raw_scores.max(-1))
            weights = jnp.where(allowed[None], jnp.exp(raw_scores - new_top[..., None]), 0.0)
            return (new_top, exp_total * jnp.exp(row_top - new_top) + weights.sum(-1))

        return (lax.cond(needed(number), stats_live, keep_same, carried), None)

    start_stats = (jnp.full((HEADS, rows_here), NEG, f32), jnp.zeros((HEADS, rows_here), f32))
    (row_top, exp_total), _ = lax.scan(stats_step, start_stats, (key_blocks, cum_blocks, numbers))
    log_total = row_top + jnp.log(exp_total)

    def value_step(carried, block_item):
        key_tile, value_tile, cum_tile, number = block_item

        def value_live(summed):
            raw_scores, allowed = scores(key_tile, cum_tile, number)
            weights = jnp.where(allowed[None], jnp.exp(raw_scores - log_total[..., None]), 0.0)
            return summed + jnp.einsum(
                "hqk,khd->qhd", weights.astype(bf16), value_tile, preferred_element_type=f32
            )

        return (lax.cond(needed(number), value_live, keep_same, carried), None)

    mixed_heads, _ = lax.scan(
        value_step,
        jnp.zeros((rows_here, HEADS, HDIM), f32),
        (key_blocks, value_blocks, cum_blocks, numbers),
    )
    attended = mixed_heads.reshape(rows_here, D)
    gate_open = jax.nn.sigmoid(projected[:, 3 * D :])
    gated = (gate_open * attended).astype(bf16)
    resid = inputs + jnp.dot(gated, w_out, preferred_element_type=f32)
    normed_ffn, norm_back_ffn = jax.vjp(rms_scale, resid, gain_ffn)
    h_second = normed_ffn.astype(bf16)
    gate_up = jnp.dot(h_second, w_gate_up, preferred_element_type=f32)
    hidden, hidden_back = jax.vjp(swiglu, gate_up)
    hidden_low = hidden.astype(bf16)
    output = resid + jnp.dot(hidden_low, w_down, preferred_element_type=f32)
    d_output = cotangent[0].astype(f32)
    d_branch_ffn = d_output.astype(bf16)
    grad_w_down = jnp.einsum("nf,nd->fd", hidden_low, d_branch_ffn, preferred_element_type=f32)
    (d_gate_up,) = hidden_back(
        jnp.einsum("nd,fd->nf", d_branch_ffn, w_down, preferred_element_type=f32)
    )
    d_gate_low = d_gate_up.astype(bf16)
    grad_w_gate_up = jnp.einsum("nd,nf->df", h_second, d_gate_low, preferred_element_type=f32)
    d_normed_ffn = jnp.einsum("nf,df->nd", d_gate_low, w_gate_up, preferred_element_type=f32)
    d_resid_norm, grad_gain_ffn = norm_back_ffn(d_normed_ffn)
    d_resid = d_output + d_resid_norm
    d_branch_attn = d_resid.astype(bf16)
    grad_w_out = jnp.einsum("nd,ne->de", gated, d_branch_attn, preferred_element_type=f32)
    d_gated = jnp.einsum("ne,de->nd", d_branch_attn, w_out, preferred_element_type=f32)
    d_gate_logit = d_gated * attended * gate_open * (1.0 - gate_open)
    d_mixed_low = (d_gated * gate_open).astype(bf16)
    d_mixed_heads = d_mixed_low.reshape(rows_here, HEADS, HDIM)
    row_delta = jnp.einsum("qhd,qhd->hq", d_mixed_heads.astype(f32), mixed_heads)
    back_keys, back_values = (
        lax.all_gather(key_low, "seq", axis=0, tiled=True),
        lax.all_gather(value_low, "seq", axis=0, tiled=True),
    )
    back_key_blocks = back_keys.reshape(blocks, block_rows, HEADS, HDIM)
    back_value_blocks = back_values.reshape(blocks, block_rows, HEADS, HDIM)

    def score_grads(key_tile, value_tile, cum_tile, number):
        raw_scores, allowed = scores(key_tile, cum_tile, number)
        weights = jnp.where(allowed[None], jnp.exp(raw_scores - log_total[..., None]), 0.0)
        d_weight = jnp.einsum("qhd,khd->hqk", d_mixed_heads, value_tile, preferred_element_type=f32)
        d_score = (weights * (d_weight - row_delta[..., None])).astype(bf16)
        return (weights, d_score)

    def grad_step(carried, block_item):
        key_tile, value_tile, cum_tile, number = block_item

        def grad_live(sums):
            d_query, d_cum_query = sums
            weights, d_score = score_grads(key_tile, value_tile, cum_tile, number)
            d_value = jnp.einsum(
                "hqk,qhd->khd", weights.astype(bf16), d_mixed_heads, preferred_element_type=f32
            )
            d_query = d_query + jnp.einsum(
                "hqk,khd->qhd", d_score, key_tile, preferred_element_type=f32
            )
            d_key = (
                jnp.einsum("hqk,qhd->khd", d_score, query_heads, preferred_element_type=f32)
                * score_scale
            )
            d_cum_query = d_cum_query + jnp.sum(d_score, axis=2, dtype=f32)
            d_cum_key = -jnp.sum(d_score, axis=1, dtype=f32).T
            return (
                (d_query, d_cum_query),
                (d_key.reshape(block_rows, D), d_value.reshape(block_rows, D), d_cum_key),
            )

        def unused(sums):
            return (
                sums,
                (
                    jnp.zeros((block_rows, D), f32),
                    jnp.zeros((block_rows, D), f32),
                    jnp.zeros((block_rows, HEADS), f32),
                ),
            )

        return lax.cond(needed(number), grad_live, unused, carried)

    start_grads = (jnp.zeros((rows_here, HEADS, HDIM), f32), jnp.zeros((HEADS, rows_here), f32))
    (d_query_sum, d_cum_query), (key_terms, value_terms, cum_terms) = lax.scan(
        grad_step, start_grads, (back_key_blocks, back_value_blocks, cum_blocks, numbers)
    )
    key_terms = key_terms.reshape(seq_total, D)
    value_terms = value_terms.reshape(seq_total, D)
    cum_terms = cum_terms.reshape(seq_total, HEADS)
    own_terms = (
        lax.dynamic_slice_in_dim(cum_terms, my_place * rows_here, rows_here, 0) + d_cum_query.T
    )
    cum_terms = lax.dynamic_update_slice_in_dim(cum_terms, own_terms, my_place * rows_here, 0)
    group_terms = to_group(cum_terms, seq_count)
    log_terms = to_device(jnp.cumsum(group_terms[::-1], axis=0)[::-1], seq_count)
    d_keys_own, d_values_own, d_logs_own = (
        lax.psum_scatter(
            key_terms.astype(jnp.bfloat16), "seq", scatter_dimension=0, tiled=True
        ).astype(jnp.float32),
        lax.psum_scatter(
            value_terms.astype(jnp.bfloat16), "seq", scatter_dimension=0, tiled=True
        ).astype(jnp.float32),
        lax.psum_scatter(
            log_terms.astype(jnp.bfloat16), "seq", scatter_dimension=0, tiled=True
        ).astype(jnp.float32),
    )
    d_forget = d_logs_own * jax.nn.sigmoid(-forget_in)
    grad_forget_bias = jnp.sum(d_forget, axis=0)
    d_query_raw, grad_query_gain = query_back(d_query_sum.reshape(rows_here, D) * score_scale)
    d_key_mixed, grad_key_gain = key_back(d_keys_own)
    d_kv_raw, d_previous, d_shift = mix_back(jnp.concatenate([d_key_mixed, d_values_own], 1))
    back_seams = padded_2(jnp.stack([d_previous[0], d_previous[1]]), (("seq", 0),), 1)
    from_next = jnp.where(my_place == seq_count - 1, d_previous[1], back_seams[3])
    d_kv_raw = d_kv_raw.at[block_rows - 1].add(from_next).at[rows_here - 1].add(back_seams[0])
    d_projected = jnp.concatenate([d_query_raw, d_kv_raw, d_gate_logit], 1).astype(bf16)
    d_head_logits = jnp.concatenate([d_forget, d_shift], 1).astype(bf16)
    grad_w_attn = jnp.einsum("nd,nf->df", h_first, d_projected, preferred_element_type=f32)
    grad_w_heads = jnp.einsum("nd,nf->df", h_first, d_head_logits, preferred_element_type=f32)
    d_normed_attn = jnp.einsum(
        "nf,df->nd", d_projected, w_attn, preferred_element_type=f32
    ) + jnp.einsum("nf,df->nd", d_head_logits, w_heads, preferred_element_type=f32)
    d_inputs_norm, grad_gain_attn = norm_back_attn(d_normed_attn)
    d_inputs = d_resid + d_inputs_norm
    (
        grad_gain_attn,
        grad_w_attn,
        grad_w_heads,
        grad_forget_bias,
        grad_query_gain,
        grad_key_gain,
        grad_w_out,
        grad_gain_ffn,
        grad_w_gate_up,
        grad_w_down,
    ) = lax.psum(
        (
            grad_gain_attn,
            grad_w_attn,
            grad_w_heads,
            grad_forget_bias,
            grad_query_gain,
            grad_key_gain,
            grad_w_out,
            grad_gain_ffn,
            grad_w_gate_up,
            grad_w_down,
        ),
        ("seq", "group"),
    )
    return (
        output[None].astype(bf16),
        d_inputs[None],
        grad_gain_attn,
        grad_w_attn,
        grad_w_heads,
        grad_forget_bias,
        grad_query_gain,
        grad_key_gain,
        grad_w_out,
        grad_gain_ffn,
        grad_w_gate_up,
        grad_w_down,
    )


def solution(mesh):
    placed = (
        P("group", "seq", None),
        P("group", "seq", None),
        P("group", None, None),
        P(),
        P(),
        P(),
        P(),
        P(),
        P(),
        P(),
        P(),
        P(),
        P(),
    )
    return jax.shard_map(
        local,
        mesh=mesh,
        in_specs=placed,
        out_specs=(
            P("group", "seq", None),
            P("group", "seq", None),
            P(),
            P(),
            P(),
            P(),
            P(),
            P(),
            P(),
            P(),
            P(),
            P(),
        ),
        check_vma=False,
    )
```

profile of v0, /device:TPU:0, one launch (start us, length us, event | category | flops | bytes accessed | tf_op | source)
XLA Modules:
  0.0 2425.8 jit_solution(8265184366205182833)
XLA Ops:
  76.1 32.0 %all_gather.12 = f32[4096,12]{0,1:T(8,128)S(1)} all-gather(f32[512,12]{0,1:T(8,128)S(1)} %fusion.96), channel_id=1, replica_groups=mesh['seq'=8,'group'=4] {'seq'}, dimensions={0}, use_global_device_ids=true | all-gather | bytes 221184 | tf_op jit(solution)/shard_map/all_gather | solution.py:119
  120.5 32.5 %all-gather.3.cloned.1.call-done = bf16[4096,768]{1,0:T(8,128)(2,1)} async-done(((bf16[512,768]{1,0:T(8,128)(2,1)}), bf16[4096,768]{1,0:T(8,128)(2,1)}) %all-gather.3.cloned.1.call-update) | async-done | bytes 6291472 | tf_op jit(solution)/shard_map/all_gather | solution.py:123
  192.8 331.5 %while.57 = (s32[]{:T(128)}, f32[12,512]{1,0:T(8,128)S(1)}, f32[12,512]{1,0:T(8,128)S(1)}, s32[16]{0:T(128)S(1)}, s32[]{:T(128)}, /*index=5*/s32[16]{0:T(128)}, ...) while((s32[]{:T(128)}, f32[12,512]{1,0:T(8,128)S(1)}, ...), condition=%wide.region_10.11_spmd.clone.clone, body=%wide.region_5.10_spmd.clone.clone.sunk | while | flops 220481856 | bytes 14606365 | solution.py:169
  545.4 367.6 %while.58 = (s32[]{:T(128)}, f32[512,12,64]{0,2,1:T(8,128)}, s32[16]{0:T(128)S(1)}, s32[]{:T(128)}, s32[16]{0:T(128)}, /*index=5*/s32[]{:T(128)}, s32[16]{0:T(12...) while((s32[]{:T(128)}, f32[512,12,64]{0,2,1:T(8,128)}, ...), condition=%wide.region_14.15_spmd.clone.clone, body=%wide.region_11.14_spmd.clone.clone.sunk | while | flops 412752192 | bytes 7860241 | solution.py:184
  952.3 603.3 %while.59 = (s32[]{:T(128)}, f32[512,12,64]{0,2,1:T(8,128)}, f32[12,512]{1,0:T(8,128)}, bf16[16,256,768]{1,2,0:T(8,128)(2,1)}, bf16[16,256,768]{1,2,0:T(8,128)(2...) while((s32[]{:T(128)}, f32[512,12,64]{0,2,1:T(8,128)}, ...), condition=%wide.region_22.23_spmd.clone.clone, body=%wide.region_17.22_spmd.clone.clone.sunk | while | flops 1034426688 | bytes 83271552 | solution.py:267
  960.2 26.2 %conditional.14 = (f32[512,12,64]{0,2,1:T(8,128)}, f32[12,512]{1,0:T(8,128)}, bf16[1,256,768]{1,2,0:T(8,128)(2,1)S(1)}, bf16[1,256,768]{1,2,0:T(8,128)(2,1)}, f32[1,256,12]{1,2,0:T(8,128)S(1)}) conditional(s32[]{:T(128)} %convert_element_type.198, (f32[512,12,64]{0,2,1:T(8,128)}, f32[12,512]{1,0:T(8,128)}) %tuple.208, (s32[]{:T(128)}, ...), branch_computations={%region_18.18_spmd, %region_19.21_spmd.clone} | conditional | flops 1034425600 | bytes 81643616 | solution.py:264
  997.9 26.2 %conditional.14 = (f32[512,12,64]{0,2,1:T(8,128)}, f32[12,512]{1,0:T(8,128)}, bf16[1,256,768]{1,2,0:T(8,128)(2,1)S(1)}, bf16[1,256,768]{1,2,0:T(8,128)(2,1)}, f32[1,256,12]{1,2,0:T(8,128)S(1)}) conditional(s32[]{:T(128)} %convert_element_type.198, (f32[512,12,64]{0,2,1:T(8,128)}, f32[12,512]{1,0:T(8,128)}) %tuple.208, (s32[]{:T(128)}, ...), branch_computations={%region_18.18_spmd, %region_19.21_spmd.clone} | conditional | flops 1034425600 | bytes 81643616 | solution.py:264
  1035.6 26.2 %conditional.14 = (f32[512,12,64]{0,2,1:T(8,128)}, f32[12,512]{1,0:T(8,128)}, bf16[1,256,768]{1,2,0:T(8,128)(2,1)S(1)}, bf16[1,256,768]{1,2,0:T(8,128)(2,1)}, f32[1,256,12]{1,2,0:T(8,128)S(1)}) conditional(s32[]{:T(128)} %convert_element_type.198, (f32[512,12,64]{0,2,1:T(8,128)}, f32[12,512]{1,0:T(8,128)}) %tuple.208, (s32[]{:T(128)}, ...), branch_computations={%region_18.18_spmd, %region_19.21_spmd.clone} | conditional | flops 1034425600 | bytes 81643616 | solution.py:264
  1111.0 26.2 %conditional.14 = (f32[512,12,64]{0,2,1:T(8,128)}, f32[12,512]{1,0:T(8,128)}, bf16[1,256,768]{1,2,0:T(8,128)(2,1)S(1)}, bf16[1,256,768]{1,2,0:T(8,128)(2,1)}, f32[1,256,12]{1,2,0:T(8,128)S(1)}) conditional(s32[]{:T(128)} %convert_element_type.198, (f32[512,12,64]{0,2,1:T(8,128)}, f32[12,512]{1,0:T(8,128)}) %tuple.208, (s32[]{:T(128)}, ...), branch_computations={%region_18.18_spmd, %region_19.21_spmd.clone} | conditional | flops 1034425600 | bytes 81643616 | solution.py:264
  1148.7 26.2 %conditional.14 = (f32[512,12,64]{0,2,1:T(8,128)}, f32[12,512]{1,0:T(8,128)}, bf16[1,256,768]{1,2,0:T(8,128)(2,1)S(1)}, bf16[1,256,768]{1,2,0:T(8,128)(2,1)}, f32[1,256,12]{1,2,0:T(8,128)S(1)}) conditional(s32[]{:T(128)} %convert_element_type.198, (f32[512,12,64]{0,2,1:T(8,128)}, f32[12,512]{1,0:T(8,128)}) %tuple.208, (s32[]{:T(128)}, ...), branch_computations={%region_18.18_spmd, %region_19.21_spmd.clone} | conditional | flops 1034425600 | bytes 81643616 | solution.py:264
  1186.4 26.2 %conditional.14 = (f32[512,12,64]{0,2,1:T(8,128)}, f32[12,512]{1,0:T(8,128)}, bf16[1,256,768]{1,2,0:T(8,128)(2,1)S(1)}, bf16[1,256,768]{1,2,0:T(8,128)(2,1)}, f32[1,256,12]{1,2,0:T(8,128)S(1)}) conditional(s32[]{:T(128)} %convert_element_type.198, (f32[512,12,64]{0,2,1:T(8,128)}, f32[12,512]{1,0:T(8,128)}) %tuple.208, (s32[]{:T(128)}, ...), branch_computations={%region_18.18_spmd, %region_19.21_spmd.clone} | conditional | flops 1034425600 | bytes 81643616 | solution.py:264
  1224.1 26.2 %conditional.14 = (f32[512,12,64]{0,2,1:T(8,128)}, f32[12,512]{1,0:T(8,128)}, bf16[1,256,768]{1,2,0:T(8,128)(2,1)S(1)}, bf16[1,256,768]{1,2,0:T(8,128)(2,1)}, f32[1,256,12]{1,2,0:T(8,128)S(1)}) conditional(s32[]{:T(128)} %convert_element_type.198, (f32[512,12,64]{0,2,1:T(8,128)}, f32[12,512]{1,0:T(8,128)}) %tuple.208, (s32[]{:T(128)}, ...), branch_computations={%region_18.18_spmd, %region_19.21_spmd.clone} | conditional | flops 1034425600 | bytes 81643616 | solution.py:264
  1261.8 26.2 %conditional.14 = (f32[512,12,64]{0,2,1:T(8,128)}, f32[12,512]{1,0:T(8,128)}, bf16[1,256,768]{1,2,0:T(8,128)(2,1)S(1)}, bf16[1,256,768]{1,2,0:T(8,128)(2,1)}, f32[1,256,12]{1,2,0:T(8,128)S(1)}) conditional(s32[]{:T(128)} %convert_element_type.198, (f32[512,12,64]{0,2,1:T(8,128)}, f32[12,512]{1,0:T(8,128)}) %tuple.208, (s32[]{:T(128)}, ...), branch_computations={%region_18.18_spmd, %region_19.21_spmd.clone} | conditional | flops 1034425600 | bytes 81643616 | solution.py:264
  1299.5 26.2 %conditional.14 = (f32[512,12,64]{0,2,1:T(8,128)}, f32[12,512]{1,0:T(8,128)}, bf16[1,256,768]{1,2,0:T(8,128)(2,1)S(1)}, bf16[1,256,768]{1,2,0:T(8,128)(2,1)}, f32[1,256,12]{1,2,0:T(8,128)S(1)}) conditional(s32[]{:T(128)} %convert_element_type.198, (f32[512,12,64]{0,2,1:T(8,128)}, f32[12,512]{1,0:T(8,128)}) %tuple.208, (s32[]{:T(128)}, ...), branch_computations={%region_18.18_spmd, %region_19.21_spmd.clone} | conditional | flops 1034425600 | bytes 81643616 | solution.py:264
  1337.2 26.2 %conditional.14 = (f32[512,12,64]{0,2,1:T(8,128)}, f32[12,512]{1,0:T(8,128)}, bf16[1,256,768]{1,2,0:T(8,128)(2,1)S(1)}, bf16[1,256,768]{1,2,0:T(8,128)(2,1)}, f32[1,256,12]{1,2,0:T(8,128)S(1)}) conditional(s32[]{:T(128)} %convert_element_type.198, (f32[512,12,64]{0,2,1:T(8,128)}, f32[12,512]{1,0:T(8,128)}) %tuple.208, (s32[]{:T(128)}, ...), branch_computations={%region_18.18_spmd, %region_19.21_spmd.clone} | conditional | flops 1034425600 | bytes 81643616 | solution.py:264
  1374.9 26.2 %conditional.14 = (f32[512,12,64]{0,2,1:T(8,128)}, f32[12,512]{1,0:T(8,128)}, bf16[1,256,768]{1,2,0:T(8,128)(2,1)S(1)}, bf16[1,256,768]{1,2,0:T(8,128)(2,1)}, f32[1,256,12]{1,2,0:T(8,128)S(1)}) conditional(s32[]{:T(128)} %convert_element_type.198, (f32[512,12,64]{0,2,1:T(8,128)}, f32[12,512]{1,0:T(8,128)}) %tuple.208, (s32[]{:T(128)}, ...), branch_computations={%region_18.18_spmd, %region_19.21_spmd.clone} | conditional | flops 1034425600 | bytes 81643616 | solution.py:264
  1412.5 26.2 %conditional.14 = (f32[512,12,64]{0,2,1:T(8,128)}, f32[12,512]{1,0:T(8,128)}, bf16[1,256,768]{1,2,0:T(8,128)(2,1)S(1)}, bf16[1,256,768]{1,2,0:T(8,128)(2,1)}, f32[1,256,12]{1,2,0:T(8,128)S(1)}) conditional(s32[]{:T(128)} %convert_element_type.198, (f32[512,12,64]{0,2,1:T(8,128)}, f32[12,512]{1,0:T(8,128)}) %tuple.208, (s32[]{:T(128)}, ...), branch_computations={%region_18.18_spmd, %region_19.21_spmd.clone} | conditional | flops 1034425600 | bytes 81643616 | solution.py:264
  1450.2 26.2 %conditional.14 = (f32[512,12,64]{0,2,1:T(8,128)}, f32[12,512]{1,0:T(8,128)}, bf16[1,256,768]{1,2,0:T(8,128)(2,1)S(1)}, bf16[1,256,768]{1,2,0:T(8,128)(2,1)}, f32[1,256,12]{1,2,0:T(8,128)S(1)}) conditional(s32[]{:T(128)} %convert_element_type.198, (f32[512,12,64]{0,2,1:T(8,128)}, f32[12,512]{1,0:T(8,128)}) %tuple.208, (s32[]{:T(128)}, ...), branch_computations={%region_18.18_spmd, %region_19.21_spmd.clone} | conditional | flops 1034425600 | bytes 81643616 | solution.py:264
  1487.9 26.2 %conditional.14 = (f32[512,12,64]{0,2,1:T(8,128)}, f32[12,512]{1,0:T(8,128)}, bf16[1,256,768]{1,2,0:T(8,128)(2,1)S(1)}, bf16[1,256,768]{1,2,0:T(8,128)(2,1)}, f32[1,256,12]{1,2,0:T(8,128)S(1)}) conditional(s32[]{:T(128)} %convert_element_type.198, (f32[512,12,64]{0,2,1:T(8,128)}, f32[12,512]{1,0:T(8,128)}) %tuple.208, (s32[]{:T(128)}, ...), branch_computations={%region_18.18_spmd, %region_19.21_spmd.clone} | conditional | flops 1034425600 | bytes 81643616 | solution.py:264
  1525.6 26.2 %conditional.14 = (f32[512,12,64]{0,2,1:T(8,128)}, f32[12,512]{1,0:T(8,128)}, bf16[1,256,768]{1,2,0:T(8,128)(2,1)S(1)}, bf16[1,256,768]{1,2,0:T(8,128)(2,1)}, f32[1,256,12]{1,2,0:T(8,128)S(1)}) conditional(s32[]{:T(128)} %convert_element_type.198, (f32[512,12,64]{0,2,1:T(8,128)}, f32[12,512]{1,0:T(8,128)}) %tuple.208, (s32[]{:T(128)}, ...), branch_computations={%region_18.18_spmd, %region_19.21_spmd.clone} | conditional | flops 1034425600 | bytes 81643616 | solution.py:264
  1639.0 119.5 %reduce-scatter.4.cloned.1.call-done = bf16[512,768]{1,0:T(8,128)(2,1)} async-done(((bf16[4096,768]{1,0:T(8,128)(2,1)}), bf16[512,768]{1,0:T(8,128)(2,1)}) %reduce-scatter.4.cloned.1.call-update) | async-done | bytes 786448 | tf_op jit(solution)/shard_map/reduce_scatter | solution.py:280
  1770.7 109.0 %reduce-scatter.6.cloned.1.call-done = bf16[512,768]{1,0:T(8,128)(2,1)} async-done(((bf16[4096,768]{1,0:T(8,128)(2,1)}), bf16[512,768]{1,0:T(8,128)(2,1)}) %reduce-scatter.6.cloned.1.call-update) | async-done | bytes 786448 | tf_op jit(solution)/shard_map/reduce_scatter | solution.py:283
  1940.2 40.1 %all-reduce.5 = (f32[768]{0:T(1024)}, f32[12]{0:T(128)}, f32[768]{0:T(1024)}, f32[768]{0:T(1024)}, f32[768]{0:T(1024)}) all-reduce(f32[768]{0:T(1024)S(1)} %get-tuple-element.1572, f32[12]{0:T(128)S(1)} %get-tuple-element.1672, f32[768]{0:T(1024)S(1)} %multiply_reduce_fusion.1, ...), channel_id=1, replica_groups=mesh['seq'=8,'group'=4] {'seq','group'}, use_global_device_ids=true, to_apply=%region_33.34 | all-reduce | flops 3084 | bytes 24672 | tf_op jit(solution)/shard_map/psum | solution.py:318
  1984.2 406.7 %all-reduce.9.cloned.1.call-done = (f32[768,3072]{1,0:T(8,128)}, f32[768,36]{0,1:T(8,128)}, f32[768,768]{1,0:T(8,128)}, f32[768,4096]{1,0:T(8,128)}, f32[2048,768]{1,0:T(8,128)}) async-done(((f32[768,3072]{1,0:T(8,128)}, f32[768,36]{0,1:T(8,128)}, f32[768,768]{1,0:T(8,128)}, f32[768,4096]{1,0:T(8,128)}, f32[2048,768]{1,0:T(8,128)}), (f32[768,3072]{1,0:T(8,128)}, f32[768,36]{0,1:T(8,128)}, ...) | async-done | bytes 30781456 | tf_op jit(solution)/shard_map/psum | solution.py:318
  (1556 shorter events, 1844.2 us)
Async XLA Ops:
  7.2 918.4 %copy-start = (bf16[2048,768]{1,0:T(8,128)(2,1)S(1)}, bf16[2048,768]{1,0:T(8,128)(2,1)}, u32[]{:S(2)}) copy-start(bf16[2048,768]{1,0:T(8,128)(2,1)} %param.41) | copy-start | bytes 9437188
  7.2 145.8 %all-gather.3.cloned.1.call-start = ((), (), s32[]{:S(2)}) async-start(), calls=%async_computation.3 | async-start | bytes 7077888 | tf_op jit(solution)/shard_map/all_gather | solution.py:123
  14.2 6.7 collective-permute-start.1
  18.3 57.7 %copy-start.43 = (f32[512,36]{0,1:T(8,128)}, f32[512,36]{0,1:T(8,128)S(1)}, u32[]{:S(2)}) copy-start(f32[512,36]{0,1:T(8,128)S(1)} %fusion.117) | copy-start | bytes 221188
  21.7 10.4 collective-permute-start
  52.0 472.3 %all-gather.5.cloned.1.call-start = ((), (), s32[]{:S(2)}) async-start(), calls=%async_computation.4 | async-start | bytes 7077888 | tf_op jit(solution)/shard_map/all_gather | solution.py:124
  54.5 1583.6 %reduce-scatter.8.cloned.1.call-start = ((), (), s32[]{:S(2)}) async-start(), calls=%async_computation.7 | async-start | bytes 147456 | tf_op jit(solution)/shard_map/reduce_scatter | solution.py:286
  919.3 19.7 copy-start.14
  919.3 19.7 copy-start.51
  960.9 12.2 copy-start.65
  1036.3 12.2 copy-start.65
  1111.7 12.2 copy-start.65
  1149.4 12.2 copy-start.65
  1187.2 12.2 copy-start.65
  1262.6 12.2 copy-start.65
  1579.4 179.1 %reduce-scatter.4.cloned.1.call-start = ((), (), s32[]{:S(2)}) async-start(), calls=%async_computation.5 | async-start | bytes 7077888 | tf_op jit(solution)/shard_map/reduce_scatter | solution.py:280
  1588.1 291.6 %reduce-scatter.6.cloned.1.call-start = ((), (), s32[]{:S(2)}) async-start(), calls=%async_computation.6 | async-start | bytes 7077888 | tf_op jit(solution)/shard_map/reduce_scatter | solution.py:283
  1596.9 794.0 %all-reduce.9.cloned.1.call-start = ((), (), s32[]{:S(2)}) async-start(), calls=%async_computation.8 | async-start | bytes 61587456 | tf_op jit(solution)/shard_map/psum | solution.py:318
  1615.1 23.0 copy-start.44
  1615.1 23.0 copy-start.74
  1615.1 143.4 %copy-start.62 = (f32[768]{0:T(1024)S(1)}, f32[768]{0:T(1024)}, u32[]{:S(2)}) copy-start(f32[768]{0:T(1024)} %param.37) | copy-start | bytes 9220
  1896.7 5.5 collective-permute-start.2
  1903.0 7.9 collective-permute-start.3
  1933.6 46.7 %copy-start.69 = (f32[512]{0:T(512)S(1)}, f32[512]{0:T(512)}, u32[]{:S(2)}) copy-start(f32[512]{0:T(512)} %copy-done.68) | copy-start | bytes 6148
  (204 other events, 1009.7 us)
Sparse Core Ops, SparseCore 0:
  52.1 100.8 all-gather.2
  155.2 97.2 all-gather.4
  1579.5 58.4 reduce-scatter.7
  1641.5 116.9 reduce-scatter.3
  1762.6 117.0 reduce-scatter.5
  1922.6 468.2 all-reduce.8
where the time goes:
time: 2450 us; the launch traced here: 2430 us
  waiting for transfers between devices  688 us (28%)
  local copies, waits for them, and re-layouts  625 us (26%)
  matrix products  486 us (20%)
  loops' own time  327 us (13%)
  other arithmetic  200 us (8%)
  blocking collectives  72 us (3%)
    psum x1, waiting for transfers between devices, local(): lax.psum((grad_gain_attn, grad_w_attn, grad_w_heads, grad_forget_bias, gr...  407 us
    dot_general x32, matrix products, scores(): jnp.einsum('qhd,khd->hqk', query_heads, key_tile, preferred_element_type=...  128 us
    reduce_scatter x1, waiting for transfers between devices, local(): lax.psum_scatter(key_terms.astype(jnp.bfloat16), 'seq', scatter_dimension...  120 us
    dynamic_slice x96, local copies, waits for them, and re-layouts, scores(): dropped = jnp.where(in_first, row_first[block], row_last[block])  119 us
    reduce_scatter x1, waiting for transfers between devices, local(): lax.psum_scatter(value_terms.astype(jnp.bfloat16), 'seq', scatter_dimensi...  109 us
    dot_general x16, matrix products, value_live(): jnp.einsum('hqk,khd->qhd', weights.astype(bf16), value_tile, preferred_el...  98.2 us
    dot_general x16, matrix products, score_grads(): jnp.einsum('qhd,khd->hqk', d_mixed_heads, value_tile, preferred_element_t...  92.2 us
    unnamed x177, local copies, waits for them, and re-layouts  87.3 us
  transfers between devices with their start and end apart: 10, of which 7 were waited for; matrix products, arithmetic and copies ran while one was open for 16% of the time, Pallas kernels for 0%

commit v1 on v0

v1 whole, which is shorter than its diff:
```python
import functools

import jax
import jax.numpy as jnp
from jax import lax
from jax.experimental import pallas as pl
from jax.experimental.pallas import tpu as pltpu
from jax.sharding import PartitionSpec as P

D, FF = 768, 2048
MESH = pl.DeviceIdType.MESH
ANY = pl.BlockSpec(memory_space=pl.ANY)

HEADS, HDIM, BLK = 12, 64, 256
EPS = 1e-06
LOG2E = 1.4426950408889634
LN2 = 0.6931471805599453
SCORE = HDIM ** -0.5
f32, bf16 = jnp.float32, jnp.bfloat16
UNROLL = 8
UNROLL_BACK = 4
NN = (((1,), (0,)), ((), ()))
NT = (((1,), (1,)), ((), ()))


def mm(a, b, dims=NN):
    return lax.dot_general(a, b, dims, preferred_element_type=f32)


def split3(v):
    hi = v.astype(bf16).astype(f32)
    rest = v - hi
    mid = rest.astype(bf16).astype(f32)
    return hi, mid, rest - mid


def place_of(block, count):
    return jnp.where(block < count, block, 2 * count - 1 - block)


def lanes_of(block, count):
    return pl.ds(pl.multiple_of(jnp.where(block < count, 0, BLK), BLK), BLK)


def first_head(device, count):
    return jnp.minimum(HEADS * device // count, HEADS - 2)


def is_mine(device, slot, place, count):
    chunk = (first_head(device, count) + slot) * count + place
    return (chunk >= HEADS * device) & (chunk < HEADS * device + HEADS)


def list_pairs(skip_ref, pairs_ref, own_ref, device, slot, count, unroll):
    spare = 2 * count

    def row(number, found):
        def column(other, found):
            pairs_ref[found] = number * 1024 + other
            return found + jnp.where(skip_ref[number, other] == 0, 1, 0)

        mine = is_mine(device, slot, place_of(number, count), count)
        own_ref[found[1]] = number
        below = lax.fori_loop(0, jnp.where(mine, number, 0), column, found[0])
        return below, found[1] + jnp.where(mine, 1, 0)

    below, own = lax.fori_loop(0, spare, row, (0, 0))
    for extra in range(unroll):
        pairs_ref[below + extra] = spare * 1024
        own_ref[own + extra] = spare
    return pl.cdiv(below, unroll), pl.cdiv(own, unroll)


def running_sum(values, count, reverse):
    t = lax.broadcasted_iota(jnp.int32, (BLK, BLK), 0)
    p = lax.broadcasted_iota(jnp.int32, (BLK, BLK), 1)
    ones = jnp.where(t >= p if reverse else t <= p, 1.0, 0.0).astype(bf16)
    halves = []
    for half in range(2):
        part = values[:, half * BLK : (half + 1) * BLK]
        halves.append(sum(mm(piece.astype(bf16), ones) for piece in split3(part)))
    edge = 0 if reverse else BLK - 1
    first, last = (jnp.broadcast_to(h[:, edge : edge + 1], (count, 128)) for h in halves)
    rows = lax.broadcasted_iota(jnp.int32, (count, 128), 0)

    def scan(total, down):
        own = total
        step = 1
        while step < count:
            moved = pltpu.roll(total, step if down else count - step, 0)
            total = total + jnp.where(rows >= step if down else rows < count - step, moved, 0.0)
            step *= 2
        return total - own

    if reverse:
        all_last = jnp.sum(last, axis=0, keepdims=True)
        offsets = scan(first, False) + all_last, scan(last, True)
    else:
        all_first = jnp.sum(first, axis=0, keepdims=True)
        offsets = scan(first, True), scan(last, False) + all_first
    return jnp.concatenate([halves[0] + offsets[0][:, :1], halves[1] + offsets[1][:, :1]], 1)


def shifted(current, before):
    lane = lax.broadcasted_iota(jnp.int32, current.shape, 1)
    return jnp.where(lane == 0, pltpu.roll(before, 1, 1), pltpu.roll(current, 1, 1))


def shifted_back(current, after):
    lane = lax.broadcasted_iota(jnp.int32, current.shape, 1)
    return jnp.where(lane == BLK - 1, pltpu.roll(after, BLK - 1, 1), pltpu.roll(current, BLK - 1, 1))


def stack_rows(top, rows, size):
    extra = size if top is None else size - top.shape[0]
    number = lax.broadcasted_iota(jnp.int32, (extra, BLK), 0)
    bottom = jnp.zeros((extra, BLK), f32)
    for i, r in enumerate(rows):
        bottom = jnp.where(number == i, r, bottom)
    return bottom if top is None else jnp.concatenate([top, bottom], 0)


def forward_kernel(count, device_ref, skip_ref, bias_ref, raw_ref, logit_ref, gain_ref,
                   mixed_ref, mixed_full_ref, q_ref, k_ref, kt_ref, vt_ref,
                   cum_ref, acc_ref, pairs_ref, own_ref):
    slot = pl.program_id(0)
    device = device_ref[0]
    blocks = 2 * count
    pair_steps, own_steps = list_pairs(skip_ref, pairs_ref, own_ref, device, slot, count, UNROLL)
    logits = logit_ref[:, 0, :] + bias_ref[slot]
    log_forget = jnp.minimum(logits, 0.0) - jnp.log1p(jnp.exp(-jnp.abs(logits)))
    cum_ref[...] = running_sum(log_forget, count, False) * LOG2E
    gain_q, gain_k = gain_ref[:, 0:1], gain_ref[:, 1:2]

    def prepare(block, carried):
        place, lanes = place_of(block, count), lanes_of(block, count)
        q_raw, k_raw, v_raw = (raw_ref[place, i, :, lanes].astype(f32) for i in range(3))
        cum = cum_ref[pl.ds(place, 1), lanes]
        parts = split3(cum)
        one = jnp.ones_like(cum)
        query = q_raw * lax.rsqrt(jnp.mean(q_raw * q_raw, 0, keepdims=True) + EPS) * (gain_q * (SCORE * LOG2E))
        q_ref[block] = stack_rows(query, (*parts, one, one, one), 128).astype(bf16)
        rate_k = jax.nn.sigmoid(logit_ref[place, 1:2, lanes])
        rate_v = jax.nn.sigmoid(logit_ref[place, 2:3, lanes])
        key = k_raw + rate_k * (shifted(k_raw, carried[0]) - k_raw)
        key = key * lax.rsqrt(jnp.mean(key * key, 0, keepdims=True) + EPS) * gain_k
        value = v_raw + rate_v * (shifted(v_raw, carried[1]) - v_raw)
        k_ref[block] = stack_rows(key, (one, one, one, *(-c for c in parts)), 128).T.astype(bf16)
        kt_ref[block] = stack_rows(key, (one,), 80).astype(bf16)
        vt_ref[block] = stack_rows(value, (one, one, one), 80).astype(bf16)
        return k_raw, v_raw

    zero = jnp.zeros((HDIM, BLK), f32)
    lax.fori_loop(0, blocks, prepare, (zero, zero))
    q_ref[blocks] = jnp.zeros(q_ref.shape[1:], bf16)

    t = lax.broadcasted_iota(jnp.int32, (BLK, BLK), 0)
    p = lax.broadcasted_iota(jnp.int32, (BLK, BLK), 1)

    def together(pairs, diagonal):
        scores = [mm(k_ref[column], q_ref[row]) for row, column in pairs]
        weights = [jnp.exp2(score) for score in scores]
        if diagonal:
            weights = [jnp.where(t <= p, weight, 0.0) for weight in weights]
        weights = [weight.astype(bf16) for weight in weights]
        parts = [mm(vt_ref[column], weight) for (row, column), weight in zip(pairs, weights)]
        for (row, column), part in zip(pairs, parts):
            acc_ref[row] = part if diagonal else acc_ref[row] + part

    def own_rows(step, carried):
        rows = [own_ref[step * UNROLL + i] for i in range(UNROLL)]
        together([(row, jnp.minimum(row, blocks - 1)) for row in rows], True)
        return carried

    def kept_pairs(step, carried):
        codes = [pairs_ref[step * UNROLL + i] for i in range(UNROLL)]
        together([(code >> 10, code & 1023) for code in codes], False)
        return carried

    lax.fori_loop(0, own_steps, own_rows, 0)
    lax.fori_loop(0, pair_steps, kept_pairs, 0)

    def finish(block, carried):
        place, lanes = place_of(block, count), lanes_of(block, count)
        total = acc_ref[block]
        norm = total[HDIM : HDIM + 1]
        mixed = total[:HDIM] * (1.0 / norm)
        mixed_full_ref[block] = mixed
        mixed_ref[place, :, lanes] = mixed.astype(bf16)
        parts = split3(cum_ref[pl.ds(place, 1), lanes] - jnp.log2(norm))
        one = jnp.ones_like(norm)
        q_ref[block, HDIM : HDIM + 16, :] = stack_rows(None, (*parts, one, one, one), 16).astype(bf16)
        return carried

    lax.fori_loop(0, blocks, finish, 0)


def buffers(count):
    return pl.Buffered(1 if count > 8 else 2)


def attend_forward(device, skip, bias, raw, logits, gains):
    count = raw.shape[0]
    blocks = 2 * count
    most = blocks * (blocks - 1) // 2 + UNROLL
    mode = buffers(count)
    by_slot = lambda *shape: pl.BlockSpec((None,) + shape, lambda s, *_: (s,) + (0,) * len(shape), pipeline_mode=mode)
    out = lambda shape, dtype: jax.ShapeDtypeStruct((2,) + shape, dtype)
    return pl.pallas_call(
        functools.partial(forward_kernel, count),
        grid_spec=pltpu.PrefetchScalarGridSpec(
            num_scalar_prefetch=3,
            grid=(2,),
            in_specs=[
                pl.BlockSpec((count, 3, None, HDIM, 2 * BLK), lambda s, *_: (0, 0, s, 0, 0), pipeline_mode=mode),
                pl.BlockSpec((count, None, 8, 2 * BLK), lambda s, *_: (0, s, 0, 0), pipeline_mode=mode),
                by_slot(HDIM, 2),
            ],
            out_specs=[
                by_slot(count, HDIM, 2 * BLK),
                by_slot(blocks, HDIM, BLK),
                by_slot(blocks + 1, 128, BLK),
                by_slot(blocks, BLK, 128),
                by_slot(blocks, 80, BLK),
                by_slot(blocks, 80, BLK),
            ],
            scratch_shapes=[
                pltpu.VMEM((count, 2 * BLK), f32),
                pltpu.VMEM((blocks + 1, 80, BLK), f32),
                pltpu.SMEM((most,), jnp.int32),
                pltpu.SMEM((blocks + UNROLL,), jnp.int32),
            ],
        ),
        out_shape=[
            out((count, HDIM, 2 * BLK), bf16),
            out((blocks, HDIM, BLK), f32),
            out((blocks + 1, 128, BLK), bf16),
            out((blocks, BLK, 128), bf16),
            out((blocks, 80, BLK), bf16),
            out((blocks, 80, BLK), bf16),
        ],
        compiler_params=pltpu.CompilerParams(vmem_limit_bytes=60 * 2**20),
        name="attend_forward",
    )(device, skip, bias, raw, logits, gains)


def norm_back(v, gain, u):
    scale = lax.rsqrt(jnp.mean(v * v, 0, keepdims=True) + EPS)
    hat = v * scale
    gu = gain * u
    return scale * (gu - hat * jnp.mean(hat * gu, 0, keepdims=True)), hat * u


def backward_kernel(count, device_ref, skip_ref, bias_ref, raw_ref, logit_ref, gain_ref, dmixed_ref, mixed_ref,
                    q_ref, k_ref, kt_ref, vt_ref, draw_ref, dlogit_ref, dgain_ref,
                    do_ref, v_ref, cum_ref, dq_ref, dk_ref, dv_ref, pairs_ref, own_ref):
    slot = pl.program_id(0)
    device = device_ref[0]
    blocks = 2 * count
    pair_steps, own_steps = list_pairs(skip_ref, pairs_ref, own_ref, device, slot, count, UNROLL_BACK)
    gain_q, gain_k = gain_ref[:, 0:1], gain_ref[:, 1:2]
    wide = jnp.zeros((128 - 80, BLK), f32)

    def prepare(block, carried):
        place, lanes = place_of(block, count), lanes_of(block, count)
        d_out = dmixed_ref[place, :, lanes].astype(f32)
        delta = jnp.sum(d_out * mixed_ref[block], 0, keepdims=True)
        do_ref[block] = stack_rows(d_out, [-d for d in split3(delta)], 128).astype(bf16)
        v_ref[block] = jnp.concatenate([vt_ref[block].astype(f32), wide], 0).T.astype(bf16)
        dq_ref[block] = jnp.zeros(dq_ref.shape[1:], f32)
        dk_ref[block] = jnp.zeros(dk_ref.shape[1:], f32)
        dv_ref[block] = jnp.zeros(dv_ref.shape[1:], f32)
        return carried

    lax.fori_loop(0, blocks, prepare, 0)
    do_ref[blocks] = jnp.zeros(do_ref.shape[1:], bf16)
    dq_ref[blocks] = jnp.zeros(dq_ref.shape[1:], f32)

    t = lax.broadcasted_iota(jnp.int32, (BLK, BLK), 0)
    p = lax.broadcasted_iota(jnp.int32, (BLK, BLK), 1)

    def together(pairs, diagonal):
        scores = [mm(k_ref[column], q_ref[row]) for row, column in pairs]
        weights = [jnp.exp2(score) for score in scores]
        if diagonal:
            weights = [jnp.where(t <= p, weight, 0.0) for weight in weights]
        d_weights = [mm(v_ref[column], do_ref[row]) for row, column in pairs]
        low_weights = [weight.astype(bf16) for weight in weights]
        d_scores = [(weight * d_weight).astype(bf16) for weight, d_weight in zip(weights, d_weights)]
        parts = [mm(do_ref[row, :HDIM], weight, NT) for (row, _), weight in zip(pairs, low_weights)]
        for (_, column), part in zip(pairs, parts):
            dv_ref[column] += part
        parts = [mm(kt_ref[column], d_score) for (_, column), d_score in zip(pairs, d_scores)]
        for (row, _), part in zip(pairs, parts):
            dq_ref[row] += part
        parts = [mm(q_ref[row, :80], d_score, NT) for (row, _), d_score in zip(pairs, d_scores)]
        for (_, column), part in zip(pairs, parts):
            dk_ref[column] += part

    def own_rows(step, carried):
        rows = [own_ref[step * UNROLL_BACK + i] for i in range(UNROLL_BACK)]
        together([(row, jnp.minimum(row, blocks - 1)) for row in rows], True)
        return carried

    def kept_pairs(step, carried):
        codes = [pairs_ref[step * UNROLL_BACK + i] for i in range(UNROLL_BACK)]
        together([(code >> 10, code & 1023) for code in codes], False)
        return carried

    lax.fori_loop(0, own_steps, own_rows, 0)
    lax.fori_loop(0, pair_steps, kept_pairs, 0)

    def finish(step, carried):
        next_k, next_v, sum_q, sum_k = carried
        block = blocks - 1 - step
        place, lanes = place_of(block, count), lanes_of(block, count)
        earlier = jnp.maximum(block - 1, 0)
        place_before, lanes_before = place_of(earlier, count), lanes_of(earlier, count)
        exists = jnp.where(block > 0, 1.0, 0.0)
        q_raw, k_raw, v_raw = (raw_ref[place, i, :, lanes].astype(f32) for i in range(3))
        k_step = shifted(k_raw, raw_ref[place_before, 1, :, lanes_before].astype(f32) * exists) - k_raw
        v_step = shifted(v_raw, raw_ref[place_before, 2, :, lanes_before].astype(f32) * exists) - v_raw
        rate_k = jax.nn.sigmoid(logit_ref[place, 1:2, lanes])
        rate_v = jax.nn.sigmoid(logit_ref[place, 2:3, lanes])
        dq, dk, dv = dq_ref[block], dk_ref[block], dv_ref[block]
        dq_raw, part_q = norm_back(q_raw, gain_q, dq[:HDIM] * SCORE)
        dk_mixed, part_k = norm_back(k_raw + rate_k * k_step, gain_k, dk[:HDIM] * LN2)
        send_k, send_v = rate_k * dk_mixed, rate_v * dv
        draw_ref[place, 0, :, lanes] = dq_raw.astype(bf16)
        draw_ref[place, 1, :, lanes] = (dk_mixed - send_k + shifted_back(send_k, next_k)).astype(bf16)
        draw_ref[place, 2, :, lanes] = (dv - send_v + shifted_back(send_v, next_v)).astype(bf16)
        dlogit_ref[place, 1:2, lanes] = (1.0 - rate_k) * jnp.sum(k_step * send_k, 0, keepdims=True)
        dlogit_ref[place, 2:3, lanes] = (1.0 - rate_v) * jnp.sum(v_step * send_v, 0, keepdims=True)
        cum_ref[pl.ds(place, 1), lanes] = dq[HDIM : HDIM + 1] - dk[HDIM + 3 : HDIM + 4]
        part_q = jnp.where(is_mine(device, slot, place, count), part_q, 0.0)
        return send_k, send_v, sum_q + part_q, sum_k + part_k

    zero = jnp.zeros((HDIM, BLK), f32)
    _, _, sum_q, sum_k = lax.fori_loop(0, blocks, finish, (zero, zero, zero, zero))
    dgain_ref[:, 0:1] = jnp.sum(sum_q, 1, keepdims=True)
    dgain_ref[:, 1:2] = jnp.sum(sum_k, 1, keepdims=True)
    d_log = running_sum(cum_ref[...], count, True)
    dlogit_ref[:, 0, :] = d_log * jax.nn.sigmoid(-(logit_ref[:, 0, :] + bias_ref[slot]))
    dlogit_ref[:, 3:, :] = jnp.zeros((count, 5, 2 * BLK), f32)


def attend_backward(device, skip, bias, raw, logits, gains, dmixed, mixed, q, k, kt, vt):
    count = raw.shape[0]
    blocks = 2 * count
    most = blocks * (blocks - 1) // 2 + UNROLL_BACK
    mode = buffers(count)
    by_slot = lambda *shape: pl.BlockSpec((None,) + shape, lambda s, *_: (s,) + (0,) * len(shape), pipeline_mode=mode)
    raw_spec = pl.BlockSpec((count, 3, None, HDIM, 2 * BLK), lambda s, *_: (0, 0, s, 0, 0), pipeline_mode=mode)
    place_spec = lambda rows: pl.BlockSpec((count, None, rows, 2 * BLK), lambda s, *_: (0, s, 0, 0), pipeline_mode=mode)
    return pl.pallas_call(
        functools.partial(backward_kernel, count),
        grid_spec=pltpu.PrefetchScalarGridSpec(
            num_scalar_prefetch=3,
            grid=(2,),
            in_specs=[
                raw_spec,
                place_spec(8),
                by_slot(HDIM, 2),
                place_spec(HDIM),
                by_slot(blocks, HDIM, BLK),
                by_slot(blocks + 1, 128, BLK),
                by_slot(blocks, BLK, 128),
                by_slot(blocks, 80, BLK),
                by_slot(blocks, 80, BLK),
            ],
            out_specs=[raw_spec, place_spec(8), by_slot(HDIM, 2)],
            scratch_shapes=[
                pltpu.VMEM((blocks + 1, 128, BLK), bf16),
                pltpu.VMEM((blocks, BLK, 128), bf16),
                pltpu.VMEM((count, 2 * BLK), f32),
                pltpu.VMEM((blocks + 1, 80, BLK), f32),
                pltpu.VMEM((blocks, 80, BLK), f32),
                pltpu.VMEM((blocks, HDIM, BLK), f32),
                pltpu.SMEM((most,), jnp.int32),
                pltpu.SMEM((blocks + UNROLL_BACK,), jnp.int32),
            ],
        ),
        out_shape=[
            jax.ShapeDtypeStruct(raw.shape, bf16),
            jax.ShapeDtypeStruct(logits.shape, f32),
            jax.ShapeDtypeStruct(gains.shape, f32),
        ],
        compiler_params=pltpu.CompilerParams(vmem_limit_bytes=60 * 2**20),
        name="attend_backward",
    )(device, skip, bias, raw, logits, gains, dmixed, mixed, q, k, kt, vt)


def holder(head, place, count):
    return (head * count + place) // HEADS


def greet(count):
    me = lax.axis_index("seq")
    barrier = pltpu.get_barrier_semaphore()
    for k in range(1, count):
        peer = lax.rem(me + k, count)
        pl.semaphore_signal(barrier, inc=1, device_id={"seq": peer}, device_id_type=MESH)
    pl.semaphore_wait(barrier, count - 1)
    return me


def far_first(count):
    return sorted(range(1, count), key=lambda k: -min(k, count - k))


def push(src, dst, send, recv, peer):
    return pltpu.make_async_remote_copy(
        src_ref=src, dst_ref=dst, send_sem=send, recv_sem=recv, device_id={"seq": peer}, device_id_type=MESH
    )


def heads_out_kernel(count, x_ref, logit_in, raw_ref, logit_ref, send, recv, local):
    me = greet(count)

    def copies(peer, source, k):
        head = first_head(peer, count)
        items = []
        for slot in range(2):
            items.append((is_mine(peer, slot, me, count), is_mine(me, slot, source, count),
                          push(x_ref.at[0, head + slot], raw_ref.at[me, 0, slot], send.at[k, slot], recv.at[k, slot], peer)))
        items.append((None, None, push(x_ref.at[pl.ds(1, 2), pl.ds(head, 2)], raw_ref.at[me, pl.ds(1, 2)], send.at[k, 2], recv.at[k, 2], peer)))
        items.append((None, None, push(logit_in.at[pl.ds(head, 2)], logit_ref.at[me], send.at[k, 3], recv.at[k, 3], peer)))
        return items

    every = []
    for k in far_first(count):
        items = copies(lax.rem(me + k, count), lax.rem(me + count - k, count), k)
        every.append(items)
        for out, _, copy in items:
            if out is None:
                copy.start()
            else:
                pl.when(out)(copy.start)
    head = first_head(me, count)
    own = [
        pltpu.make_async_copy(x_ref.at[:, pl.ds(head, 2)], raw_ref.at[me], local.at[0]),
        pltpu.make_async_copy(logit_in.at[pl.ds(head, 2)], logit_ref.at[me], local.at[1]),
    ]
    for copy in own:
        copy.start()
    for items in every:
        for out, into, copy in items:
            if out is None:
                copy.wait()
            else:
                pl.when(out)(copy.wait_send)
                pl.when(into)(copy.wait_recv)
    for copy in own:
        copy.wait()


def heads_out(qkv, logits, count):
    return pl.pallas_call(
        functools.partial(heads_out_kernel, count),
        out_shape=[
            jax.ShapeDtypeStruct((count, 3, 2, HDIM, 2 * BLK), bf16),
            jax.ShapeDtypeStruct((count, 2, 8, 2 * BLK), f32),
        ],
        in_specs=[ANY, ANY],
        out_specs=[ANY, ANY],
        scratch_shapes=[pltpu.SemaphoreType.DMA((count, 4)), pltpu.SemaphoreType.DMA((count, 4)), pltpu.SemaphoreType.DMA((2,))],
        compiler_params=pltpu.CompilerParams(collective_id=0, has_side_effects=True),
        name="heads_out",
    )(qkv, logits)


def mixed_back_kernel(count, x_ref, o_ref, send, recv, local):
    me = greet(count)
    first = first_head(me, count)
    started = []
    for k in far_first(count) + [0]:
        peer = lax.rem(me + k, count)
        for slot in range(2):
            mine = is_mine(me, slot, peer, count)
            src, dst = x_ref.at[slot, peer], o_ref.at[first + slot]
            if k:
                copy = push(src, dst, send.at[k, slot], recv.at[first + slot], peer)
            else:
                copy = pltpu.make_async_copy(src, dst, local.at[slot])
            started.append((mine, k, copy))
            pl.when(mine)(copy.start)
    for mine, k, copy in started:
        pl.when(mine)(copy.wait_send if k else copy.wait)
    for head in range(HEADS):
        source = holder(head, me, count)
        copy = push(x_ref.at[0, 0], o_ref.at[head], send.at[0, 0], recv.at[head], lax.rem(me + 1, count))
        pl.when(source != me)(copy.wait_recv)


def mixed_back(mixed, count):
    return pl.pallas_call(
        functools.partial(mixed_back_kernel, count),
        out_shape=jax.ShapeDtypeStruct((HEADS, HDIM, 2 * BLK), bf16),
        in_specs=[ANY],
        out_specs=ANY,
        scratch_shapes=[pltpu.SemaphoreType.DMA((count, 2)), pltpu.SemaphoreType.DMA((HEADS,)), pltpu.SemaphoreType.DMA((2,))],
        compiler_params=pltpu.CompilerParams(collective_id=1, has_side_effects=True),
        name="mixed_back",
    )(mixed)


def grads_out_kernel(count, x_ref, o_ref, send, recv, local):
    me = greet(count)
    started = []
    for head in range(HEADS):
        peer = holder(head, me, count)
        slot = head - first_head(peer, count)
        away = peer != me
        there = jnp.where(away, peer, lax.rem(me + 1, count))
        copy = push(x_ref.at[head], o_ref.at[me, slot], send.at[head], recv.at[me, slot], there)
        own = pltpu.make_async_copy(x_ref.at[head], o_ref.at[me, slot], local.at[slot])
        pl.when(away)(copy.start)
        pl.when(peer == me)(own.start)
        started.append((away, peer == me, copy, own))
    for away, here, copy, own in started:
        pl.when(away)(copy.wait_send)
        pl.when(here)(own.wait)
    for k in range(1, count):
        source = lax.rem(me + k, count)
        for slot in range(2):
            copy = push(x_ref.at[0], o_ref.at[source, slot], send.at[0], recv.at[source, slot], source)
            pl.when(is_mine(me, slot, source, count))(copy.wait_recv)


def grads_out(d_mixed, count):
    return pl.pallas_call(
        functools.partial(grads_out_kernel, count),
        out_shape=jax.ShapeDtypeStruct((count, 2, HDIM, 2 * BLK), bf16),
        in_specs=[ANY],
        out_specs=ANY,
        scratch_shapes=[pltpu.SemaphoreType.DMA((HEADS,)), pltpu.SemaphoreType.DMA((count, 2)), pltpu.SemaphoreType.DMA((2,))],
        compiler_params=pltpu.CompilerParams(collective_id=2, has_side_effects=True),
        name="grads_out",
    )(d_mixed)


def heads_back_kernel(count, x_ref, logit_in, q_ref, kv_ref, logit_ref, send, recv, recv_q, local):
    me = greet(count)
    first = first_head(me, count)
    started = []
    for k in far_first(count) + [0]:
        peer = lax.rem(me + k, count)
        pairs = [
            (None, x_ref.at[peer, pl.ds(1, 2)], kv_ref.at[me], recv.at[k, 0]),
            (None, logit_in.at[peer], logit_ref.at[me], recv.at[k, 1]),
        ]
        for slot in range(2):
            pairs.append((is_mine(me, slot, peer, count), x_ref.at[peer, 0, slot], q_ref.at[first + slot], recv_q.at[first + slot]))
        for i, (mine, src, dst, sem) in enumerate(pairs):
            copy = push(src, dst, send.at[k, i], sem, peer) if k else pltpu.make_async_copy(src, dst, local.at[i])
            started.append((mine, k, copy))
            if mine is None:
                copy.start()
            else:
                pl.when(mine)(copy.start)
    for mine, k, copy in started:
        if mine is not None:
            pl.when(mine)(copy.wait_send if k else copy.wait)
        else:
            copy.wait()
    for head in range(HEADS):
        source = holder(head, me, count)
        copy = push(x_ref.at[0, 0, 0], q_ref.at[head], send.at[0, 0], recv_q.at[head], lax.rem(me + 1, count))
        pl.when(source != me)(copy.wait_recv)


def heads_back(d_raw, d_logits, count):
    return pl.pallas_call(
        functools.partial(heads_back_kernel, count),
        out_shape=[
            jax.ShapeDtypeStruct((HEADS, HDIM, 2 * BLK), bf16),
            jax.ShapeDtypeStruct((count, 2, 2, HDIM, 2 * BLK), bf16),
            jax.ShapeDtypeStruct((count, 2, 8, 2 * BLK), f32),
        ],
        in_specs=[ANY, ANY],
        out_specs=[ANY, ANY, ANY],
        scratch_shapes=[
            pltpu.SemaphoreType.DMA((count, 4)),
            pltpu.SemaphoreType.DMA((count, 2)),
            pltpu.SemaphoreType.DMA((HEADS,)),
            pltpu.SemaphoreType.DMA((4,)),
        ],
        compiler_params=pltpu.CompilerParams(collective_id=3, has_side_effects=True),
        name="heads_back",
    )(d_raw, d_logits)


def dot(a, b, i, j):
    return lax.dot_general(a, b, (((i,), (j,)), ((), ())), preferred_element_type=f32)


def rms_scale(values, gains):
    inverse = lax.rsqrt(jnp.mean(values * values, axis=-1, keepdims=True) + EPS)
    return values * inverse * gains


def swiglu(gate_up):
    return jax.nn.silu(gate_up[:, :FF]) * gate_up[:, FF:]


def held_heads(count):
    first = [min(HEADS * d // count, HEADS - 2) for d in range(count)]
    return [
        [(d, h - first[d]) for d in range(h * count // HEADS, ((h + 1) * count - 1) // HEADS + 1)]
        for h in range(HEADS)
    ]


def total(parts):
    return functools.reduce(jnp.add, parts)


def local(tokens, cotangent, skip_table, gain_attn, w_attn, w_heads, forget_bias, query_gain, key_gain,
          w_out, gain_ffn, w_gate_up, w_down):
    count = lax.axis_size("seq")
    me = lax.axis_index("seq")
    rows = tokens.shape[1]
    both = ("seq", "group")
    inputs = tokens[0].astype(f32)
    device = me.astype(jnp.int32)[None]
    head = first_head(me, count)
    skip = skip_table[0]
    gains = jnp.stack([query_gain.reshape(HEADS, HDIM), key_gain.reshape(HEADS, HDIM)], 2)
    gains = lax.dynamic_slice_in_dim(gains, head, 2, 0)
    bias = lax.dynamic_slice_in_dim(forget_bias, head, 2, 0)
    w_small = jnp.pad(w_heads.reshape(D, 3, HEADS).transpose(0, 2, 1), ((0, 0), (0, 0), (0, 5))).reshape(D, HEADS * 8)

    normed_attn, norm_back_attn = jax.vjp(rms_scale, inputs, gain_attn)
    h_first = normed_attn.astype(bf16)
    qkv = dot(w_attn[:, : 3 * D], h_first, 0, 1).astype(bf16).reshape(3, HEADS, HDIM, rows)
    gate_logit = dot(w_attn[:, 3 * D :], h_first, 0, 1)
    logits_here = dot(w_small, h_first, 0, 1).reshape(HEADS, 8, rows)

    raw, logits = heads_out(qkv, logits_here, count)
    mixed_low, mixed, q, k, kt, vt = attend_forward(device, skip, bias, raw, logits, gains)
    attended = mixed_back(mixed_low, count).reshape(D, rows).astype(f32)

    gate_open = jax.nn.sigmoid(gate_logit)
    gated = (gate_open * attended).astype(bf16)
    resid = inputs + dot(gated, w_out, 0, 0)
    normed_ffn, norm_back_ffn = jax.vjp(rms_scale, resid, gain_ffn)
    h_second = normed_ffn.astype(bf16)
    gate_up = dot(h_second, w_gate_up, 1, 0)
    hidden, hidden_back = jax.vjp(swiglu, gate_up)
    hidden_low = hidden.astype(bf16)
    output = resid + dot(hidden_low, w_down, 1, 0)
    d_low = cotangent[0]
    d_output = d_low.astype(f32)
    (d_gate_up,) = hidden_back(dot(d_low, w_down, 1, 1))
    d_gate_low = d_gate_up.astype(bf16)
    d_resid_norm, grad_gain_ffn = norm_back_ffn(dot(d_gate_low, w_gate_up, 1, 1))
    d_resid = d_output + d_resid_norm
    d_branch = d_resid.astype(bf16)
    d_gated = dot(w_out, d_branch, 1, 1)
    d_gate_logit = (d_gated * attended * gate_open * (1.0 - gate_open)).astype(bf16)
    d_mixed = (d_gated * gate_open).astype(bf16).reshape(HEADS, HDIM, rows)

    grad_w_down = dot(hidden_low, d_low, 0, 0).astype(bf16)
    grad_w_gate_up = dot(h_second, d_gate_low, 0, 0).astype(bf16)
    grad_w_out = dot(gated, d_branch, 1, 0).astype(bf16)
    grad_gate = dot(h_first, d_gate_logit, 0, 1).astype(bf16)
    early = lax.psum((grad_w_down, grad_w_gate_up, grad_w_out, grad_gate), both)

    d_mixed_all = grads_out(d_mixed, count)
    d_raw, d_logits, d_gains = attend_backward(device, skip, bias, raw, logits, gains, d_mixed_all, mixed, q, k, kt, vt)
    d_q, d_kv_parts, d_logit_parts = heads_back(d_raw, d_logits, count)

    holders = held_heads(count)
    d_kv = [
        jnp.concatenate([total([d_kv_parts[d, i, s].astype(f32) for d, s in held]) for held in holders], 0).astype(bf16)
        for i in range(2)
    ]
    d_small = jnp.concatenate([total([d_logit_parts[d, s] for d, s in held]) for held in holders], 0)
    d_small_low = d_small.astype(bf16)
    d_projected = jnp.concatenate([d_q.reshape(D, rows), d_kv[0], d_kv[1], d_gate_logit], 0)
    grad_qkv = dot(h_first, d_projected[: 3 * D], 0, 1).astype(bf16)
    grad_small = dot(h_first, d_small_low, 0, 1)
    d_normed = dot(d_projected, w_attn, 0, 1) + dot(d_small_low, w_small, 0, 1)
    d_inputs_norm, grad_gain_attn = norm_back_attn(d_normed)
    d_inputs = d_resid + d_inputs_norm

    grad_bias = jnp.sum(d_small.reshape(HEADS, 8, rows)[:, 0], axis=1)
    placed = jnp.zeros((HEADS, HDIM, 2), f32)
    placed = lax.dynamic_update_slice(placed, d_gains, (head, 0, 0)).reshape(D, 2)
    grad_qkv, early = lax.optimization_barrier((grad_qkv, early))
    late, small = lax.psum((grad_qkv, (grad_small, grad_gain_ffn, grad_gain_attn, grad_bias, placed)), both)
    grad_small, grad_gain_ffn, grad_gain_attn, grad_bias, placed = small
    grad_w_heads = grad_small.reshape(D, HEADS, 8)[:, :, :3].transpose(0, 2, 1).reshape(D, 3 * HEADS)
    grad_w_attn = jnp.concatenate([late, early[3]], 1).astype(f32)
    return (
        output[None].astype(bf16),
        d_inputs[None],
        grad_gain_attn,
        grad_w_attn,
        grad_w_heads,
        grad_bias,
        placed[:, 0],
        placed[:, 1],
        early[2].astype(f32),
        grad_gain_ffn,
        early[1].astype(f32),
        early[0].astype(f32),
    )


def solution(mesh):
    rows = P("group", "seq", None)
    return jax.shard_map(
        local,
        mesh=mesh,
        in_specs=(rows, rows, P("group", None, None)) + (P(),) * 10,
        out_specs=(rows, rows) + (P(),) * 10,
        check_vma=False,
    )
```

time: 2450 us -> 793 us (0.32)
  local copies, waits for them, and re-layouts: 625 us -> 94.7 us
  waiting for transfers between devices: 688 us -> 241 us
  matrix products: 486 us -> 69.1 us
  loops' own time: 327 us -> 0 us
  Pallas kernels: 0 us -> 272 us
  other arithmetic: 200 us -> 48.2 us
  blocking collectives: 72 us -> 40 us
    dot_general x127 -> x17, matrix products: 486 us -> 69.1 us  [dot(): lax.dot_general(a, b, (((i,), (j,)), ((), ())), preferred_element_type=f32)]
    another operation x51 -> x0, loops' own time: 327 us -> none  [the longest x1 66.2 us: local(): lax.scan(grad_step, start_grads, (back_key_blocks, back_value_blocks, cum...]
    dynamic_slice x241 -> x1, local copies, waits for them, and re-layouts: 276 us -> 1.24 us  [local(): bias = lax.dynamic_slice_in_dim(forget_bias, head, 2, 0)]
    pallas_call x0 -> x6, Pallas kernels: none -> 272 us  [the longest x1 68 us: heads_back(): pl.pallas_call(functools.partial(heads_back_kernel, count), out_shape=[ja...]
    reduce_scatter x3 -> x0, waiting for transfers between devices: 244 us -> none  [the longest x1 120 us: local(): lax.psum_scatter(key_terms.astype(jnp.bfloat16), 'seq', scatter_dimension...]
    psum x1 -> x3, waiting for transfers between devices: 407 us -> 241 us  [the longest x2 209 us: local(): lax.psum((grad_qkv, (grad_small, grad_gain_ffn, grad_gain_attn, grad_bias...]
    eq x48 -> x0, other arithmetic: 70.5 us -> none  [scores(): allowed = (key_pos[None, :] <= query_pos[:, None]) & (dropped[:, None] == 0)]
    reduce_sum x23 -> x1, other arithmetic: 68 us -> 0.17 us  [local(): grad_bias = jnp.sum(d_small.reshape(HEADS, 8, rows)[:, 0], axis=1)]
  transfers between devices with their start and end apart: 10 -> 3, of which waited for: 7 -> 3; matrix products, arithmetic and copies ran while one was open for 16% -> 18% of each run, Pallas kernels for 0% -> 19%
where the time goes in v1:
time: 793 us; the launch traced here: 779 us
  Pallas kernels  272 us (34%)
  waiting for transfers between devices  241 us (30%)
  local copies, waits for them, and re-layouts  94.7 us (12%)
  matrix products  69.1 us (9%)
  other arithmetic  48.2 us (6%)
  blocking collectives  40 us (5%)
  between operations  14.6 us (2%)
    psum x2, waiting for transfers between devices, local(): lax.psum((grad_qkv, (grad_small, grad_gain_ffn, grad_gain_attn, grad_bias...  209 us
    dot_general x17, matrix products, dot(): lax.dot_general(a, b, (((i,), (j,)), ((), ())), preferred_element_type=f32)  69.1 us
    pallas_call x1, Pallas kernels, heads_back(): pl.pallas_call(functools.partial(heads_back_kernel, count), out_shape=[ja...  68 us
    pallas_call x1, Pallas kernels, heads_out(): pl.pallas_call(functools.partial(heads_out_kernel, count), out_shape=[jax...  60.4 us
    pallas_call x1, Pallas kernels, attend_backward(): pl.pallas_call(functools.partial(backward_kernel, count), grid_spec=pltpu...  51.5 us
    psum x1, blocking collectives, local(): lax.psum((grad_qkv, (grad_small, grad_gain_ffn, grad_gain_attn, grad_bias...  40 us
    pallas_call x1, Pallas kernels, mixed_back(): pl.pallas_call(functools.partial(mixed_back_kernel, count), out_shape=jax...  33.9 us
    unnamed x74, local copies, waits for them, and re-layouts  31.2 us
  transfers between devices with their start and end apart: 3, of which 3 were waited for; matrix products, arithmetic and copies ran while one was open for 18% of the time, Pallas kernels for 19%

profile of v1, /device:TPU:0, one launch (start us, length us, event | category | flops | bytes accessed | tf_op | source)
XLA Modules:
  0.0 779.4 jit_solution(3467155911076537457)
XLA Ops:
  8.8 5.8 fusion.3
  14.5 4.3 copy.159
  25.0 60.4 %heads_out.1 = (bf16[8,3,2,64,512]{4,3,2,1,0:T(8,128)(2,1)}, f32[8,2,8,512]{3,2,1,0:T(8,128)}) custom-call(bf16[3,12,64,512]{3,2,1,0:T(8,128)(2,1)} %bitcast.232, f32[12,8,512]{2,1,0:T(8,128)} %fusion.29.logit_in), custom_call_target="tpu_custom_call" | custom-call | tf_op jit(solution)/shard_map/heads_out/pallas_call | solution.py:458
  87.0 27.7 %attend_forward.1 = (bf16[2,8,64,512]{3,2,1,0:T(8,128)(2,1)}, f32[2,16,64,256]{3,2,1,0:T(8,128)}, bf16[2,17,128,256]{3,2,1,0:T(8,128)(2,1)}, bf16[2,16,256,128]{...) custom-call(s32[1]{0:T(128)} %bitcast.2.device_ref, s32[16,16]{1,0:T(8,128)} %bitcast.240, ...), custom_call_target="tpu_custom_call" | custom-call | tf_op jit(solution)/shard_map/attend_forward/pallas_call | solution.py:209
  114.7 33.9 %mixed_back.1 = bf16[12,64,512]{2,1,0:T(8,128)(2,1)} custom-call(bf16[2,8,64,512]{3,2,1,0:T(8,128)(2,1)} %get-tuple-element.33.x_ref), custom_call_target="tpu_custom_call" | custom-call | tf_op jit(solution)/shard_map/mixed_back/pallas_call | solution.py:496
  158.2 6.2 fusion.58
  164.5 5.6 fusion.37
  170.1 6.5 multiply_reduce_fusion
  176.6 9.8 %convolution_convert_fusion = bf16[768,4096]{1,0:T(8,128)(2,1)} fusion(f32[512,2048]{1,0:T(8,128)} %get-tuple-element.81, f32[512,2048]{1,0:T(8,128)} %get-tuple-element.80, f32[512,768]{1,0:T(8,128)S(1)} %get-tuple-element.104, f32[768]{0:T(1024)S(1)} %copy-done.16, f32[512]{0:T(512)S(1)} %fusion.53), kind=kOutput, calls=%fused_computation.1 | convolution fusion | flops 3229745152 | bytes 16258048 | tf_op jit(solution)/shard_map/dot_general | solution.py:594
  191.1 3.5 convolution_convert_fusion.3
  199.0 30.3 %grads_out.1.dmixed_ref = bf16[8,2,64,512]{3,2,1,0:T(8,128)(2,1)} custom-call(bf16[12,64,512]{2,1,0:T(8,128)(2,1)} %bitcast.235), custom_call_target="tpu_custom_call" | custom-call | tf_op jit(solution)/shard_map/grads_out/pallas_call | solution.py:531
  229.3 51.5 %attend_backward.1 = (bf16[8,3,2,64,512]{4,3,2,1,0:T(8,128)(2,1)}, f32[8,2,8,512]{3,2,1,0:T(8,128)}, f32[2,64,2]{2,1,0:T(8,128)}) custom-call(s32[1]{0:T(128)} %bitcast.2.device_ref, s32[16,16]{1,0:T(8,128)} %bitcast.241, f32[2]{0:T(128)} %dynamic_slice.6.bias_ref, bf16[8,3,2,64,512]{4,3,2,1,0:T(8,128)(2,1)} %get-tuple-element.31.raw_ref, ...), custom_call_target="tpu_custom_call" | custom-call | tf_op jit(solution)/shard_map/attend_backward/pallas_call | solution.py:355
  280.8 68.0 %heads_back.1 = (bf16[12,64,512]{2,1,0:T(8,128)(2,1)}, bf16[8,2,2,64,512]{4,3,2,1,0:T(8,128)(2,1)}, f32[8,2,8,512]{3,2,1,0:T(8,128)}) custom-call(bf16[8,3,2,64,512]{4,3,2,1,0:T(8,128)(2,1)} %get-tuple-element.39.x_ref, f32[8,2,8,512]{3,2,1,0:T(8,128)} %get-tuple-element.40.logit_in), custom_call_target="tpu_custom_call" | custom-call | tf_op jit(solution)/shard_map/heads_back/pallas_call | solution.py:573
  436.6 7.3 concatenate.18
  443.9 7.3 fusion.72
  452.0 4.1 convolution_convert_fusion.1
  456.6 31.2 %all-reduce.13.cloned.1.call-done = (bf16[2048,768]{1,0:T(8,128)(2,1)}, bf16[768,4096]{1,0:T(8,128)(2,1)}, bf16[768,768]{1,0:T(8,128)(2,1)}, bf16[768,768]{1,0:T(8,128)(2,1)}) async-done(((bf16[2048,768]{1,0:T(8,128)(2,1)}, bf16[768,4096]{1,0:T(8,128)(2,1)}, bf16[768,768]{1,0:T(8,128)(2,1)}, bf16[768,768]{1,0:T(8,128)(2,1)}), (bf16[2048,768]{1,0:T(8,128)(2,1)}, bf16[768,4096]{1,0:T(8,128)(2,1)}, ...) | async-done | bytes 11796496 | tf_op jit(solution)/shard_map/psum | solution.py:667
  487.8 3.4 fusion.13
  491.3 40.0 %all-reduce.3 = (f32[768]{0:T(1024)}, f32[12]{0:T(128)}, f32[768,2]{0,1:T(2,128)S(1)}, f32[768]{0:T(1024)}) all-reduce(f32[768]{0:T(1024)S(1)} %get-tuple-element.52, f32[12]{0:T(128)S(1)} %slice_reduce_fusion, f32[768,2]{0,1:T(2,128)S(1)} %reshape.188, f32[768]{0:T(1024)S(1)} %get-tuple-element.50), channel_id=1, replica_groups=mesh['seq'=8,'group'=4] {'seq','group'}, use_global_device_ids=true, to_apply=%region_5.6 | all-reduce | flops 3084 | bytes 24672 | tf_op jit(solution)/shard_map/psum | solution.py:691
  531.9 3.8 fusion.20
  538.4 79.7 %all-reduce.11.cloned.1.call-done = f32[768,12,8]{0,2,1:T(8,128)} async-done(((f32[768,12,8]{0,2,1:T(8,128)}), f32[768,12,8]{0,2,1:T(8,128)}) %all-reduce.11.cloned.1.call-update) | async-done | bytes 294928 | tf_op jit(solution)/shard_map/psum | solution.py:691
  622.7 9.5 %convert_element_type.281 = f32[768,4096]{1,0:T(8,128)} convert(bf16[768,4096]{1,0:T(8,128)(2,1)} %get-tuple-element.48) | non-fusion elementwise | flops 3145728 | bytes 18874368 | tf_op jit(solution)/shard_map/convert_element_type | solution.py:706
  635.3 129.8 %all-reduce.9.cloned.1.call-done = bf16[768,2304]{1,0:T(8,128)(2,1)} async-done(((bf16[768,2304]{1,0:T(8,128)(2,1)}), bf16[768,2304]{1,0:T(8,128)(2,1)}) %all-reduce.9.cloned.1.call-update) | async-done | bytes 3538960 | tf_op jit(solution)/shard_map/psum | solution.py:691
  765.1 7.4 maximum_convert_fusion
  (154 shorter events, 127.8 us)
Async XLA Ops:
  7.2 157.3 %copy-start = (bf16[2048,768]{1,0:T(8,128)(2,1)S(1)}, bf16[2048,768]{1,0:T(8,128)(2,1)}, u32[]{:S(2)}) copy-start(bf16[2048,768]{1,0:T(8,128)(2,1)} %param.25) | copy-start | bytes 9437188
  7.2 480.6 %all-reduce.13.cloned.1.call-start = ((), (), s32[]{:S(2)}) async-start(), calls=%async_computation.2 | async-start | bytes 23592960 | tf_op jit(solution)/shard_map/psum | solution.py:667
  14.5 4.3 copy-start.18
  14.5 5.0 copy-start.19
  14.5 7.3 copy-start.20
  154.1 3.2 copy-start.2
  154.1 3.2 copy-start.9
  158.2 28.3 %copy-start.5 = (f32[512,768]{1,0:T(8,128)}, f32[512,768]{1,0:T(8,128)S(1)}, u32[]{:S(2)}) copy-start(f32[512,768]{1,0:T(8,128)S(1)} %get-tuple-element.104) | copy-start | bytes 4718596
  158.2 6.3 copy-start.10
  158.2 11.9 %slice-start = ((s8[6291456]{0:T(1024)(128)(4,1)}), s8[4194304]{0:T(1024)(128)(4,1)S(1)}, s32[]{:S(2)}) async-start(s8[6291456]{0:T(1024)(128)(4,1)} %bitcast.233), calls=%async_computation.3 | async-start | bytes 8388608
  164.5 5.7 slice-start.1
  186.9 4.3 copy-start.1
  186.9 2.4 copy-start.4
  191.1 3.5 copy-start.8
  196.6 421.5 %all-reduce.11.cloned.1.call-start = ((), (), s32[]{:S(2)}) async-start(), calls=%async_computation.1 | async-start | bytes 589824 | tf_op jit(solution)/shard_map/psum | solution.py:691
  360.6 404.5 %all-reduce.9.cloned.1.call-start = ((), (), s32[]{:S(2)}) async-start(), calls=%async_computation | async-start | bytes 7077888 | tf_op jit(solution)/shard_map/psum | solution.py:691
  443.9 7.3 copy-start.15
  443.9 8.1 %copy-start.3 = (bf16[1,512,768]{2,1,0:T(8,128)(2,1)S(1)}, bf16[1,512,768]{2,1,0:T(8,128)(2,1)}, u32[]{:S(2)}) copy-start(bf16[1,512,768]{2,1,0:T(8,128)(2,1)} %param.13) | copy-start | bytes 2359300
  452.0 4.1 copy-start.17
  452.0 4.3 copy-start.14
  456.1 31.7 %copy-start.12 = (bf16[768,12,3]{0,2,1:T(4,128)(2,1)S(1)}, bf16[768,12,3]{0,2,1:T(4,128)(2,1)}, u32[]{:S(2)}) copy-start(bf16[768,12,3]{0,2,1:T(4,128)(2,1)} %copy-done.11) | copy-start | bytes 165892
  531.9 3.9 copy-start.6
  531.9 3.9 copy-start.22
  622.7 9.5 %copy-start.7 = (bf16[2048,768]{1,0:T(8,128)(2,1)S(1)}, bf16[2048,768]{1,0:T(8,128)(2,1)}, u32[]{:S(2)}) copy-start(bf16[2048,768]{1,0:T(8,128)(2,1)} %get-tuple-element.49) | copy-start | bytes 9437188
  (4 other events, 4.1 us)
Sparse Core Ops, SparseCore 0:
  196.8 290.9 all-reduce.12
  493.1 124.9 all-reduce.10
  625.3 139.7 all-reduce.8

commit v2 on v1

--- a/solution.py
+++ b/solution.py
@@ -594,13 +594,95 @@
     return lax.dot_general(a, b, (((i,), (j,)), ((), ())), preferred_element_type=f32)
 
 
-def rms_scale(values, gains):
-    inverse = lax.rsqrt(jnp.mean(values * values, axis=-1, keepdims=True) + EPS)
-    return values * inverse * gains
-
-
-def swiglu(gate_up):
-    return jax.nn.silu(gate_up[:, :FF]) * gate_up[:, FF:]
+SMALL = 48
+UNIT = 16
+PIECE = 8
+
+
+def group_bits(group_count, count):
+    bits = [("group", 1 << i) for i in range(group_count.bit_length() - 1)]
+    return bits, [("seq", 1 << i) for i in range(count.bit_length() - 1)]
+
+
+def partner(bit):
+    axis, step = bit
+    here = lax.axis_index(axis)
+    side = lax.rem(here // step, 2)
+    return {axis: here + step - 2 * step * side}, side
+
+
+def greet_all(bits):
+    barrier = pltpu.get_barrier_semaphore()
+    for bit in bits:
+        there, _ = partner(bit)
+        pl.semaphore_signal(barrier, inc=1, device_id=there, device_id_type=MESH)
+    pl.semaphore_wait(barrier, len(bits))
+
+
+def orders(near, far, seq):
+    rest = [far] + seq
+    return [[near] + rest[i:] + rest[:i] for i in range(3)]
+
+
+class Summing:
+    def __init__(self, base, size, order, own, landing, result, send, recv):
+        self.start, self.size, self.order = base, size, order
+        self.own, self.landing, self.result, self.send, self.recv = own, landing, result, send, recv
+        self.base, self.at, self.stage, self.copy = base, base, 0, None
+
+    def give(self):
+        there, side = partner(self.order[self.stage])
+        half = self.size // 2
+        self.keep = self.start + side * half
+        self.copy = pltpu.make_async_remote_copy(
+            src_ref=self.own.at[pl.ds(self.start + (1 - side) * half, half)],
+            dst_ref=self.landing.at[pl.ds(self.at, half)],
+            send_sem=self.send.at[self.stage], recv_sem=self.recv.at[self.stage],
+            device_id=there, device_id_type=MESH,
+        )
+        self.copy.start()
+
+    def add(self):
+        self.copy.wait()
+        half = self.size // 2
+        step = PIECE if half % PIECE == 0 else 1
+        keep, at, own, landing = self.keep, self.at, self.own, self.landing
+
+        def piece(i, carried):
+            mine = pl.ds(keep + i * step, step)
+            theirs = landing[pl.ds(at + i * step, step)].astype(f32)
+            own[mine] = (own[mine].astype(f32) + theirs).astype(bf16)
+            return carried
+
+        lax.fori_loop(0, half // step, piece, 0)
+        self.start, self.size, self.at, self.stage = keep, half, at + half, self.stage + 1
+
+    def settle(self, sem):
+        copy = pltpu.make_async_copy(
+            self.own.at[pl.ds(self.start, self.size)], self.result.at[pl.ds(self.start, self.size)], sem
+        )
+        copy.start()
+        copy.wait()
+        self.left = len(self.order)
+
+    def spread(self):
+        self.left -= 1
+        there, side = partner(self.order[self.left])
+        part = self.result.at[pl.ds(self.start, self.size)]
+        stage = 2 * len(self.order) - 1 - self.left
+        self.copy = pltpu.make_async_remote_copy(
+            src_ref=part, dst_ref=part, send_sem=self.send.at[stage], recv_sem=self.recv.at[stage],
+            device_id=there, device_id_type=MESH,
+        )
+        self.copy.start()
+        self.start, self.size = self.start - side * self.size, 2 * self.size
+
+    def gathered(self):
+        self.copy.wait()
+
+
+def total(parts):
+    return functools.reduce(jnp.add, parts)
 
 
 def held_heads(count):
@@ -611,8 +693,141 @@
     ]
 
 
-def total(parts):
-    return functools.reduce(jnp.add, parts)
+def part_sizes(units, least):
+    pieces = units // least
+    return [least * ((pieces + 2 - i) // 3) for i in range(3)]
+
+
+def last_kernel(count, sets, h_ref, dq_ref, dkv_ref, dlogit_ref, dgate_ref, w_ref, wsmall_ref, x_ref, gain_ref,
+                dresid_ref, extra_ref, grads_ref, dx_ref, small_ref,
+                proj_ref, ht_ref, dsmall_ref, rows_ref, dn_ref, g_ref, land_ref, small_land, send, recv, ssend, srecv, local):
+    near, far, seq = sets
+    bits = [near, far] + seq
+    greet_all(bits)
+    rows = h_ref.shape[0]
+    holders = held_heads(count)
+    proj_ref[0:D] = dq_ref[...].reshape(D, rows)
+    for head, held in enumerate(holders):
+        for i in range(2):
+            start = D * (1 + i) + head * HDIM
+            if len(held) == 1:
+                d, s = held[0]
+                proj_ref[start : start + HDIM] = dkv_ref[d, i, s]
+            else:
+                proj_ref[start : start + HDIM] = total([dkv_ref[d, i, s].astype(f32) for d, s in held]).astype(bf16)
+        dsmall_ref[8 * head : 8 * head + 8] = total([dlogit_ref[d, s] for d, s in held])
+    proj_ref[3 * D :] = dgate_ref[...]
+    for i in range(3):
+        cols = slice(256 * i, 256 * i + 256)
+        ht_ref[cols, :] = h_ref[:, cols].astype(f32).T.astype(bf16)
+
+    def block(i, carried):
+        part = mm(ht_ref[...], proj_ref[pl.ds(pl.multiple_of(i * 256, 256), 256)], NT).astype(bf16)
+        g_ref[pl.ds(i * (D // UNIT), D // UNIT)] = part.reshape(D // UNIT, UNIT, 256)
+        return carried
+
+    lax.fori_loop(0, 9, block, 0)
+    used = 9 * (D // UNIT)
+    units = g_ref.shape[0]
+    g_ref[used:] = jnp.zeros((units - used, UNIT, 256), bf16)
+
+    sums, base = [], 0
+    for i, size in enumerate(part_sizes(units, 1 << len(bits))):
+        sums.append(Summing(base, size, orders(near, far, seq)[i], g_ref, land_ref, grads_ref, send.at[i], recv.at[i]))
+        base += size
+    for part in sums:
+        part.give()
+
+    low_small = dsmall_ref[...].astype(bf16)
+    for i in range(3):
+        cols = slice(256 * i, 256 * i + 256)
+        part = mm(w_ref[cols, :], proj_ref[...]) + mm(wsmall_ref[cols, :], low_small)
+        dn_ref[:, cols] = part.T
+    small = mm(low_small, h_ref[...])
+    for head in range(HEADS):
+        rows_ref[3 * head : 3 * head + 3] = small[8 * head : 8 * head + 3]
+    rows_ref[3 * HEADS :] = extra_ref[...]
+    gain = gain_ref[...]
+    dgain = jnp.zeros((1, D), f32)
+    for i in range(rows // 128):
+        here = slice(128 * i, 128 * i + 128)
+        v, u = x_ref[here].astype(f32), dn_ref[here]
+        scale = lax.rsqrt(jnp.mean(v * v, 1, keepdims=True) + EPS)
+        hat, gu = v * scale, u * gain
+        dx_ref[here] = dresid_ref[here] + scale * (gu - hat * jnp.mean(hat * gu, 1, keepdims=True))
+        dgain = dgain + jnp.sum(hat * u, 0, keepdims=True)
+    rows_ref[3 * HEADS : 3 * HEADS + 1] = dgain
+    bias_rows = jnp.concatenate([dsmall_ref[8 * head : 8 * head + 1] for head in range(HEADS)], 0)
+    bias_sum = jnp.sum(bias_rows, 1, keepdims=True)
+    lane = lax.broadcasted_iota(jnp.int32, (HEADS, 128), 1)
+    row = lax.broadcasted_iota(jnp.int32, (HEADS, 128), 0)
+    rows_ref[3 * HEADS + 4 : 3 * HEADS + 5, 0:128] = jnp.sum(jnp.where(lane == row, bias_sum, 0.0), 0, keepdims=True)
+
+    for stage, bit in enumerate(bits):
+        there, _ = partner(bit)
+        swap = pltpu.make_async_remote_copy(
+            src_ref=rows_ref, dst_ref=small_land.at[stage], send_sem=ssend.at[stage], recv_sem=srecv.at[stage],
+            device_id=there, device_id_type=MESH,
+        )
+        swap.start()
+        for part in sums:
+            part.add()
+            if stage + 1 < len(bits):
+                part.give()
+            else:
+                part.settle(local)
+                part.spread()
+        swap.wait()
+        rows_ref[...] += small_land[stage]
+    for stage in range(len(bits)):
+        for part in sums:
+            part.gathered()
+            if stage + 1 < len(bits):
+                part.spread()
+    small_ref[...] = rows_ref[...]
+
+
+def last(count, groups, h, d_q, d_kv, d_logits, d_gate, w_attn, w_small, x, gain, d_resid, extra):
+    bits = group_bits(groups, count)
+    sets = (bits[0][0], bits[0][1], bits[1])
+    stages = len(bits[0]) + len(bits[1])
+    least = 1 << stages
+    units = -(-9 * (D // UNIT) // least) * least
+    rows = h.shape[0]
+    vmem = pl.BlockSpec(memory_space=pltpu.VMEM)
+    dma = pltpu.SemaphoreType.DMA
+    return pl.pallas_call(
+        functools.partial(last_kernel, count, sets),
+        out_shape=[
+            jax.ShapeDtypeStruct((units, UNIT, 256), bf16),
+            jax.ShapeDtypeStruct((rows, D), f32),
+            jax.ShapeDtypeStruct((SMALL, D), f32),
+        ],
+        in_specs=[vmem] * 11,
+        out_specs=[ANY, vmem, vmem],
+        scratch_shapes=[
+            pltpu.VMEM((4 * D, rows), bf16),
+            pltpu.VMEM((D, rows), bf16),
+            pltpu.VMEM((8 * HEADS, rows), f32),
+            pltpu.VMEM((SMALL, D), f32),
+            pltpu.VMEM((rows, D), f32),
+            pltpu.VMEM((units, UNIT, 256), bf16),
+            pltpu.VMEM((units, UNIT, 256), bf16),
+            pltpu.VMEM((stages, SMALL, D), f32),
+            dma((3, 2 * stages)), dma((3, 2 * stages)), dma((stages,)), dma((stages,)), dma,
+        ],
+        compiler_params=pltpu.CompilerParams(collective_id=4, has_side_effects=True, vmem_limit_bytes=62 * 2**20),
+        name="last",
+    )(h, d_q, d_kv, d_logits, d_gate, w_attn, w_small, x, gain, d_resid, extra)
+
+
+def rms_scale(values, gains):
+    inverse = lax.rsqrt(jnp.mean(values * values, axis=-1, keepdims=True) + EPS)
+    return values * inverse * gains
+
+
+def swiglu(gate_up):
+    return jax.nn.silu(gate_up[:, :FF]) * gate_up[:, FF:]
 
 
 def local(tokens, cotangent, skip_table, gain_attn, w_attn, w_heads, forget_bias, query_gain, key_gain,
@@ -670,39 +885,27 @@
     d_raw, d_logits, d_gains = attend_backward(device, skip, bias, raw, logits, gains, d_mixed_all, mixed, q, k, kt, vt)
     d_q, d_kv_parts, d_logit_parts = heads_back(d_raw, d_logits, count)
 
-    holders = held_heads(count)
-    d_kv = [
-        jnp.concatenate([total([d_kv_parts[d, i, s].astype(f32) for d, s in held]) for held in holders], 0).astype(bf16)
-        for i in range(2)
-    ]
-    d_small = jnp.concatenate([total([d_logit_parts[d, s] for d, s in held]) for held in holders], 0)
-    d_small_low = d_small.astype(bf16)
-    d_projected = jnp.concatenate([d_q.reshape(D, rows), d_kv[0], d_kv[1], d_gate_logit], 0)
-    grad_qkv = dot(h_first, d_projected[: 3 * D], 0, 1).astype(bf16)
-    grad_small = dot(h_first, d_small_low, 0, 1)
-    d_normed = dot(d_projected, w_attn, 0, 1) + dot(d_small_low, w_small, 0, 1)
-    d_inputs_norm, grad_gain_attn = norm_back_attn(d_normed)
-    d_inputs = d_resid + d_inputs_norm
-
-    grad_bias = jnp.sum(d_small.reshape(HEADS, 8, rows)[:, 0], axis=1)
     placed = jnp.zeros((HEADS, HDIM, 2), f32)
-    placed = lax.dynamic_update_slice(placed, d_gains, (head, 0, 0)).reshape(D, 2)
-    grad_qkv, early = lax.optimization_barrier((grad_qkv, early))
-    late, small = lax.psum((grad_qkv, (grad_small, grad_gain_ffn, grad_gain_attn, grad_bias, placed)), both)
-    grad_small, grad_gain_ffn, grad_gain_attn, grad_bias, placed = small
-    grad_w_heads = grad_small.reshape(D, HEADS, 8)[:, :, :3].transpose(0, 2, 1).reshape(D, 3 * HEADS)
+    placed = lax.dynamic_update_slice(placed, d_gains, (head, 0, 0)).reshape(D, 2).T
+    extra = jnp.concatenate([jnp.zeros((1, D), f32), grad_gain_ffn[None], placed, jnp.zeros((SMALL - 3 * HEADS - 4, D), f32)], 0)
+    late, d_inputs, small = last(
+        count, lax.axis_size("group"), h_first, d_q, d_kv_parts, d_logit_parts, d_gate_logit, w_attn, w_small,
+        tokens[0], gain_attn[None], d_resid, extra,
+    )
+    late = late[: 9 * (D // UNIT)].reshape(9, D, 256).transpose(1, 0, 2).reshape(D, 3 * D)
     grad_w_attn = jnp.concatenate([late, early[3]], 1).astype(f32)
+    row = 3 * HEADS
     return (
         output[None].astype(bf16),
         d_inputs[None],
-        grad_gain_attn,
+        small[row],
         grad_w_attn,
-        grad_w_heads,
-        grad_bias,
-        placed[:, 0],
-        placed[:, 1],
+        small[:row].reshape(HEADS, 3, D).transpose(2, 1, 0).reshape(D, row),
+        small[row + 4, :HEADS],
+        small[row + 2],
+        small[row + 3],
         early[2].astype(f32),
-        grad_gain_ffn,
+        small[row + 1],
         early[1].astype(f32),
         early[0].astype(f32),
     )

time: 793 us -> 549 us (0.69); the launches traced: 779 us -> 549 us
  waiting for transfers between devices: 241 us -> 18.6 us
  Pallas kernels: 272 us -> 402 us
  local copies, waits for them, and re-layouts: 94.7 us -> 33.2 us
  blocking collectives: 40 us -> 0 us
  other arithmetic: 48.2 us -> 25.4 us
  matrix products: 69.1 us -> 55.1 us
    psum x2 -> x0, waiting for transfers between devices: 209 us -> none  [local(): lax.psum((grad_qkv, (grad_small, grad_gain_ffn, grad_gain_attn, grad_bias...]
    pallas_call x0 -> x1, Pallas kernels: none -> 128 us  [last(): pl.pallas_call(functools.partial(last_kernel, count, sets), out_shape=[ja...]
    psum x1 -> x0, blocking collectives: 40 us -> none  [local(): lax.psum((grad_qkv, (grad_small, grad_gain_ffn, grad_gain_attn, grad_bias...]
    convert_element_type x19 -> x0, local copies, waits for them, and re-layouts: 30.9 us -> none  [the longest x17 25.6 us: local(): d_kv_parts[d, i, s].astype(f32)]
    unnamed x74 -> x55, local copies, waits for them, and re-layouts: 31.2 us -> 11.6 us
    unnamed x13 -> x1, other arithmetic: 15.3 us -> 0.01 us
    dot_general x17 -> x13, matrix products: 69.1 us -> 55.1 us  [dot(): lax.dot_general(a, b, (((i,), (j,)), ((), ())), preferred_element_type=f32)]
    psum x1, waiting for transfers between devices: 31.2 us -> 18.6 us  [local(): early = lax.psum((grad_w_down, grad_w_gate_up, grad_w_out, grad_gate), both)]
  transfers between devices with their start and end apart: 3 -> 1, of which waited for: 3 -> 1; matrix products, arithmetic and copies ran while one was open for 18% -> 4% of each run, Pallas kernels for 19% -> 51%
where the time goes in v2:
time: 549 us
  Pallas kernels  402 us (73%)
  matrix products  55.1 us (10%)
  local copies, waits for them, and re-layouts  33.2 us (6%)
  other arithmetic  25.4 us (5%)
  waiting for transfers between devices  18.6 us (3%)
  between operations  14.4 us (3%)
    pallas_call x1, Pallas kernels, last(): pl.pallas_call(functools.partial(last_kernel, count, sets), out_shape=[ja...  128 us
    pallas_call x1, Pallas kernels, heads_back(): pl.pallas_call(functools.partial(heads_back_kernel, count), out_shape=[ja...  68.7 us
    pallas_call x1, Pallas kernels, heads_out(): pl.pallas_call(functools.partial(heads_out_kernel, count), out_shape=[jax...  60.4 us
    dot_general x13, matrix products, dot(): lax.dot_general(a, b, (((i,), (j,)), ((), ())), preferred_element_type=f32)  55.1 us
    pallas_call x1, Pallas kernels, attend_backward(): pl.pallas_call(functools.partial(backward_kernel, count), grid_spec=pltpu...  52.3 us
    pallas_call x1, Pallas kernels, mixed_back(): pl.pallas_call(functools.partial(mixed_back_kernel, count), out_shape=jax...  34.4 us
    pallas_call x1, Pallas kernels, grads_out(): pl.pallas_call(functools.partial(grads_out_kernel, count), out_shape=jax....  30.8 us
    pallas_call x1, Pallas kernels, attend_forward(): pl.pallas_call(functools.partial(forward_kernel, count), grid_spec=pltpu....  27.7 us
  transfers between devices with their start and end apart: 1, of which 1 were waited for; matrix products, arithmetic and copies ran while one was open for 4% of the time, Pallas kernels for 51%

profile of v2, /device:TPU:0, one launch (start us, length us, event | category | flops | bytes accessed | tf_op | source)
XLA Modules:
  0.0 548.7 jit_solution(15134338780337916336)
XLA Ops:
  10.1 5.7 %fusion.3 = bf16[2304,512]{0,1:T(8,128)(2,1)} fusion(bf16[512,768]{1,0:T(8,128)(2,1)S(1)} %fusion.11.h_ref, bf16[768,3072]{1,0:T(8,128)(2,1)} %w_ref.1), kind=kOutput, calls=%fused_computation.10 | convolution fusion | flops 1813118976 | bytes 6684672 | tf_op jit(solution)/shard_map/dot_general | solution.py:594
  15.8 4.4 copy.70
  23.2 60.4 %heads_out.1 = (bf16[8,3,2,64,512]{4,3,2,1,0:T(8,128)(2,1)}, f32[8,2,8,512]{3,2,1,0:T(8,128)}) custom-call(bf16[3,12,64,512]{3,2,1,0:T(8,128)(2,1)} %bitcast.81, f32[12,8,512]{2,1,0:T(8,128)} %fusion.17.logit_in), custom_call_target="tpu_custom_call" | custom-call | tf_op jit(solution)/shard_map/heads_out/pallas_call | solution.py:458
  84.3 27.7 %attend_forward.1 = (bf16[2,8,64,512]{3,2,1,0:T(8,128)(2,1)}, f32[2,16,64,256]{3,2,1,0:T(8,128)}, bf16[2,17,128,256]{3,2,1,0:T(8,128)(2,1)}, bf16[2,16,256,128]{...) custom-call(s32[1]{0:T(128)} %bitcast.2.device_ref, s32[16,16]{1,0:T(8,128)} %bitcast.89, ...), custom_call_target="tpu_custom_call" | custom-call | tf_op jit(solution)/shard_map/attend_forward/pallas_call | solution.py:209
  112.0 34.4 %mixed_back.1 = bf16[12,64,512]{2,1,0:T(8,128)(2,1)} custom-call(bf16[2,8,64,512]{3,2,1,0:T(8,128)(2,1)} %get-tuple-element.31.x_ref), custom_call_target="tpu_custom_call" | custom-call | tf_op jit(solution)/shard_map/mixed_back/pallas_call | solution.py:496
  146.4 2.5 fusion.5
  150.0 6.2 %fusion.34 = f32[512,4096]{1,0:T(8,128)S(1)} fusion(bf16[768,4096]{1,0:T(8,128)(2,1)} %param.24, f32[512,768]{1,0:T(8,128)S(1)} %get-tuple-element.112, f32[768]{0:T(1024)S(1)} %copy-done.16, f32[512]{0:T(512)S(1)} %fusion.30), kind=kOutput, calls=%fused_computation.71 | convolution fusion | flops 3222405120 | bytes 16258048 | tf_op jit(solution)/shard_map/dot_general | solution.py:594
  156.2 7.1 %fusion.25 = (f32[512,2048]{1,0:T(8,128)}, f32[512,2048]{1,0:T(8,128)}, bf16[512,2048]{1,0:T(8,128)(2,1)S(1)}) fusion(f32[512,4096]{1,0:T(8,128)S(1)} %fusion.34, bf16[2048,768]{1,0:T(8,128)(2,1)} %param.25, bf16[1,512,768]{2,1,0:T(8,128)(2,1)S(1)} %copy-done.13), kind=kOutput, calls=%fused_computation.49 | convolution fusion | flops 1625292800 | bytes 22806528 | tf_op jit(solution)/shard_map/dot_general | solution.py:594
  163.4 7.3 %multiply_reduce_fusion = (f32[768]{0:T(1024)S(1)}, f32[512]{0:T(512)S(1)}, f32[512,768]{1,0:T(8,128)S(1)}) fusion(f32[512,768]{1,0:T(8,128)S(1)} %get-tuple-element.112, f32[512]{0:T(512)S(1)} %fusion.30, f32[768]{0:T(1024)S(1)} %copy-done.16, bf16[768,4096]{1,0:T(8,128)(2,1)S(1)} %bitcast.84, f32[512,2048]{1,0:T(8,128)} %get-tuple-element.105, ...), kind=kOutput, calls=%fused_computation.30 | convolution fusion | flops 3227777792 | bytes 17836032 | tf_op jit(solution)/shard_map/dot_general | solution.py:594
  170.7 9.8 %convolution_convert_fusion = bf16[768,4096]{1,0:T(8,128)(2,1)} fusion(f32[512,2048]{1,0:T(8,128)} %get-tuple-element.105, f32[512,2048]{1,0:T(8,128)} %get-tuple-element.104, f32[512,768]{1,0:T(8,128)S(1)} %get-tuple-element.112, f32[768]{0:T(1024)S(1)} %copy-done.16, f32[512]{0:T(512)S(1)} %fusion.30), kind=kOutput, calls=%fused_computation.1 | convolution fusion | flops 3229745152 | bytes 16258048 | tf_op jit(solution)/shard_map/dot_general | solution.py:594
  182.7 1.9 fusion.8
  186.5 3.5 convolution_convert_fusion.2
  190.6 30.8 %grads_out.1.dmixed_ref = bf16[8,2,64,512]{3,2,1,0:T(8,128)(2,1)} custom-call(bf16[12,64,512]{2,1,0:T(8,128)(2,1)} %bitcast.85), custom_call_target="tpu_custom_call" | custom-call | tf_op jit(solution)/shard_map/grads_out/pallas_call | solution.py:531
  222.3 52.3 %attend_backward.1 = (bf16[8,3,2,64,512]{4,3,2,1,0:T(8,128)(2,1)}, f32[8,2,8,512]{3,2,1,0:T(8,128)}, f32[2,64,2]{2,1,0:T(8,128)}) custom-call(s32[1]{0:T(128)} %bitcast.2.device_ref, s32[16,16]{1,0:T(8,128)} %bitcast.90, f32[2]{0:T(128)} %dynamic_slice.6.bias_ref, bf16[8,3,2,64,512]{4,3,2,1,0:T(8,128)(2,1)} %get-tuple-element.29.raw_ref, ...), custom_call_target="tpu_custom_call" | custom-call | tf_op jit(solution)/shard_map/attend_backward/pallas_call | solution.py:355
  275.8 68.7 %heads_back.1 = (bf16[12,64,512]{2,1,0:T(8,128)(2,1)}, bf16[8,2,2,64,512]{4,3,2,1,0:T(8,128)(2,1)}, f32[8,2,8,512]{3,2,1,0:T(8,128)}) custom-call(bf16[8,3,2,64,512]{4,3,2,1,0:T(8,128)(2,1)} %get-tuple-element.37.x_ref, f32[8,2,8,512]{3,2,1,0:T(8,128)} %get-tuple-element.38.logit_in), custom_call_target="tpu_custom_call" | custom-call | tf_op jit(solution)/shard_map/heads_back/pallas_call | solution.py:573
  345.2 127.6 %last.1 = (bf16[448,16,256]{2,1,0:T(8,128)(2,1)}, f32[512,768]{1,0:T(8,128)}, f32[48,768]{1,0:T(8,128)}) custom-call(bf16[512,768]{1,0:T(8,128)(2,1)} %copy-done.9, bf16[12,64,512]{2,1,0:T(8,128)(2,1)} %get-tuple-element.39.dq_ref, bf16[8,2,2,64,512]{4,3,2,1,0:T(8,128)(2,1)} %get-tuple-element.40.dkv_ref, f32[8,2,8,512]{3,2,1,0:T(8,128)} %get-tuple-element.41.dlogit_ref, ...), custom_call_target="tpu_custom_call" | custom-call | tf_op jit(solution)/shard_map/last/pallas_call | solution.py:799
  472.9 4.1 slice.38
  476.9 6.0 %copy.77 = bf16[9,768,256]{1,2,0:T(8,128)(2,1)} copy(bf16[9,768,256]{2,1,0:T(8,128)(2,1)} %bitcast.80) | data formatting | bytes 7077888 | tf_op jit(solution)/shard_map/reshape | solution.py:895
  484.8 5.3 fusion.14
  490.1 18.6 %all-reduce.6.cloned.1.call-done = (bf16[768,768]{1,0:T(8,128)(2,1)}, bf16[768,768]{1,0:T(8,128)(2,1)}, bf16[768,4096]{1,0:T(8,128)(2,1)}, bf16[2048,768]{1,0:T(8,128)(2,1)}) async-done(((bf16[768,768]{1,0:T(8,128)(2,1)}, bf16[768,768]{1,0:T(8,128)(2,1)}, bf16[768,4096]{1,0:T(8,128)(2,1)}, bf16[2048,768]{1,0:T(8,128)(2,1)}), (bf16[768,768]{1,0:T(8,128)(2,1)}, bf16[768,768]{1,0:T(8,128)(2,1)}, ...) | async-done | bytes 11796496 | tf_op jit(solution)/shard_map/psum | solution.py:882
  510.3 6.5 %maximum_convert_fusion = f32[768,3072]{0,1:T(8,128)} fusion(bf16[768,768]{0,1:T(8,128)(2,1)S(1)} %copy.78, bf16[768,2304]{0,1:T(8,128)(2,1)} %bitcast.79), kind=kLoop, calls=%fused_computation.3 | loop fusion | flops 9437184 | bytes 14155776 | tf_op jit(solution)/shard_map/convert_element_type | solution.py:896
  516.8 9.7 %copy.80 = f32[768,3072]{1,0:T(8,128)} copy(f32[768,3072]{0,1:T(8,128)} %maximum_convert_fusion) | data formatting | bytes 18874368
  528.0 9.5 %convert_element_type.105 = f32[768,4096]{1,0:T(8,128)} convert(bf16[768,4096]{1,0:T(8,128)(2,1)} %get-tuple-element.102) | non-fusion elementwise | flops 3145728 | bytes 18874368 | tf_op jit(solution)/shard_map/convert_element_type | solution.py:909
  537.5 3.2 convert_element_type.107
  (92 shorter events, 21.2 us)
Async XLA Ops:
  7.2 141.8 %copy-start = (bf16[768,768]{1,0:T(8,128)(2,1)S(1)}, bf16[768,768]{1,0:T(8,128)(2,1)}, u32[]{:S(2)}) copy-start(bf16[768,768]{1,0:T(8,128)(2,1)} %param.22) | copy-start | bytes 3538948
  7.2 501.5 %all-reduce.6.cloned.1.call-start = ((), (), s32[]{:S(2)}) async-start(), calls=%async_computation | async-start | bytes 23592960 | tf_op jit(solution)/shard_map/psum | solution.py:882
  10.1 136.3 %copy-start.9 = (bf16[512,768]{1,0:T(8,128)(2,1)}, bf16[512,768]{1,0:T(8,128)(2,1)S(1)}, u32[]{:S(2)}) copy-start(bf16[512,768]{1,0:T(8,128)(2,1)S(1)} %fusion.11.h_ref) | copy-start | bytes 2359300
  15.8 4.4 copy-start.18
  15.8 5.1 copy-start.3
  15.8 5.1 copy-start.19
  15.8 6.2 %copy-start.20 = (f32[768]{0:T(1024)S(1)}, f32[768]{0:T(1024)}, u32[]{:S(2)}) copy-start(f32[768]{0:T(1024)} %param.20) | copy-start | bytes 9220
  20.2 2.1 copy-start.21
  20.2 2.4 copy-start.22
  149.9 30.5 %copy-start.4 = (f32[512,768]{1,0:T(8,128)}, f32[512,768]{1,0:T(8,128)S(1)}, u32[]{:S(2)}) copy-start(f32[512,768]{1,0:T(8,128)S(1)} %get-tuple-element.112) | copy-start | bytes 4718596
  149.9 6.3 %copy-start.13 = (bf16[1,512,768]{2,1,0:T(8,128)(2,1)S(1)}, bf16[1,512,768]{2,1,0:T(8,128)(2,1)}, u32[]{:S(2)}) copy-start(bf16[1,512,768]{2,1,0:T(8,128)(2,1)} %param.14) | copy-start | bytes 2359300
  150.0 13.4 %slice-start = ((s8[6291456]{0:T(1024)(128)(4,1)}), s8[4194304]{0:T(1024)(128)(4,1)S(1)}, s32[]{:S(2)}) async-start(s8[6291456]{0:T(1024)(128)(4,1)} %bitcast.83), calls=%async_computation.1 | async-start | bytes 8388608
  156.2 7.2 %slice-start.1 = ((s8[6291456]{0:T(1024)(128)(4,1)}), s8[2097152]{0:T(1024)(128)(4,1)S(1)}, s32[]{:S(2)}) async-start(s8[6291456]{0:T(1024)(128)(4,1)} %bitcast.83), calls=%async_computation.2 | async-start | bytes 4194304
  163.4 23.2 %copy-start.23 = (bf16[512,2048]{1,0:T(8,128)(2,1)}, bf16[512,2048]{1,0:T(8,128)(2,1)S(1)}, u32[]{:S(2)}) copy-start(bf16[512,2048]{1,0:T(8,128)(2,1)S(1)} %get-tuple-element.106) | copy-start | bytes 6291460
  180.9 3.8 copy-start.2
  182.7 1.9 copy-start.10
  184.6 5.4 copy-start.8
  190.0 31.4 %copy-start.15 = (bf16[768,12,3]{0,2,1:T(4,128)(2,1)S(1)}, bf16[768,12,3]{0,2,1:T(4,128)(2,1)}, u32[]{:S(2)}) copy-start(bf16[768,12,3]{0,2,1:T(4,128)(2,1)} %copy-done.14) | copy-start | bytes 165892
  476.9 6.0 %copy-start.17 = (f32[48,768]{1,0:T(8,128)S(1)}, f32[48,768]{1,0:T(8,128)}, u32[]{:S(2)}) copy-start(f32[48,768]{1,0:T(8,128)} %get-tuple-element.44) | copy-start | bytes 442372
  476.9 7.9 %copy-start.5 = (f32[512,768]{1,0:T(8,128)S(1)}, f32[512,768]{1,0:T(8,128)}, u32[]{:S(2)}) copy-start(f32[512,768]{1,0:T(8,128)} %copy-done.4) | copy-start | bytes 4718596
  516.7 9.7 %copy-start.12 = (bf16[768,768]{1,0:T(8,128)(2,1)S(1)}, bf16[768,768]{1,0:T(8,128)(2,1)}, u32[]{:S(2)}) copy-start(bf16[768,768]{1,0:T(8,128)(2,1)} %get-tuple-element.101) | copy-start | bytes 3538948
  528.0 9.5 %copy-start.7 = (bf16[2048,768]{1,0:T(8,128)(2,1)S(1)}, bf16[2048,768]{1,0:T(8,128)(2,1)}, u32[]{:S(2)}) copy-start(bf16[2048,768]{1,0:T(8,128)(2,1)} %get-tuple-element.103) | copy-start | bytes 9437188
  537.5 3.2 copy-start.11
  537.5 4.3 copy-start.1
  (3 other events, 3.4 us)
Sparse Core Ops, SparseCore 0:
  190.2 318.4 all-reduce.5

commit v3 on v2

--- a/solution.py
+++ b/solution.py
@@ -504,7 +504,11 @@
     )(mixed)
 
 
-def grads_out_kernel(count, x_ref, o_ref, send, recv, local):
+TN = (((0,), (0,)), ((), ()))
+
+
+def grads_out_kernel(count, x_ref, h1_ref, dgate_ref, h2_ref, dgu_ref, hidden_ref, dlow_ref, gated_ref, branch_ref,
+                     o_ref, grads_ref, send, recv, local):
     me = greet(count)
     started = []
     for head in range(HEADS):
@@ -517,6 +521,35 @@
         pl.when(away)(copy.start)
         pl.when(peer == me)(own.start)
         started.append((away, peer == me, copy, own))
+
+    def put(unit, part):
+        grads_ref[pl.ds(unit, 16)] = part.astype(bf16).reshape(16, UNIT, 256)
+
+    def gate_up(i, carried):
+        right = dgu_ref[:, pl.ds(pl.multiple_of(i * 256, 256), 256)]
+        for j in range(3):
+            put(i * 48 + 16 * j, mm(h2_ref[:, 256 * j : 256 * j + 256], right, TN))
+        return carried
+
+    lax.fori_loop(0, 2 * FF // 256, gate_up, 0)
+
+    def down(i, carried):
+        left = hidden_ref[:, pl.ds(pl.multiple_of(i * 256, 256), 256)]
+        for j in range(3):
+            put(768 + 128 * j + 16 * i, mm(left, dlow_ref[:, 256 * j : 256 * j + 256], TN))
+        return carried
+
+    lax.fori_loop(0, FF // 256, down, 0)
+    for i in range(3):
+        for j in range(3):
+            put(1152 + 48 * i + 16 * j, mm(gated_ref[256 * j : 256 * j + 256, :], branch_ref[:, 256 * i : 256 * i + 256]))
+            put(1296 + 48 * i + 16 * j, lax.dot_general(
+                h1_ref[:, 256 * j : 256 * j + 256], dgate_ref[256 * i : 256 * i + 256, :],
+                (((0,), (1,)), ((), ())), preferred_element_type=f32))
+    units = grads_ref.shape[0]
+    if units > 1440:
+        grads_ref[1440:] = jnp.zeros((units - 1440, UNIT, 256), bf16)
+
     for away, here, copy, own in started:
         pl.when(away)(copy.wait_send)
         pl.when(here)(own.wait)
@@ -527,67 +560,20 @@
             pl.when(is_mine(me, slot, source, count))(copy.wait_recv)
 
 
-def grads_out(d_mixed, count):
+def grads_out(count, units, d_mixed, *operands):
+    vmem = pl.BlockSpec(memory_space=pltpu.VMEM)
     return pl.pallas_call(
         functools.partial(grads_out_kernel, count),
-        out_shape=jax.ShapeDtypeStruct((count, 2, HDIM, 2 * BLK), bf16),
-        in_specs=[ANY],
-        out_specs=ANY,
+        out_shape=[
+            jax.ShapeDtypeStruct((count, 2, HDIM, 2 * BLK), bf16),
+            jax.ShapeDtypeStruct((units, UNIT, 256), bf16),
+        ],
+        in_specs=[ANY] + [vmem] * 8,
+        out_specs=[ANY, vmem],
         scratch_shapes=[pltpu.SemaphoreType.DMA((HEADS,)), pltpu.SemaphoreType.DMA((count, 2)), pltpu.SemaphoreType.DMA((2,))],
-        compiler_params=pltpu.CompilerParams(collective_id=2, has_side_effects=True),
+        compiler_params=pltpu.CompilerParams(collective_id=2, has_side_effects=True, vmem_limit_bytes=60 * 2**20),
         name="grads_out",
-    )(d_mixed)
-
-
-def heads_back_kernel(count, x_ref, logit_in, q_ref, kv_ref, logit_ref, send, recv, recv_q, local):
-    me = greet(count)
-    first = first_head(me, count)
-    started = []
-    for k in far_first(count) + [0]:
-        peer = lax.rem(me + k, count)
-        pairs = [
-            (None, x_ref.at[peer, pl.ds(1, 2)], kv_ref.at[me], recv.at[k, 0]),
-            (None, logit_in.at[peer], logit_ref.at[me], recv.at[k, 1]),
-        ]
-        for slot in range(2):
-            pairs.append((is_mine(me, slot, peer, count), x_ref.at[peer, 0, slot], q_ref.at[first + slot], recv_q.at[first + slot]))
-        for i, (mine, src, dst, sem) in enumerate(pairs):
-            copy = push(src, dst, send.at[k, i], sem, peer) if k else pltpu.make_async_copy(src, dst, local.at[i])
-            started.append((mine, k, copy))
-            if mine is None:
-                copy.start()
-            else:
-                pl.when(mine)(copy.start)
-    for mine, k, copy in started:
-        if mine is not None:
-            pl.when(mine)(copy.wait_send if k else copy.wait)
-        else:
-            copy.wait()
-    for head in range(HEADS):
-        source = holder(head, me, count)
-        copy = push(x_ref.at[0, 0, 0], q_ref.at[head], send.at[0, 0], recv_q.at[head], lax.rem(me + 1, count))
-        pl.when(source != me)(copy.wait_recv)
-
-
-def heads_back(d_raw, d_logits, count):
-    return pl.pallas_call(
-        functools.partial(heads_back_kernel, count),
-        out_shape=[
-            jax.ShapeDtypeStruct((HEADS, HDIM, 2 * BLK), bf16),
-            jax.ShapeDtypeStruct((count, 2, 2, HDIM, 2 * BLK), bf16),
-            jax.ShapeDtypeStruct((count, 2, 8, 2 * BLK), f32),
-        ],
-        in_specs=[ANY, ANY],
-        out_specs=[ANY, ANY, ANY],
-        scratch_shapes=[
-            pltpu.SemaphoreType.DMA((count, 4)),
-            pltpu.SemaphoreType.DMA((count, 2)),
-            pltpu.SemaphoreType.DMA((HEADS,)),
-            pltpu.SemaphoreType.DMA((4,)),
-        ],
-        compiler_params=pltpu.CompilerParams(collective_id=3, has_side_effects=True),
-        name="heads_back",
-    )(d_raw, d_logits)
+    )(d_mixed, *operands)
 
 
 def dot(a, b, i, j):
@@ -611,31 +597,52 @@
     return {axis: here + step - 2 * step * side}, side
 
 
-def greet_all(bits):
+def greet_all(bits, count):
+    me = lax.axis_index("seq")
+    others = [partner(bit)[0] for bit in bits if bit[0] != "seq"]
+    others += [{"seq": lax.rem(me + k, count)} for k in range(1, count)]
     barrier = pltpu.get_barrier_semaphore()
-    for bit in bits:
-        there, _ = partner(bit)
+    for there in others:
         pl.semaphore_signal(barrier, inc=1, device_id=there, device_id_type=MESH)
-    pl.semaphore_wait(barrier, len(bits))
+    pl.semaphore_wait(barrier, len(others))
+    return me
 
 
 def orders(near, far, seq):
-    rest = [far] + seq
-    return [[near] + rest[i:] + rest[:i] for i in range(3)]
+    x, others = seq[0], seq[1:]
+    z = others[0]
+    rest = others[1:]
+    return [
+        [near, far, x, z] + rest,
+        [near, x, far, z] + rest,
+        [near, z, x, far] + rest,
+        [near, far, z, x] + rest,
+        [near, x, z] + rest + [far],
+        [near, z, far] + rest + [x],
+    ]
+
+
+PARTS = 6
 
 
 class Summing:
-    def __init__(self, base, size, order, own, landing, result, send, recv):
-        self.start, self.size, self.order = base, size, order
+    def __init__(self, base, size, order, source, own, landing, result, send, recv, local):
+        self.start, self.size, self.order, self.source, self.local = base, size, order, source, local
         self.own, self.landing, self.result, self.send, self.recv = own, landing, result, send, recv
-        self.base, self.at, self.stage, self.copy = base, base, 0, None
+        self.at, self.stage, self.copy, self.load = base, 0, None, None
 
     def give(self):
         there, side = partner(self.order[self.stage])
         half = self.size // 2
         self.keep = self.start + side * half
+        held = self.own
+        if self.stage == 0 and self.source is not None:
+            held = self.source
+            mine = pl.ds(self.keep, half)
+            self.load = pltpu.make_async_copy(self.source.at[mine], self.own.at[mine], self.local)
+            self.load.start()
         self.copy = pltpu.make_async_remote_copy(
-            src_ref=self.own.at[pl.ds(self.start + (1 - side) * half, half)],
+            src_ref=held.at[pl.ds(self.start + (1 - side) * half, half)],
             dst_ref=self.landing.at[pl.ds(self.at, half)],
             send_sem=self.send.at[self.stage], recv_sem=self.recv.at[self.stage],
             device_id=there, device_id_type=MESH,
@@ -644,6 +651,9 @@
 
     def add(self):
         self.copy.wait()
+        if self.load is not None:
+            self.load.wait()
+            self.load = None
         half = self.size // 2
         step = PIECE if half % PIECE == 0 else 1
         keep, at, own, landing = self.keep, self.at, self.own, self.landing
@@ -657,9 +667,9 @@
         lax.fori_loop(0, half // step, piece, 0)
         self.start, self.size, self.at, self.stage = keep, half, at + half, self.stage + 1
 
-    def settle(self, sem):
+    def settle(self):
         copy = pltpu.make_async_copy(
-            self.own.at[pl.ds(self.start, self.size)], self.result.at[pl.ds(self.start, self.size)], sem
+            self.own.at[pl.ds(self.start, self.size)], self.result.at[pl.ds(self.start, self.size)], self.local
         )
         copy.start()
         copy.wait()
@@ -693,51 +703,104 @@
     ]
 
 
-def part_sizes(units, least):
-    pieces = units // least
-    return [least * ((pieces + 2 - i) // 3) for i in range(3)]
-
-
-def last_kernel(count, sets, h_ref, dq_ref, dkv_ref, dlogit_ref, dgate_ref, w_ref, wsmall_ref, x_ref, gain_ref,
-                dresid_ref, extra_ref, grads_ref, dx_ref, small_ref,
-                proj_ref, ht_ref, dsmall_ref, rows_ref, dn_ref, g_ref, land_ref, small_land, send, recv, ssend, srecv, local):
+def padded(units, least):
+    return -(-units // least) * least
+
+
+def sums_of(units, least, sets, source, own, landing, result, send, recv, local):
+    pieces, base, sums = units // least, 0, []
+    for i, order in enumerate(orders(*sets)):
+        size = least * ((pieces + PARTS - 1 - i) // PARTS)
+        if not size:
+            break
+        sums.append(Summing(base, size, order, source, own, landing, result, send.at[i], recv.at[i], local.at[i]))
+        base += size
+    return sums
+
+
+def step(sums, stages):
+    for part in sums:
+        if part.stage < stages:
+            part.add()
+            if part.stage < stages:
+                part.give()
+            else:
+                part.settle()
+                part.spread()
+        else:
+            part.gathered()
+            if part.left > 0:
+                part.spread()
+
+
+def last_kernel(count, sets, draw_ref, dlogit_ref, early_ref, h_ref, dgate_ref, w_ref, wsmall_ref, x_ref, gain_ref,
+                dresid_ref, extra_ref, late_out, early_out, dx_ref,
+                proj_ref, logit_ref, part_ref, dsmall_ref, rows_ref, dn_ref, g_ref, land_ref, e_ref, eland_ref,
+                send, recv, recv_q, recv_kv, local, gsend, grecv, gsem, esend, erecv, esem):
     near, far, seq = sets
     bits = [near, far] + seq
-    greet_all(bits)
+    stages, least = len(bits), 1 << len(bits)
+    me = greet_all(bits, count)
     rows = h_ref.shape[0]
+    early = sums_of(e_ref.shape[0], least, sets, early_ref, e_ref, eland_ref, early_out, esend, erecv, esem)
+    for part in early:
+        part.give()
+
     holders = held_heads(count)
-    proj_ref[0:D] = dq_ref[...].reshape(D, rows)
+    first = first_head(me, count)
+    started = []
+    for k in far_first(count) + [0]:
+        peer = lax.rem(me + k, count)
+        pairs = [(None, dlogit_ref.at[peer], logit_ref.at[me], recv.at[k])]
+        for slot in range(2):
+            head = first + slot
+            target = proj_ref.at[pl.ds(pl.multiple_of(head * HDIM, HDIM), HDIM)]
+            pairs.append((is_mine(me, slot, peer, count), draw_ref.at[peer, 0, slot], target, recv_q.at[head]))
+            used = (head * count < HEADS * (me + 1)) & (head * count + count > HEADS * me)
+            order = me - holder(head, 0, count)
+            pairs.append((used, draw_ref.at[peer, pl.ds(1, 2), slot], part_ref.at[head, order], recv_kv.at[head, order]))
+        for i, (mine, src, dst, sem) in enumerate(pairs):
+            copy = push(src, dst, send.at[k, i], sem, peer) if k else pltpu.make_async_copy(src, dst, local.at[i])
+            started.append((mine, k, copy))
+            if mine is None:
+                copy.start()
+            else:
+                pl.when(mine)(copy.start)
+
+    step(early, stages)
+    step(early, stages)
+
+    for mine, k, copy in started:
+        if mine is not None:
+            pl.when(mine)(copy.wait_send if k else copy.wait)
+        else:
+            copy.wait()
+    for head in range(HEADS):
+        source = holder(head, me, count)
+        copy = push(draw_ref.at[0, 0, 0], proj_ref.at[pl.ds(head * HDIM, HDIM)], send.at[0, 0], recv_q.at[head], lax.rem(me + 1, count))
+        pl.when(source != me)(copy.wait_recv)
+        for j, (d, s) in enumerate(holders[head]):
+            copy = push(draw_ref.at[0, pl.ds(1, 2), 0], part_ref.at[head, j], send.at[0, 0], recv_kv.at[head, j], lax.rem(me + 1, count))
+            pl.when(me != d)(copy.wait_recv)
+
     for head, held in enumerate(holders):
         for i in range(2):
             start = D * (1 + i) + head * HDIM
             if len(held) == 1:
-                d, s = held[0]
-                proj_ref[start : start + HDIM] = dkv_ref[d, i, s]
+                proj_ref[start : start + HDIM] = part_ref[head, 0, i]
             else:
-                proj_ref[start : start + HDIM] = total([dkv_ref[d, i, s].astype(f32) for d, s in held]).astype(bf16)
-        dsmall_ref[8 * head : 8 * head + 8] = total([dlogit_ref[d, s] for d, s in held])
+                proj_ref[start : start + HDIM] = total([part_ref[head, j, i].astype(f32) for j in range(len(held))]).astype(bf16)
+        dsmall_ref[8 * head : 8 * head + 8] = total([logit_ref[d, s] for d, s in held])
     proj_ref[3 * D :] = dgate_ref[...]
-    for i in range(3):
-        cols = slice(256 * i, 256 * i + 256)
-        ht_ref[cols, :] = h_ref[:, cols].astype(f32).T.astype(bf16)
 
     def block(i, carried):
-        part = mm(ht_ref[...], proj_ref[pl.ds(pl.multiple_of(i * 256, 256), 256)], NT).astype(bf16)
-        g_ref[pl.ds(i * (D // UNIT), D // UNIT)] = part.reshape(D // UNIT, UNIT, 256)
+        grads = proj_ref[pl.ds(pl.multiple_of(i * 256, 256), 256)]
+        for j in range(3):
+            part = lax.dot_general(h_ref[:, 256 * j : 256 * j + 256], grads, (((0,), (1,)), ((), ())), preferred_element_type=f32)
+            g_ref[pl.ds(i * (D // UNIT) + j * 16, 16)] = part.astype(bf16).reshape(16, UNIT, 256)
         return carried
 
     lax.fori_loop(0, 9, block, 0)
-    used = 9 * (D // UNIT)
-    units = g_ref.shape[0]
-    g_ref[used:] = jnp.zeros((units - used, UNIT, 256), bf16)
-
-    sums, base = [], 0
-    for i, size in enumerate(part_sizes(units, 1 << len(bits))):
-        sums.append(Summing(base, size, orders(near, far, seq)[i], g_ref, land_ref, grads_ref, send.at[i], recv.at[i]))
-        base += size
-    for part in sums:
-        part.give()
-
     low_small = dsmall_ref[...].astype(bf16)
     for i in range(3):
         cols = slice(256 * i, 256 * i + 256)
@@ -763,62 +826,89 @@
     row = lax.broadcasted_iota(jnp.int32, (HEADS, 128), 0)
     rows_ref[3 * HEADS + 4 : 3 * HEADS + 5, 0:128] = jnp.sum(jnp.where(lane == row, bias_sum, 0.0), 0, keepdims=True)
 
-    for stage, bit in enumerate(bits):
-        there, _ = partner(bit)
-        swap = pltpu.make_async_remote_copy(
-            src_ref=rows_ref, dst_ref=small_land.at[stage], send_sem=ssend.at[stage], recv_sem=srecv.at[stage],
-            device_id=there, device_id_type=MESH,
-        )
-        swap.start()
-        for part in sums:
-            part.add()
-            if stage + 1 < len(bits):
-                part.give()
-            else:
-                part.settle(local)
-                part.spread()
-        swap.wait()
-        rows_ref[...] += small_land[stage]
-    for stage in range(len(bits)):
-        for part in sums:
-            part.gathered()
-            if stage + 1 < len(bits):
-                part.spread()
-    small_ref[...] = rows_ref[...]
-
-
-def last(count, groups, h, d_q, d_kv, d_logits, d_gate, w_attn, w_small, x, gain, d_resid, extra):
-    bits = group_bits(groups, count)
-    sets = (bits[0][0], bits[0][1], bits[1])
-    stages = len(bits[0]) + len(bits[1])
-    least = 1 << stages
-    units = -(-9 * (D // UNIT) // least) * least
+    used = 9 * (D // UNIT)
+    units = g_ref.shape[0]
+    for i in range(3):
+        g_ref[used + 3 * i : used + 3 * i + 3] = rows_ref[:, 256 * i : 256 * i + 256].astype(bf16).reshape(3, UNIT, 256)
+    if units > used + 9:
+        g_ref[used + 9 :] = jnp.zeros((units - used - 9, UNIT, 256), bf16)
+    late = sums_of(units, least, sets, None, g_ref, land_ref, late_out, gsend, grecv, gsem)
+    for part in late:
+        part.give()
+    step(early, stages)
+    early_left = 2 * stages - 3
+    for stage in range(2 * stages):
+        step(late, stages)
+        if stage < early_left:
+            step(early, stages)
+
+
+def last(count, sets, d_raw, d_logits, early, h, d_gate, w_attn, w_small, x, gain, d_resid, extra):
+    stages = 2 + len(sets[2])
+    units = padded(9 * (D // UNIT) + 9, 1 << stages)
     rows = h.shape[0]
+    most = max(len(held) for held in held_heads(count))
     vmem = pl.BlockSpec(memory_space=pltpu.VMEM)
     dma = pltpu.SemaphoreType.DMA
+    shape = (UNIT, 256)
     return pl.pallas_call(
         functools.partial(last_kernel, count, sets),
         out_shape=[
-            jax.ShapeDtypeStruct((units, UNIT, 256), bf16),
+            jax.ShapeDtypeStruct((units,) + shape, bf16),
+            jax.ShapeDtypeStruct(early.shape, bf16),
             jax.ShapeDtypeStruct((rows, D), f32),
-            jax.ShapeDtypeStruct((SMALL, D), f32),
         ],
-        in_specs=[vmem] * 11,
-        out_specs=[ANY, vmem, vmem],
+        in_specs=[ANY] * 3 + [vmem] * 8,
+        out_specs=[ANY, ANY, vmem],
         scratch_shapes=[
             pltpu.VMEM((4 * D, rows), bf16),
-            pltpu.VMEM((D, rows), bf16),
+            pltpu.VMEM((count, 2, 8, rows), f32),
+            pltpu.VMEM((HEADS, most, 2, HDIM, rows), bf16),
             pltpu.VMEM((8 * HEADS, rows), f32),
             pltpu.VMEM((SMALL, D), f32),
             pltpu.VMEM((rows, D), f32),
-            pltpu.VMEM((units, UNIT, 256), bf16),
-            pltpu.VMEM((units, UNIT, 256), bf16),
-            pltpu.VMEM((stages, SMALL, D), f32),
-            dma((3, 2 * stages)), dma((3, 2 * stages)), dma((stages,)), dma((stages,)), dma,
+            pltpu.VMEM((units,) + shape, bf16),
+            pltpu.VMEM((units,) + shape, bf16),
+            pltpu.VMEM(early.shape, bf16),
+            pltpu.VMEM(early.shape, bf16),
+            dma((count, 5)), dma((count,)), dma((HEADS,)), dma((HEADS, most)), dma((5,)),
+            dma((PARTS, 2 * stages)), dma((PARTS, 2 * stages)), dma((PARTS,)),
+            dma((PARTS, 2 * stages)), dma((PARTS, 2 * stages)), dma((PARTS,)),
         ],
-        compiler_params=pltpu.CompilerParams(collective_id=4, has_side_effects=True, vmem_limit_bytes=62 * 2**20),
+        compiler_params=pltpu.CompilerParams(collective_id=3, has_side_effects=True, vmem_limit_bytes=62 * 2**20),
         name="last",
-    )(h, d_q, d_kv, d_logits, d_gate, w_attn, w_small, x, gain, d_resid, extra)
+    )(d_raw, d_logits, early, h, d_gate, w_attn, w_small, x, gain, d_resid, extra)
+
+
+def unpack_kernel(parts, *refs):
+    o_ref = refs[-1]
+    at = 0
+    for ref, blocks in zip(refs, parts):
+        here = (pl.program_id(0) >= at) & (pl.program_id(0) < at + blocks)
+
+        @pl.when(here)
+        def _():
+            o_ref[...] = ref[...].reshape(o_ref.shape).astype(f32)
+
+        at += blocks
+
+
+def unpack(rows, *parts):
+    size = rows // UNIT
+    specs, at = [], 0
+    for _, first, blocks in parts:
+        index = lambda i, at=at, first=first, blocks=blocks: (first + jnp.clip(i - at, 0, blocks - 1), 0, 0)
+        specs.append(pl.BlockSpec((size, UNIT, 256), index))
+        at += blocks
+    return pl.pallas_call(
+        functools.partial(unpack_kernel, [blocks for _, _, blocks in parts]),
+        grid=(at,),
+        in_specs=specs,
+        out_specs=pl.BlockSpec((rows, 256), lambda i: (0, i)),
+        out_shape=jax.ShapeDtypeStruct((rows, 256 * at), f32),
+        compiler_params=pltpu.CompilerParams(vmem_limit_bytes=32 * 2**20),
+        name="unpack",
+    )(*[units for units, _, _ in parts])
 
 
 def rms_scale(values, gains):
@@ -875,39 +965,36 @@
     d_gate_logit = (d_gated * attended * gate_open * (1.0 - gate_open)).astype(bf16)
     d_mixed = (d_gated * gate_open).astype(bf16).reshape(HEADS, HDIM, rows)
 
-    grad_w_down = dot(hidden_low, d_low, 0, 0).astype(bf16)
-    grad_w_gate_up = dot(h_second, d_gate_low, 0, 0).astype(bf16)
-    grad_w_out = dot(gated, d_branch, 1, 0).astype(bf16)
-    grad_gate = dot(h_first, d_gate_logit, 0, 1).astype(bf16)
-    early = lax.psum((grad_w_down, grad_w_gate_up, grad_w_out, grad_gate), both)
-
-    d_mixed_all = grads_out(d_mixed, count)
+    near_far, seq_bits = group_bits(lax.axis_size("group"), count)
+    sets = (near_far[0], near_far[1], seq_bits)
+    units = padded(1440, 1 << (2 + len(seq_bits)))
+    d_mixed_all, early = grads_out(
+        count, units, d_mixed, h_first, d_gate_logit, h_second, d_gate_low, hidden_low, d_low, gated, d_branch
+    )
     d_raw, d_logits, d_gains = attend_backward(device, skip, bias, raw, logits, gains, d_mixed_all, mixed, q, k, kt, vt)
-    d_q, d_kv_parts, d_logit_parts = heads_back(d_raw, d_logits, count)
 
     placed = jnp.zeros((HEADS, HDIM, 2), f32)
     placed = lax.dynamic_update_slice(placed, d_gains, (head, 0, 0)).reshape(D, 2).T
     extra = jnp.concatenate([jnp.zeros((1, D), f32), grad_gain_ffn[None], placed, jnp.zeros((SMALL - 3 * HEADS - 4, D), f32)], 0)
-    late, d_inputs, small = last(
-        count, lax.axis_size("group"), h_first, d_q, d_kv_parts, d_logit_parts, d_gate_logit, w_attn, w_small,
-        tokens[0], gain_attn[None], d_resid, extra,
+    late, early, d_inputs = last(
+        count, sets, d_raw, d_logits, early, h_first, d_gate_logit, w_attn, w_small, tokens[0], gain_attn[None], d_resid, extra
     )
-    late = late[: 9 * (D // UNIT)].reshape(9, D, 256).transpose(1, 0, 2).reshape(D, 3 * D)
-    grad_w_attn = jnp.concatenate([late, early[3]], 1).astype(f32)
     row = 3 * HEADS
+    used = 9 * (D // UNIT)
+    small = late[used : used + 9].reshape(3, SMALL, 256).transpose(1, 0, 2).reshape(SMALL, D).astype(f32)
     return (
         output[None].astype(bf16),
         d_inputs[None],
         small[row],
-        grad_w_attn,
+        unpack(D, (late, 0, 9), (early, 27, 3)),
         small[:row].reshape(HEADS, 3, D).transpose(2, 1, 0).reshape(D, row),
         small[row + 4, :HEADS],
         small[row + 2],
         small[row + 3],
-        early[2].astype(f32),
+        unpack(D, (early, 24, 3)),
         small[row + 1],
-        early[1].astype(f32),
-        early[0].astype(f32),
+        unpack(D, (early, 0, 16)),
+        unpack(FF, (early, 6, 3)),
     )
 
 

time: 549 us -> 496 us (0.903)
  Pallas kernels: 402 us -> 422 us
  matrix products: 55.1 us -> 35.3 us
  waiting for transfers between devices: 18.6 us -> 0 us
  other arithmetic: 25.4 us -> 8.96 us
  between operations: 14.4 us -> 1.02 us
  local copies, waits for them, and re-layouts: 33.2 us -> 26.6 us
    pallas_call x1, Pallas kernels: 128 us -> 199 us  [last(): pl.pallas_call(functools.partial(last_kernel, count, sets), out_shape=[ja...]
    pallas_call x2 -> x5, Pallas kernels: 99.5 us -> 48.3 us  [the longest x1 30 us: grads_out(): pl.pallas_call(functools.partial(grads_out_kernel, count), out_shape=[jax...]
    dot_general x13 -> x9, matrix products: 55.1 us -> 35.3 us  [dot(): lax.dot_general(a, b, (((i,), (j,)), ((), ())), preferred_element_type=f32)]
    psum x1 -> x0, waiting for transfers between devices: 18.6 us -> none  [local(): early = lax.psum((grad_w_down, grad_w_gate_up, grad_w_out, grad_gate), both)]
    convert_element_type x4, other arithmetic: 20.7 us -> 5.9 us  [the longest x1 4.08 us: local(): d_gate_low = d_gate_up.astype(bf16)]
    reshape x1 -> x0, local copies, waits for them, and re-layouts: 5.99 us -> none  [local(): late[:9 * (D // UNIT)].reshape(9, D, 256).transpose(1, 0, 2)]
    unnamed x55 -> x47, local copies, waits for them, and re-layouts: 11.6 us -> 11.6 us
  transfers between devices with their start and end apart: 1 -> 0, of which waited for: 1 -> 0; matrix products, arithmetic and copies ran while one was open for 4% -> 0% of each run, Pallas kernels for 51% -> 0%
where the time goes in v3:
time: 496 us; the launch traced here: 494 us
  Pallas kernels  422 us (85%)
  matrix products  35.3 us (7%)
  local copies, waits for them, and re-layouts  26.6 us (5%)
  other arithmetic  8.96 us (2%)
    pallas_call x1, Pallas kernels, last(): pl.pallas_call(functools.partial(last_kernel, count, sets), out_shape=[ja...  199 us
    pallas_call x1, Pallas kernels, heads_out(): pl.pallas_call(functools.partial(heads_out_kernel, count), out_shape=[jax...  60.4 us
    pallas_call x1, Pallas kernels, attend_backward(): pl.pallas_call(functools.partial(backward_kernel, count), grid_spec=pltpu...  52.2 us
    dot_general x9, matrix products, dot(): lax.dot_general(a, b, (((i,), (j,)), ((), ())), preferred_element_type=f32)  35.3 us
    pallas_call x1, Pallas kernels, mixed_back(): pl.pallas_call(functools.partial(mixed_back_kernel, count), out_shape=jax...  33.8 us
    pallas_call x1, Pallas kernels, grads_out(): pl.pallas_call(functools.partial(grads_out_kernel, count), out_shape=[jax...  30 us
    pallas_call x1, Pallas kernels, attend_forward(): pl.pallas_call(functools.partial(forward_kernel, count), grid_spec=pltpu....  28.3 us
    pallas_call x4, Pallas kernels, unpack(): pl.pallas_call(functools.partial(unpack_kernel, [blocks for _, _, blocks...  18.3 us

profile of v3, /device:TPU:0, one launch (start us, length us, event | category | flops | bytes accessed | tf_op | source)
XLA Modules:
  0.0 494.1 jit_solution(2861009009112283212)
XLA Ops:
  2.2 1.4 fusion.9
  9.3 5.7 %fusion.3 = bf16[2304,512]{0,1:T(8,128)(2,1)} fusion(bf16[512,768]{1,0:T(8,128)(2,1)S(1)} %fusion.11.h1_ref.h_ref, bf16[768,3072]{1,0:T(8,128)(2,1)} %w_ref.1), kind=kOutput, calls=%fused_computation.8 | convolution fusion | flops 1813118976 | bytes 6684672 | tf_op jit(solution)/shard_map/dot_general | solution.py:580
  15.0 4.3 copy.62
  19.2 60.4 %heads_out.1 = (bf16[8,3,2,64,512]{4,3,2,1,0:T(8,128)(2,1)}, f32[8,2,8,512]{3,2,1,0:T(8,128)}) custom-call(bf16[3,12,64,512]{3,2,1,0:T(8,128)(2,1)} %bitcast.81, f32[12,8,512]{2,1,0:T(8,128)} %fusion.17.logit_in), custom_call_target="tpu_custom_call" | custom-call | tf_op jit(solution)/shard_map/heads_out/pallas_call | solution.py:458
  79.6 28.3 %attend_forward.1 = (bf16[2,8,64,512]{3,2,1,0:T(8,128)(2,1)}, f32[2,16,64,256]{3,2,1,0:T(8,128)}, bf16[2,17,128,256]{3,2,1,0:T(8,128)(2,1)}, bf16[2,16,256,128]{...) custom-call(s32[1]{0:T(128)} %bitcast.2.device_ref, s32[16,16]{1,0:T(8,128)} %bitcast.95, ...), custom_call_target="tpu_custom_call" | custom-call | tf_op jit(solution)/shard_map/attend_forward/pallas_call | solution.py:209
  108.0 33.8 %mixed_back.1 = bf16[12,64,512]{2,1,0:T(8,128)(2,1)} custom-call(bf16[2,8,64,512]{3,2,1,0:T(8,128)(2,1)} %get-tuple-element.30.x_ref), custom_call_target="tpu_custom_call" | custom-call | tf_op jit(solution)/shard_map/mixed_back/pallas_call | solution.py:496
  141.8 3.7 fusion.5
  146.6 5.8 %fusion.31 = f32[512,4096]{1,0:T(8,128)S(1)} fusion(bf16[512,768]{1,0:T(8,128)(2,1)S(1)} %multiply_convert_fusion.1.h2_ref, bf16[768,4096]{1,0:T(8,128)(2,1)} %param.24), kind=kOutput, calls=%fused_computation.60 | convolution fusion | flops 3221225472 | bytes 15466496 | tf_op jit(solution)/shard_map/dot_general | solution.py:580
  152.5 5.6 %fusion.21 = (f32[512,2048]{1,0:T(8,128)}, f32[512,2048]{1,0:T(8,128)}, bf16[512,2048]{1,0:T(8,128)(2,1)}) fusion(f32[512,4096]{1,0:T(8,128)S(1)} %fusion.31, bf16[2048,768]{1,0:T(8,128)(2,1)S(1)} %copy-done.19, bf16[1,512,768]{2,1,0:T(8,128)(2,1)S(1)} %copy-done.10), kind=kOutput, calls=%fused_computation.40 | convolution fusion | flops 1625292800 | bytes 22806528 | tf_op jit(solution)/shard_map/dot_general | solution.py:580
  158.2 4.1 add_convert_fusion.dgu_ref
  162.3 6.7 %fusion.14 = bf16[1,512,768]{2,1,0:T(8,128)(2,1)} fusion(f32[512,768]{1,0:T(8,128)S(1)} %get-tuple-element.62, bf16[512,2048]{1,0:T(8,128)(2,1)} %get-tuple-element.50.hidden_ref, bf16[2048,768]{1,0:T(8,128)(2,1)} %param.25), kind=kOutput, calls=%fused_computation.34 | convolution fusion | flops 1611399168 | bytes 7602176 | tf_op jit(solution)/shard_map/dot_general | solution.py:580
  169.0 3.6 multiply_reduce_fusion
  172.7 1.6 fusion.27
  174.8 2.1 fusion.8
  176.9 30.0 %grads_out.1 = (bf16[8,2,64,512]{3,2,1,0:T(8,128)(2,1)}, bf16[1440,16,256]{2,1,0:T(8,128)(2,1)}) custom-call(bf16[12,64,512]{2,1,0:T(8,128)(2,1)} %bitcast.86, bf16[512,768]{1,0:T(8,128)(2,1)} %copy-done.7, bf16[768,512]{1,0:T(8,128)(2,1)} %get-tuple-element.51.dgate_ref, bf16[512,768]{1,0:T(8,128)(2,1)} %copy-done.9, bf16[512,4096]{1,0:T(8,128)(2,1)} %copy-done.5, ...), custom_call_target="tpu_custom_call" | custom-call | tf_op jit(solution)/shard_map/grads_out/pallas_call | solution.py:565
  206.9 52.2 %attend_backward.1 = (bf16[8,3,2,64,512]{4,3,2,1,0:T(8,128)(2,1)}, f32[8,2,8,512]{3,2,1,0:T(8,128)}, f32[2,64,2]{2,1,0:T(8,128)}) custom-call(s32[1]{0:T(128)} %bitcast.2.device_ref, s32[16,16]{1,0:T(8,128)} %bitcast.96, f32[2]{0:T(128)} %dynamic_slice.6.bias_ref, bf16[8,3,2,64,512]{4,3,2,1,0:T(8,128)(2,1)} %get-tuple-element.28.raw_ref, ...), custom_call_target="tpu_custom_call" | custom-call | tf_op jit(solution)/shard_map/attend_backward/pallas_call | solution.py:355
  261.0 199.1 %last.1 = (bf16[448,16,256]{2,1,0:T(8,128)(2,1)}, bf16[1440,16,256]{2,1,0:T(8,128)(2,1)}, f32[512,768]{1,0:T(8,128)}) custom-call(bf16[8,3,2,64,512]{4,3,2,1,0:T(8,128)(2,1)} %get-tuple-element.37.draw_ref, f32[8,2,8,512]{3,2,1,0:T(8,128)} %get-tuple-element.38.dlogit_ref, bf16[1440,16,256]{2,1,0:T(8,128)(2,1)} %get-tuple-element.39.early_ref, ...), custom_call_target="tpu_custom_call" | custom-call | tf_op jit(solution)/shard_map/last/pallas_call | solution.py:854
  464.9 4.3 copy-done.2
  469.2 1.9 unpack.5
  471.1 3.3 copy-done.3
  474.5 2.0 copy-done.4
  476.5 5.9 %unpack.4 = f32[768,3072]{1,0:T(8,128)} custom-call(bf16[448,16,256]{2,1,0:T(8,128)(2,1)S(1)} %copy-done.4, bf16[1440,16,256]{2,1,0:T(8,128)(2,1)S(1)} %copy-done.3), custom_call_target="tpu_custom_call" | custom-call | tf_op jit(solution)/shard_map/unpack/pallas_call | solution.py:903
  482.3 2.9 unpack.7
  485.3 7.7 %unpack.6 = f32[768,4096]{1,0:T(8,128)} custom-call(bf16[1440,16,256]{2,1,0:T(8,128)(2,1)S(1)} %copy-done.3), custom_call_target="tpu_custom_call" | custom-call | tf_op jit(solution)/shard_map/unpack/pallas_call | solution.py:903
  (82 shorter events, 16.6 us)
Async XLA Ops:
  0.6 144.8 %copy-start = (bf16[768,768]{1,0:T(8,128)(2,1)S(1)}, bf16[768,768]{1,0:T(8,128)(2,1)}, u32[]{:S(2)}) copy-start(bf16[768,768]{1,0:T(8,128)(2,1)} %param.22) | copy-start | bytes 3538948
  0.7 5.9 %copy-start.6 = (bf16[1,512,768]{2,1,0:T(8,128)(2,1)S(1)}, bf16[1,512,768]{2,1,0:T(8,128)(2,1)}, u32[]{:S(2)}) copy-start(bf16[1,512,768]{2,1,0:T(8,128)(2,1)} %param.13) | copy-start | bytes 2359300
  0.7 5.9 %copy-start.16 = (f32[768]{0:T(1024)S(1)}, f32[768]{0:T(1024)}, u32[]{:S(2)}) copy-start(f32[768]{0:T(1024)} %param.16) | copy-start | bytes 9220
  2.1 5.6 %copy-start.17 = (f32[768]{0:T(1024)S(1)}, f32[768]{0:T(1024)}, u32[]{:S(2)}) copy-start(f32[768]{0:T(1024)} %param.20) | copy-start | bytes 9220
  2.2 5.8 %copy-start.18 = (f32[768]{0:T(1024)S(1)}, f32[768]{0:T(1024)}, u32[]{:S(2)}) copy-start(f32[768]{0:T(1024)} %param.21) | copy-start | bytes 9220
  9.3 132.5 %copy-start.7 = (bf16[512,768]{1,0:T(8,128)(2,1)}, bf16[512,768]{1,0:T(8,128)(2,1)S(1)}, u32[]{:S(2)}) copy-start(bf16[512,768]{1,0:T(8,128)(2,1)S(1)} %fusion.11.h1_ref.h_ref) | copy-start | bytes 2359300
  145.4 0.9 copy-start.14
  145.4 0.9 copy-start.15
  146.6 5.9 %copy-start.9 = (bf16[512,768]{1,0:T(8,128)(2,1)}, bf16[512,768]{1,0:T(8,128)(2,1)S(1)}, u32[]{:S(2)}) copy-start(bf16[512,768]{1,0:T(8,128)(2,1)S(1)} %multiply_convert_fusion.1.h2_ref) | copy-start | bytes 2359300
  146.6 5.9 %copy-start.10 = (bf16[1,512,768]{2,1,0:T(8,128)(2,1)S(1)}, bf16[1,512,768]{2,1,0:T(8,128)(2,1)}, u32[]{:S(2)}) copy-start(bf16[1,512,768]{2,1,0:T(8,128)(2,1)} %param.14) | copy-start | bytes 2359300
  146.6 5.9 %copy-start.19 = (bf16[2048,768]{1,0:T(8,128)(2,1)S(1)}, bf16[2048,768]{1,0:T(8,128)(2,1)}, u32[]{:S(2)}) copy-start(bf16[2048,768]{1,0:T(8,128)(2,1)} %param.25) | copy-start | bytes 9437188
  146.6 22.3 %slice-start = ((s8[6291456]{0:T(1024)(128)(4,1)}), s8[4194304]{0:T(1024)(128)(4,1)S(1)}, s32[]{:S(2)}) async-start(s8[6291456]{0:T(1024)(128)(4,1)} %bitcast.83), calls=%async_computation | async-start | bytes 8388608
  152.5 16.5 %slice-start.1 = ((s8[6291456]{0:T(1024)(128)(4,1)}), s8[2097152]{0:T(1024)(128)(4,1)S(1)}, s32[]{:S(2)}) async-start(s8[6291456]{0:T(1024)(128)(4,1)} %bitcast.83), calls=%async_computation.1 | async-start | bytes 4194304
  162.2 6.7 %copy-start.5 = (bf16[512,4096]{1,0:T(8,128)(2,1)}, bf16[512,4096]{1,0:T(8,128)(2,1)S(1)}, u32[]{:S(2)}) copy-start(bf16[512,4096]{1,0:T(8,128)(2,1)S(1)} %add_convert_fusion.dgu_ref) | copy-start | bytes 12582916
  172.6 1.6 copy-start.11
  172.6 2.2 copy-start.13
  174.3 2.7 copy-start.8
  464.9 4.4 copy-start.2
  469.2 5.2 %copy-start.3 = (bf16[1440,16,256]{2,1,0:T(8,128)(2,1)S(1)}, bf16[1440,16,256]{2,1,0:T(8,128)(2,1)}, u32[]{:S(2)}) copy-start(bf16[1440,16,256]{2,1,0:T(8,128)(2,1)} %get-tuple-element.43.refs_1_.refs_0_) | copy-start | bytes 35389444
  474.4 2.0 copy-start.4
  485.2 7.7 %copy-start.12 = (f32[512,768]{1,0:T(8,128)S(1)}, f32[512,768]{1,0:T(8,128)}, u32[]{:S(2)}) copy-start(f32[512,768]{1,0:T(8,128)} %get-tuple-element.41) | copy-start | bytes 4718596
  485.3 8.8 %copy-start.1 = (bf16[768,768]{1,0:T(8,128)(2,1)S(1)}, bf16[768,768]{1,0:T(8,128)(2,1)}, u32[]{:S(2)}) copy-start(bf16[768,768]{1,0:T(8,128)(2,1)} %param.22) | copy-start | bytes 3538948

commit v4 on v3

--- a/solution.py
+++ b/solution.py
@@ -21,6 +21,7 @@
 UNROLL_BACK = 4
 NN = (((1,), (0,)), ((), ()))
 NT = (((1,), (1,)), ((), ()))
+TN = (((0,), (0,)), ((), ()))
 
 
 def mm(a, b, dims=NN):
@@ -120,6 +121,46 @@
     return bottom if top is None else jnp.concatenate([top, bottom], 0)
 
 
+def prepare_block(count, block, carried, raw_ref, logit_ref, gain_ref, cum_ref, q_ref, k_ref, kt_ref, vt_ref):
+    place, lanes = place_of(block, count), lanes_of(block, count)
+    q_raw, k_raw, v_raw = (raw_ref[place, i, :, lanes].astype(f32) for i in range(3))
+    cum = cum_ref[pl.ds(place, 1), lanes]
+    parts = split3(cum)
+    one = jnp.ones_like(cum)
+    query = q_raw * lax.rsqrt(jnp.mean(q_raw * q_raw, 0, keepdims=True) + EPS) * (gain_ref[:, 0:1] * (SCORE * LOG2E))
+    q_ref[block] = stack_rows(query, (*parts, one, one, one), 128).astype(bf16)
+    rate_k = jax.nn.sigmoid(logit_ref[place, 1:2, lanes])
+    rate_v = jax.nn.sigmoid(logit_ref[place, 2:3, lanes])
+    key = k_raw + rate_k * (shifted(k_raw, carried[0]) - k_raw)
+    key = key * lax.rsqrt(jnp.mean(key * key, 0, keepdims=True) + EPS) * gain_ref[:, 1:2]
+    value = v_raw + rate_v * (shifted(v_raw, carried[1]) - v_raw)
+    k_ref[block] = stack_rows(key, (one, one, one, *(-c for c in parts)), 128).T.astype(bf16)
+    kt_ref[block] = stack_rows(key, (one,), 80).astype(bf16)
+    vt_ref[block] = stack_rows(value, (one, one, one), 80).astype(bf16)
+    return k_raw, v_raw
+
+
+def finish_block(count, block, acc_ref, cum_ref, mixed_full_ref, mixed_ref, q_ref):
+    place, lanes = place_of(block, count), lanes_of(block, count)
+    summed = acc_ref[block]
+    norm = summed[HDIM : HDIM + 1]
+    mixed = summed[:HDIM] * (1.0 / norm)
+    mixed_full_ref[block] = mixed
+    mixed_ref[place, :, lanes] = mixed.astype(bf16)
+    parts = split3(cum_ref[pl.ds(place, 1), lanes] - jnp.log2(norm))
+    one = jnp.ones_like(norm)
+    q_ref[block, HDIM : HDIM + 16, :] = stack_rows(None, (*parts, one, one, one), 16).astype(bf16)
+
+
+def log_forget_sums(logits, count):
+    log_forget = jnp.minimum(logits, 0.0) - jnp.log1p(jnp.exp(-jnp.abs(logits)))
+    return running_sum(log_forget, count, False) * LOG2E
+
+
+def causal():
+    return lax.broadcasted_iota(jnp.int32, (BLK, BLK), 0) <= lax.broadcasted_iota(jnp.int32, (BLK, BLK), 1)
+
+
 def forward_kernel(count, device_ref, skip_ref, bias_ref, raw_ref, logit_ref, gain_ref,
                    mixed_ref, mixed_full_ref, q_ref, k_ref, kt_ref, vt_ref,
                    cum_ref, acc_ref, pairs_ref, own_ref):
@@ -127,41 +168,20 @@
     device = device_ref[0]
     blocks = 2 * count
     pair_steps, own_steps = list_pairs(skip_ref, pairs_ref, own_ref, device, slot, count, UNROLL)
-    logits = logit_ref[:, 0, :] + bias_ref[slot]
-    log_forget = jnp.minimum(logits, 0.0) - jnp.log1p(jnp.exp(-jnp.abs(logits)))
-    cum_ref[...] = running_sum(log_forget, count, False) * LOG2E
-    gain_q, gain_k = gain_ref[:, 0:1], gain_ref[:, 1:2]
+    cum_ref[...] = log_forget_sums(logit_ref[:, 0, :] + bias_ref[slot], count)
 
     def prepare(block, carried):
-        place, lanes = place_of(block, count), lanes_of(block, count)
-        q_raw, k_raw, v_raw = (raw_ref[place, i, :, lanes].astype(f32) for i in range(3))
-        cum = cum_ref[pl.ds(place, 1), lanes]
-        parts = split3(cum)
-        one = jnp.ones_like(cum)
-        query = q_raw * lax.rsqrt(jnp.mean(q_raw * q_raw, 0, keepdims=True) + EPS) * (gain_q * (SCORE * LOG2E))
-        q_ref[block] = stack_rows(query, (*parts, one, one, one), 128).astype(bf16)
-        rate_k = jax.nn.sigmoid(logit_ref[place, 1:2, lanes])
-        rate_v = jax.nn.sigmoid(logit_ref[place, 2:3, lanes])
-        key = k_raw + rate_k * (shifted(k_raw, carried[0]) - k_raw)
-        key = key * lax.rsqrt(jnp.mean(key * key, 0, keepdims=True) + EPS) * gain_k
-        value = v_raw + rate_v * (shifted(v_raw, carried[1]) - v_raw)
-        k_ref[block] = stack_rows(key, (one, one, one, *(-c for c in parts)), 128).T.astype(bf16)
-        kt_ref[block] = stack_rows(key, (one,), 80).astype(bf16)
-        vt_ref[block] = stack_rows(value, (one, one, one), 80).astype(bf16)
-        return k_raw, v_raw
+        return prepare_block(count, block, carried, raw_ref, logit_ref, gain_ref, cum_ref, q_ref, k_ref, kt_ref, vt_ref)
 
     zero = jnp.zeros((HDIM, BLK), f32)
     lax.fori_loop(0, blocks, prepare, (zero, zero))
     q_ref[blocks] = jnp.zeros(q_ref.shape[1:], bf16)
-
-    t = lax.broadcasted_iota(jnp.int32, (BLK, BLK), 0)
-    p = lax.broadcasted_iota(jnp.int32, (BLK, BLK), 1)
 
     def together(pairs, diagonal):
         scores = [mm(k_ref[column], q_ref[row]) for row, column in pairs]
         weights = [jnp.exp2(score) for score in scores]
         if diagonal:
-            weights = [jnp.where(t <= p, weight, 0.0) for weight in weights]
+            weights = [jnp.where(causal(), weight, 0.0) for weight in weights]
         weights = [weight.astype(bf16) for weight in weights]
         parts = [mm(vt_ref[column], weight) for (row, column), weight in zip(pairs, weights)]
         for (row, column), part in zip(pairs, parts):
@@ -181,18 +201,29 @@
     lax.fori_loop(0, pair_steps, kept_pairs, 0)
 
     def finish(block, carried):
-        place, lanes = place_of(block, count), lanes_of(block, count)
-        total = acc_ref[block]
-        norm = total[HDIM : HDIM + 1]
-        mixed = total[:HDIM] * (1.0 / norm)
-        mixed_full_ref[block] = mixed
-        mixed_ref[place, :, lanes] = mixed.astype(bf16)
-        parts = split3(cum_ref[pl.ds(place, 1), lanes] - jnp.log2(norm))
-        one = jnp.ones_like(norm)
-        q_ref[block, HDIM : HDIM + 16, :] = stack_rows(None, (*parts, one, one, one), 16).astype(bf16)
+        finish_block(count, block, acc_ref, cum_ref, mixed_full_ref, mixed_ref, q_ref)
         return carried
 
     lax.fori_loop(0, blocks, finish, 0)
+
+
+def own_places(device, slot, count):
+    start = (first_head(device, count) + slot) * count
+    low = jnp.clip(HEADS * device - start, 0, count)
+    return low, jnp.clip(HEADS * device + HEADS - start, low, count)
+
+
+def pairs_of_place(place, batch, size, count):
+    found = []
+    for i in range(size):
+        number = batch * size + i
+        lower = number < place
+        found.append((jnp.where(lower, place, 2 * count - 1 - place), jnp.where(lower, number, number - place)))
+    return found
+
+
+def keep_factor(skip_ref, row, column):
+    return jnp.where(skip_ref[row, column] == 0, 1.0, 0.0)
 
 
 def buffers(count):
@@ -276,14 +307,11 @@
     do_ref[blocks] = jnp.zeros(do_ref.shape[1:], bf16)
     dq_ref[blocks] = jnp.zeros(dq_ref.shape[1:], f32)
 
-    t = lax.broadcasted_iota(jnp.int32, (BLK, BLK), 0)
-    p = lax.broadcasted_iota(jnp.int32, (BLK, BLK), 1)
-
     def together(pairs, diagonal):
         scores = [mm(k_ref[column], q_ref[row]) for row, column in pairs]
         weights = [jnp.exp2(score) for score in scores]
         if diagonal:
-            weights = [jnp.where(t <= p, weight, 0.0) for weight in weights]
+            weights = [jnp.where(causal(), weight, 0.0) for weight in weights]
         d_weights = [mm(v_ref[column], do_ref[row]) for row, column in pairs]
         low_weights = [weight.astype(bf16) for weight in weights]
         d_scores = [(weight * d_weight).astype(bf16) for weight, d_weight in zip(weights, d_weights)]
@@ -504,9 +532,6 @@
     )(mixed)
 
 
-TN = (((0,), (0,)), ((), ()))
-
-
 def grads_out_kernel(count, x_ref, h1_ref, dgate_ref, h2_ref, dgu_ref, hidden_ref, dlow_ref, gated_ref, branch_ref,
                      o_ref, grads_ref, send, recv, local):
     me = greet(count)
@@ -578,6 +603,201 @@
 
 def dot(a, b, i, j):
     return lax.dot_general(a, b, (((i,), (j,)), ((), ())), preferred_element_type=f32)
+
+
+def front_kernel(count, skip_ref, bias_ref, x_ref, w_ref, wsmall_ref, gain_ref, gains_ref,
+                 h_ref, gate_ref, att_ref, raw_out, logit_out, full_out, q_out, k_out, kt_out, vt_out,
+                 ht_ref, proj_ref, small_ref, raw_ref, logit_ref, mixed_ref, full_ref, q_ref, k_ref, kt_ref, vt_ref, cum_ref, acc_ref,
+                 send, recv, own, back_send, back_recv, back_own, keep):
+    me = lax.axis_index("seq")
+    barrier = pltpu.get_barrier_semaphore()
+    for k in range(1, count):
+        pl.semaphore_signal(barrier, inc=1, device_id={"seq": lax.rem(me + k, count)}, device_id_type=MESH)
+    blocks = 2 * count
+    rows = x_ref.shape[0]
+    for i in range(rows // 128):
+        here = slice(128 * i, 128 * i + 128)
+        v = x_ref[here].astype(f32)
+        normed = v * lax.rsqrt(jnp.mean(v * v, 1, keepdims=True) + EPS) * gain_ref[...]
+        h_ref[here] = normed.astype(bf16)
+        ht_ref[:, here] = normed.T.astype(bf16)
+
+    def project(i, carried):
+        block = mm(w_ref[:, pl.ds(pl.multiple_of(256 * i, 256), 256)], ht_ref[...], TN)
+        proj_ref[pl.ds(4 * i, 4)] = block.astype(bf16).reshape(4, HDIM, rows)
+        return carried
+
+    small_ref[...] = mm(wsmall_ref[...], ht_ref[...], TN).reshape(HEADS, 8, rows)
+    lax.fori_loop(0, 9, project, 0)
+    pl.semaphore_wait(barrier, count - 1)
+    first = first_head(me, count)
+
+    def out(slot, k, peer):
+        head = first_head(peer, count) + slot
+        sems = lambda i: (send.at[k, slot, i], recv.at[k, slot, i], peer)
+        return [
+            push(proj_ref.at[head], raw_ref.at[me, 0, slot], *sems(0)),
+            push(proj_ref.at[HEADS + head], raw_ref.at[me, 1, slot], *sems(1)),
+            push(proj_ref.at[2 * HEADS + head], raw_ref.at[me, 2, slot], *sems(2)),
+            push(small_ref.at[head], logit_ref.at[me, slot], *sems(3)),
+        ]
+
+    def own_copies(slot):
+        head = first + slot
+        return [
+            pltpu.make_async_copy(proj_ref.at[head], raw_ref.at[me, 0, slot], own.at[slot, 0]),
+            pltpu.make_async_copy(proj_ref.at[HEADS + head], raw_ref.at[me, 1, slot], own.at[slot, 1]),
+            pltpu.make_async_copy(proj_ref.at[2 * HEADS + head], raw_ref.at[me, 2, slot], own.at[slot, 2]),
+            pltpu.make_async_copy(small_ref.at[head], logit_ref.at[me, slot], own.at[slot, 3]),
+        ]
+
+    for slot in range(2):
+        for k in far_first(count):
+            peer = lax.rem(me + k, count)
+            copies = out(slot, k, peer)
+            pl.when(is_mine(peer, slot, me, count))(copies[0].start)
+            for copy in copies[1:]:
+                copy.start()
+        for copy in own_copies(slot):
+            copy.start()
+
+    def gate(i, carried):
+        here = pl.ds(pl.multiple_of(256 * i, 256), 256)
+        gate_ref[here] = mm(w_ref[:, pl.ds(pl.multiple_of(3 * D + 256 * i, 256), 256)], ht_ref[...], TN)
+        return carried
+
+    lax.fori_loop(0, 3, gate, 0)
+
+    def saved(slot):
+        return [
+            pltpu.make_async_copy(src.at[slot], dst.at[slot], keep.at[slot, i])
+            for i, (src, dst) in enumerate(
+                ((full_ref, full_out), (q_ref, q_out), (k_ref, k_out), (kt_ref, kt_out), (vt_ref, vt_out)))
+        ]
+
+    def back(slot, k, peer):
+        target = att_ref.at[pl.ds(pl.multiple_of((first + slot) * HDIM, HDIM), HDIM)]
+        if k:
+            return push(mixed_ref.at[slot, peer], target, back_send.at[k, slot], back_recv.at[first + slot], peer)
+        return pltpu.make_async_copy(mixed_ref.at[slot, peer], target, back_own.at[slot])
+
+    def one_slot(slot, carried):
+        for copy in own_copies(slot):
+            copy.wait()
+        for k in far_first(count):
+            source = lax.rem(me + count - k, count)
+            copies = out(slot, k, source)
+            pl.when(is_mine(me, slot, source, count))(copies[0].wait_recv)
+            for copy in copies[1:]:
+                copy.wait_recv()
+        raws, logits, gains = raw_ref.at[:, :, slot], logit_ref.at[:, slot], gains_ref.at[slot]
+        qs, ks, kts, vts = q_ref.at[slot], k_ref.at[slot], kt_ref.at[slot], vt_ref.at[slot]
+        cum_ref[...] = log_forget_sums(logits[:, 0, :] + bias_ref[slot], count)
+
+        def prepare(block, state):
+            acc_ref[block] = jnp.zeros(acc_ref.shape[1:], f32)
+            return prepare_block(count, block, state, raws, logits, gains, cum_ref, qs, ks, kts, vts)
+
+        zero = jnp.zeros((HDIM, BLK), f32)
+        lax.fori_loop(0, blocks, prepare, (zero, zero))
+        qs[blocks] = jnp.zeros(q_ref.shape[2:], bf16)
+
+        def batch(pairs, on_diagonal):
+            weights = [jnp.exp2(mm(ks[column], qs[row])) for row, column in pairs]
+            low = []
+            for (row, column), weight, diagonal in zip(pairs, weights, on_diagonal):
+                weight = jnp.where(causal(), weight, 0.0) if diagonal else weight * keep_factor(skip_ref, row, column)
+                low.append(weight.astype(bf16))
+            parts = [mm(vts[column], weight) for (_, column), weight in zip(pairs, low)]
+            for (row, _), part in zip(pairs, parts):
+                acc_ref[row] += part
+
+        def one_place(place, state):
+            number = blocks // UNROLL
+            for i in range(number):
+                pairs = pairs_of_place(place, i, UNROLL, count)
+                diagonal = [False] * UNROLL
+                if i == number - 1:
+                    pairs.append((place, place))
+                    diagonal[-1:] = [True, True]
+                batch(pairs, diagonal)
+            return state
+
+        low, high = own_places(me, slot, count)
+        lax.fori_loop(low, high, one_place, 0)
+
+        def finish(block, state):
+            finish_block(count, block, acc_ref, cum_ref, full_ref.at[slot], mixed_ref.at[slot], qs)
+            return state
+
+        lax.fori_loop(0, blocks, finish, 0)
+        for k in far_first(count) + [0]:
+            peer = lax.rem(me + k, count)
+            pl.when(is_mine(me, slot, peer, count))(back(slot, k, peer).start)
+        for copy in saved(slot):
+            copy.start()
+        return carried
+
+    lax.fori_loop(0, 2, one_slot, 0)
+    keep_raw = [
+        pltpu.make_async_copy(raw_ref, raw_out, keep.at[0, 5]),
+        pltpu.make_async_copy(logit_ref, logit_out, keep.at[1, 5]),
+    ]
+    for copy in keep_raw:
+        copy.start()
+    for slot in range(2):
+        for k in far_first(count):
+            peer = lax.rem(me + k, count)
+            copies = out(slot, k, peer)
+            pl.when(is_mine(peer, slot, me, count))(copies[0].wait_send)
+            for copy in copies[1:]:
+                copy.wait_send()
+        for k in far_first(count) + [0]:
+            peer = lax.rem(me + k, count)
+            copy = back(slot, k, peer)
+            pl.when(is_mine(me, slot, peer, count))(copy.wait_send if k else copy.wait)
+    for head in range(HEADS):
+        source = holder(head, me, count)
+        copy = push(mixed_ref.at[0, 0], att_ref.at[pl.ds(head * HDIM, HDIM)], back_send.at[0, 0], back_recv.at[head], lax.rem(me + 1, count))
+        pl.when(source != me)(copy.wait_recv)
+    for slot in range(2):
+        for copy in saved(slot):
+            copy.wait()
+    for copy in keep_raw:
+        copy.wait()
+
+
+def front(count, skip, bias, x, w_attn, w_small, gain, gains):
+    rows = x.shape[0]
+    blocks = 2 * count
+    vmem = pl.BlockSpec(memory_space=pltpu.VMEM)
+    smem = pl.BlockSpec(memory_space=pltpu.SMEM)
+    dma = pltpu.SemaphoreType.DMA
+    raw, logit = (count, 3, 2, HDIM, rows), (count, 2, 8, rows)
+    state = [((2, blocks, HDIM, BLK), f32), ((2, blocks + 1, 128, BLK), bf16), ((2, blocks, BLK, 128), bf16),
+             ((2, blocks, 80, BLK), bf16), ((2, blocks, 80, BLK), bf16)]
+    return pl.pallas_call(
+        functools.partial(front_kernel, count),
+        out_shape=[jax.ShapeDtypeStruct(s, t) for s, t in [
+            ((rows, D), bf16), ((D, rows), f32), ((D, rows), bf16), (raw, bf16), (logit, f32)] + state],
+        in_specs=[smem, smem] + [vmem] * 5,
+        out_specs=[vmem] * 3 + [ANY] * 7,
+        scratch_shapes=[
+            pltpu.VMEM((D, rows), bf16),
+            pltpu.VMEM((3 * HEADS, HDIM, rows), bf16),
+            pltpu.VMEM((HEADS, 8, rows), f32),
+            pltpu.VMEM(raw, bf16),
+            pltpu.VMEM(logit, f32),
+            pltpu.VMEM((2, count, HDIM, rows), bf16),
+        ] + [pltpu.VMEM(s, t) for s, t in state] + [
+            pltpu.VMEM((count, rows), f32),
+            pltpu.VMEM((blocks + 1, 80, BLK), f32),
+            dma((count, 2, 4)), dma((count, 2, 4)), dma((2, 4)),
+            dma((count, 2)), dma((HEADS,)), dma((2,)), dma((2, 6)),
+        ],
+        compiler_params=pltpu.CompilerParams(collective_id=0, has_side_effects=True, vmem_limit_bytes=60 * 2**20),
+        name="front",
+    )(skip, bias, x, w_attn, w_small, gain, gains)
 
 
 SMALL = 48
@@ -935,15 +1155,19 @@
     bias = lax.dynamic_slice_in_dim(forget_bias, head, 2, 0)
     w_small = jnp.pad(w_heads.reshape(D, 3, HEADS).transpose(0, 2, 1), ((0, 0), (0, 0), (0, 5))).reshape(D, HEADS * 8)
 
-    normed_attn, norm_back_attn = jax.vjp(rms_scale, inputs, gain_attn)
-    h_first = normed_attn.astype(bf16)
-    qkv = dot(w_attn[:, : 3 * D], h_first, 0, 1).astype(bf16).reshape(3, HEADS, HDIM, rows)
-    gate_logit = dot(w_attn[:, 3 * D :], h_first, 0, 1)
-    logits_here = dot(w_small, h_first, 0, 1).reshape(HEADS, 8, rows)
-
-    raw, logits = heads_out(qkv, logits_here, count)
-    mixed_low, mixed, q, k, kt, vt = attend_forward(device, skip, bias, raw, logits, gains)
-    attended = mixed_back(mixed_low, count).reshape(D, rows).astype(f32)
+    if count <= 8:
+        h_first, gate_logit, attended, raw, logits, mixed, q, k, kt, vt = front(
+            count, skip, bias, tokens[0], w_attn, w_small, gain_attn[None], gains
+        )
+    else:
+        h_first = rms_scale(inputs, gain_attn).astype(bf16)
+        qkv = dot(w_attn[:, : 3 * D], h_first, 0, 1).astype(bf16).reshape(3, HEADS, HDIM, rows)
+        gate_logit = dot(w_attn[:, 3 * D :], h_first, 0, 1)
+        logits_here = dot(w_small, h_first, 0, 1).reshape(HEADS, 8, rows)
+        raw, logits = heads_out(qkv, logits_here, count)
+        mixed_low, mixed, q, k, kt, vt = attend_forward(device, skip, bias, raw, logits, gains)
+        attended = mixed_back(mixed_low, count).reshape(D, rows)
+    attended = attended.astype(f32)
 
     gate_open = jax.nn.sigmoid(gate_logit)
     gated = (gate_open * attended).astype(bf16)

time: 496 us -> 461 us (0.929)
  Pallas kernels: 422 us -> 403 us
  matrix products: 35.3 us -> 22.6 us
    dot_general x9 -> x6, matrix products: 35.3 us -> 22.6 us  [dot(): lax.dot_general(a, b, (((i,), (j,)), ((), ())), preferred_element_type=f32)]
    pallas_call x3 -> x1, Pallas kernels: 122 us -> 110 us  [front(): pl.pallas_call(functools.partial(front_kernel, count), out_shape=[jax.Sha...]
    pallas_call x1, Pallas kernels: 30 us -> 23.7 us  [grads_out(): pl.pallas_call(functools.partial(grads_out_kernel, count), out_shape=[jax...]
    unnamed x47 -> x39, local copies, waits for them, and re-layouts: 11.6 us -> 11.5 us
where the time goes in v4:
time: 461 us; the launch traced here: 460 us
  Pallas kernels  403 us (87%)
  local copies, waits for them, and re-layouts  23.6 us (5%)
  matrix products  22.6 us (5%)
  other arithmetic  9.57 us (2%)
    pallas_call x1, Pallas kernels, last(): pl.pallas_call(functools.partial(last_kernel, count, sets), out_shape=[ja...  199 us
    pallas_call x1, Pallas kernels, front(): pl.pallas_call(functools.partial(front_kernel, count), out_shape=[jax.Sha...  110 us
    pallas_call x1, Pallas kernels, attend_backward(): pl.pallas_call(functools.partial(backward_kernel, count), grid_spec=pltpu...  52.4 us
    pallas_call x1, Pallas kernels, grads_out(): pl.pallas_call(functools.partial(grads_out_kernel, count), out_shape=[jax...  23.7 us
    dot_general x6, matrix products, dot(): lax.dot_general(a, b, (((i,), (j,)), ((), ())), preferred_element_type=f32)  22.6 us
    pallas_call x4, Pallas kernels, unpack(): pl.pallas_call(functools.partial(unpack_kernel, [blocks for _, _, blocks...  18.3 us
    unnamed x39, local copies, waits for them, and re-layouts  11.5 us

profile of v4, /device:TPU:0, one launch (start us, length us, event | category | flops | bytes accessed | tf_op | source)
XLA Modules:
  0.0 459.8 jit_solution(9347167635892028064)
XLA Ops:
  0.7 1.3 dynamic_slice.6.bias_ref
  2.1 1.3 broadcast_in_dim.26.gain_ref
  5.1 1.0 stack_reshape.8
  6.1 1.0 stack_reshape.9
  7.8 110.0 %front.1 = (bf16[512,768]{1,0:T(8,128)(2,1)}, f32[768,512]{1,0:T(8,128)}, bf16[768,512]{1,0:T(8,128)(2,1)}, bf16[8,3,2,64,512]{4,3,2,1,0:T(8,128)(2,1)}, f32[8,2...) custom-call(s32[16,16]{1,0:T(8,128)} %bitcast.67, ...), custom_call_target="tpu_custom_call" | custom-call | tf_op jit(solution)/shard_map/front/pallas_call | solution.py:779
  117.8 2.2 fusion.3.gated_ref
  121.3 3.4 fusion.19
  124.7 5.6 %fusion.10 = (f32[512,2048]{1,0:T(8,128)}, f32[512,2048]{1,0:T(8,128)}, bf16[512,2048]{1,0:T(8,128)(2,1)}) fusion(f32[512,4096]{1,0:T(8,128)S(1)} %fusion.19, bf16[2048,768]{1,0:T(8,128)(2,1)S(1)} %copy-done.15, bf16[1,512,768]{2,1,0:T(8,128)(2,1)S(1)} %copy-done.8), kind=kOutput, calls=%fused_computation.25 | convolution fusion | flops 1625292800 | bytes 22806528 | tf_op jit(solution)/shard_map/dot_general | solution.py:605
  130.3 4.1 add_convert_fusion.dgu_ref
  134.4 6.7 %fusion.9 = bf16[1,512,768]{2,1,0:T(8,128)(2,1)} fusion(f32[512,768]{1,0:T(8,128)S(1)} %get-tuple-element.64, bf16[512,2048]{1,0:T(8,128)(2,1)} %get-tuple-element.54.hidden_ref, bf16[2048,768]{1,0:T(8,128)(2,1)} %param.25), kind=kOutput, calls=%fused_computation.24 | convolution fusion | flops 1611399168 | bytes 7602176 | tf_op jit(solution)/shard_map/dot_general | solution.py:605
  141.1 3.6 multiply_reduce_fusion
  144.8 1.6 fusion.15
  146.9 2.3 fusion.6
  149.2 23.7 %grads_out.1 = (bf16[8,2,64,512]{3,2,1,0:T(8,128)(2,1)}, bf16[1440,16,256]{2,1,0:T(8,128)(2,1)}) custom-call(bf16[12,64,512]{2,1,0:T(8,128)(2,1)} %bitcast.62, bf16[512,768]{1,0:T(8,128)(2,1)} %get-tuple-element.34.h1_ref.h_ref, bf16[768,512]{1,0:T(8,128)(2,1)} %get-tuple-element.55.dgate_ref, bf16[512,768]{1,0:T(8,128)(2,1)} %copy-done.6, ...), custom_call_target="tpu_custom_call" | custom-call | tf_op jit(solution)/shard_map/grads_out/pallas_call | solution.py:590
  173.0 52.4 %attend_backward.1 = (bf16[8,3,2,64,512]{4,3,2,1,0:T(8,128)(2,1)}, f32[8,2,8,512]{3,2,1,0:T(8,128)}, f32[2,64,2]{2,1,0:T(8,128)}) custom-call(s32[1]{0:T(128)} %bitcast.5.device_ref, s32[16,16]{1,0:T(8,128)} %bitcast.68, f32[2]{0:T(128)} %dynamic_slice.6.bias_ref, bf16[8,3,2,64,512]{4,3,2,1,0:T(8,128)(2,1)} %get-tuple-element.32.raw_ref, ...), custom_call_target="tpu_custom_call" | custom-call | tf_op jit(solution)/shard_map/attend_backward/pallas_call | solution.py:383
  227.2 198.6 %last.1 = (bf16[448,16,256]{2,1,0:T(8,128)(2,1)}, bf16[1440,16,256]{2,1,0:T(8,128)(2,1)}, f32[512,768]{1,0:T(8,128)}) custom-call(bf16[8,3,2,64,512]{4,3,2,1,0:T(8,128)(2,1)} %get-tuple-element.41.draw_ref, f32[8,2,8,512]{3,2,1,0:T(8,128)} %get-tuple-element.42.dlogit_ref, bf16[1440,16,256]{2,1,0:T(8,128)(2,1)} %get-tuple-element.43.early_ref, ...), custom_call_target="tpu_custom_call" | custom-call | tf_op jit(solution)/shard_map/last/pallas_call | solution.py:1074
  430.6 4.3 copy-done.2
  434.9 1.9 unpack.5
  436.8 3.3 copy-done.3
  440.1 2.0 copy-done.4
  442.2 5.9 %unpack.4 = f32[768,3072]{1,0:T(8,128)} custom-call(bf16[448,16,256]{2,1,0:T(8,128)(2,1)S(1)} %copy-done.4, bf16[1440,16,256]{2,1,0:T(8,128)(2,1)S(1)} %copy-done.3), custom_call_target="tpu_custom_call" | custom-call | tf_op jit(solution)/shard_map/unpack/pallas_call | solution.py:1123
  448.0 2.9 unpack.7
  450.9 7.7 %unpack.6 = f32[768,4096]{1,0:T(8,128)} custom-call(bf16[1440,16,256]{2,1,0:T(8,128)(2,1)S(1)} %copy-done.3), custom_call_target="tpu_custom_call" | custom-call | tf_op jit(solution)/shard_map/unpack/pallas_call | solution.py:1123
  458.6 1.1 copy.72
  (66 shorter events, 10.8 us)
Async XLA Ops:
  0.6 119.4 %copy-start = (bf16[768,768]{1,0:T(8,128)(2,1)S(1)}, bf16[768,768]{1,0:T(8,128)(2,1)}, u32[]{:S(2)}) copy-start(bf16[768,768]{1,0:T(8,128)(2,1)} %param.22) | copy-start | bytes 3538948
  7.8 112.2 %copy-start.7 = (bf16[1,512,768]{2,1,0:T(8,128)(2,1)S(1)}, bf16[1,512,768]{2,1,0:T(8,128)(2,1)}, u32[]{:S(2)}) copy-start(bf16[1,512,768]{2,1,0:T(8,128)(2,1)} %param.13) | copy-start | bytes 2359300
  7.8 113.4 %slice-start = ((s8[6291456]{0:T(1024)(128)(4,1)}), s8[2097152]{0:T(1024)(128)(4,1)S(1)}, s32[]{:S(2)}) async-start(s8[6291456]{0:T(1024)(128)(4,1)} %bitcast.53), calls=%async_computation | async-start | bytes 4194304
  117.7 3.5 slice-start.1
  120.0 0.9 copy-start.10
  120.0 1.0 copy-start.14
  121.2 3.5 copy-start.6
  121.2 3.5 copy-start.8
  121.2 3.5 copy-start.15
  134.4 6.7 %copy-start.5 = (bf16[512,4096]{1,0:T(8,128)(2,1)}, bf16[512,4096]{1,0:T(8,128)(2,1)S(1)}, u32[]{:S(2)}) copy-start(bf16[512,4096]{1,0:T(8,128)(2,1)S(1)} %add_convert_fusion.dgu_ref) | copy-start | bytes 12582916
  144.8 1.6 copy-start.11
  144.8 2.1 copy-start.13
  146.4 2.8 copy-start.9
  430.6 4.4 copy-start.2
  434.9 5.2 %copy-start.3 = (bf16[1440,16,256]{2,1,0:T(8,128)(2,1)S(1)}, bf16[1440,16,256]{2,1,0:T(8,128)(2,1)}, u32[]{:S(2)}) copy-start(bf16[1440,16,256]{2,1,0:T(8,128)(2,1)} %get-tuple-element.47.refs_1_.refs_0_) | copy-start | bytes 35389444
  440.1 2.0 copy-start.4
  450.9 7.7 %copy-start.12 = (f32[512,768]{1,0:T(8,128)S(1)}, f32[512,768]{1,0:T(8,128)}, u32[]{:S(2)}) copy-start(f32[512,768]{1,0:T(8,128)} %get-tuple-element.45) | copy-start | bytes 4718596
  450.9 8.8 %copy-start.1 = (bf16[768,768]{1,0:T(8,128)(2,1)S(1)}, bf16[768,768]{1,0:T(8,128)(2,1)}, u32[]{:S(2)}) copy-start(bf16[768,768]{1,0:T(8,128)(2,1)} %param.22) | copy-start | bytes 3538948

commit v5 on v4

--- a/solution.py
+++ b/solution.py
@@ -282,6 +282,69 @@
     return scale * (gu - hat * jnp.mean(hat * gu, 0, keepdims=True)), hat * u
 
 
+def prepare_back(count, block, dmixed_ref, mixed_ref, vt_ref, do_ref, v_ref, dq_ref, dk_ref, dv_ref):
+    place, lanes = place_of(block, count), lanes_of(block, count)
+    d_out = dmixed_ref[place, :, lanes].astype(f32)
+    delta = jnp.sum(d_out * mixed_ref[block], 0, keepdims=True)
+    do_ref[block] = stack_rows(d_out, [-d for d in split3(delta)], 128).astype(bf16)
+    wide = jnp.zeros((128 - 80, BLK), f32)
+    v_ref[block] = jnp.concatenate([vt_ref[block].astype(f32), wide], 0).T.astype(bf16)
+    dq_ref[block] = jnp.zeros(dq_ref.shape[1:], f32)
+    dk_ref[block] = jnp.zeros(dk_ref.shape[1:], f32)
+    dv_ref[block] = jnp.zeros(dv_ref.shape[1:], f32)
+
+
+def batch_back(pairs, masks, q_ref, k_ref, kt_ref, v_ref, do_ref, dq_ref, dk_ref, dv_ref):
+    weights = [jnp.exp2(mm(k_ref[column], q_ref[row])) for row, column in pairs]
+    for i, mask in enumerate(masks):
+        if mask is True:
+            weights[i] = jnp.where(causal(), weights[i], 0.0)
+        elif mask is not None:
+            weights[i] = weights[i] * mask
+    d_weights = [mm(v_ref[column], do_ref[row]) for row, column in pairs]
+    low_weights = [weight.astype(bf16) for weight in weights]
+    d_scores = [(weight * d_weight).astype(bf16) for weight, d_weight in zip(weights, d_weights)]
+    parts = [mm(do_ref[row, :HDIM], weight, NT) for (row, _), weight in zip(pairs, low_weights)]
+    for (_, column), part in zip(pairs, parts):
+        dv_ref[column] += part
+    parts = [mm(kt_ref[column], d_score) for (_, column), d_score in zip(pairs, d_scores)]
+    for (row, _), part in zip(pairs, parts):
+        dq_ref[row] += part
+    parts = [mm(q_ref[row, :80], d_score, NT) for (row, _), d_score in zip(pairs, d_scores)]
+    for (_, column), part in zip(pairs, parts):
+        dk_ref[column] += part
+
+
+def finish_back(count, block, carried, mine, raw_ref, logit_ref, gain_ref, dq_ref, dk_ref, dv_ref, draw_ref, dlogit_ref, cum_ref):
+    next_k, next_v, sum_q, sum_k = carried
+    place, lanes = place_of(block, count), lanes_of(block, count)
+    earlier = jnp.maximum(block - 1, 0)
+    place_before, lanes_before = place_of(earlier, count), lanes_of(earlier, count)
+    exists = jnp.where(block > 0, 1.0, 0.0)
+    q_raw, k_raw, v_raw = (raw_ref[place, i, :, lanes].astype(f32) for i in range(3))
+    k_step = shifted(k_raw, raw_ref[place_before, 1, :, lanes_before].astype(f32) * exists) - k_raw
+    v_step = shifted(v_raw, raw_ref[place_before, 2, :, lanes_before].astype(f32) * exists) - v_raw
+    rate_k = jax.nn.sigmoid(logit_ref[place, 1:2, lanes])
+    rate_v = jax.nn.sigmoid(logit_ref[place, 2:3, lanes])
+    dq, dk, dv = dq_ref[block], dk_ref[block], dv_ref[block]
+    dq_raw, part_q = norm_back(q_raw, gain_ref[:, 0:1], dq[:HDIM] * SCORE)
+    dk_mixed, part_k = norm_back(k_raw + rate_k * k_step, gain_ref[:, 1:2], dk[:HDIM] * LN2)
+    send_k, send_v = rate_k * dk_mixed, rate_v * dv
+    draw_ref[place, 0, :, lanes] = dq_raw.astype(bf16)
+    draw_ref[place, 1, :, lanes] = (dk_mixed - send_k + shifted_back(send_k, next_k)).astype(bf16)
+    draw_ref[place, 2, :, lanes] = (dv - send_v + shifted_back(send_v, next_v)).astype(bf16)
+    dlogit_ref[place, 1:2, lanes] = (1.0 - rate_k) * jnp.sum(k_step * send_k, 0, keepdims=True)
+    dlogit_ref[place, 2:3, lanes] = (1.0 - rate_v) * jnp.sum(v_step * send_v, 0, keepdims=True)
+    cum_ref[pl.ds(place, 1), lanes] = dq[HDIM : HDIM + 1] - dk[HDIM + 3 : HDIM + 4]
+    return send_k, send_v, sum_q + jnp.where(mine, part_q, 0.0), sum_k + part_k
+
+
+def forget_back(count, bias, logit_ref, cum_ref, dlogit_ref):
+    d_log = running_sum(cum_ref[...], count, True)
+    dlogit_ref[:, 0, :] = d_log * jax.nn.sigmoid(-(logit_ref[:, 0, :] + bias))
+    dlogit_ref[:, 3:, :] = jnp.zeros((count, 5, 2 * BLK), f32)
+
+
 def backward_kernel(count, device_ref, skip_ref, bias_ref, raw_ref, logit_ref, gain_ref, dmixed_ref, mixed_ref,
                     q_ref, k_ref, kt_ref, vt_ref, draw_ref, dlogit_ref, dgain_ref,
                     do_ref, v_ref, cum_ref, dq_ref, dk_ref, dv_ref, pairs_ref, own_ref):
@@ -289,87 +352,41 @@
     device = device_ref[0]
     blocks = 2 * count
     pair_steps, own_steps = list_pairs(skip_ref, pairs_ref, own_ref, device, slot, count, UNROLL_BACK)
-    gain_q, gain_k = gain_ref[:, 0:1], gain_ref[:, 1:2]
-    wide = jnp.zeros((128 - 80, BLK), f32)
+    sums = (dq_ref, dk_ref, dv_ref)
 
     def prepare(block, carried):
-        place, lanes = place_of(block, count), lanes_of(block, count)
-        d_out = dmixed_ref[place, :, lanes].astype(f32)
-        delta = jnp.sum(d_out * mixed_ref[block], 0, keepdims=True)
-        do_ref[block] = stack_rows(d_out, [-d for d in split3(delta)], 128).astype(bf16)
-        v_ref[block] = jnp.concatenate([vt_ref[block].astype(f32), wide], 0).T.astype(bf16)
-        dq_ref[block] = jnp.zeros(dq_ref.shape[1:], f32)
-        dk_ref[block] = jnp.zeros(dk_ref.shape[1:], f32)
-        dv_ref[block] = jnp.zeros(dv_ref.shape[1:], f32)
+        prepare_back(count, block, dmixed_ref, mixed_ref, vt_ref, do_ref, v_ref, *sums)
         return carried
 
     lax.fori_loop(0, blocks, prepare, 0)
     do_ref[blocks] = jnp.zeros(do_ref.shape[1:], bf16)
     dq_ref[blocks] = jnp.zeros(dq_ref.shape[1:], f32)
 
-    def together(pairs, diagonal):
-        scores = [mm(k_ref[column], q_ref[row]) for row, column in pairs]
-        weights = [jnp.exp2(score) for score in scores]
-        if diagonal:
-            weights = [jnp.where(causal(), weight, 0.0) for weight in weights]
-        d_weights = [mm(v_ref[column], do_ref[row]) for row, column in pairs]
-        low_weights = [weight.astype(bf16) for weight in weights]
-        d_scores = [(weight * d_weight).astype(bf16) for weight, d_weight in zip(weights, d_weights)]
-        parts = [mm(do_ref[row, :HDIM], weight, NT) for (row, _), weight in zip(pairs, low_weights)]
-        for (_, column), part in zip(pairs, parts):
-            dv_ref[column] += part
-        parts = [mm(kt_ref[column], d_score) for (_, column), d_score in zip(pairs, d_scores)]
-        for (row, _), part in zip(pairs, parts):
-            dq_ref[row] += part
-        parts = [mm(q_ref[row, :80], d_score, NT) for (row, _), d_score in zip(pairs, d_scores)]
-        for (_, column), part in zip(pairs, parts):
-            dk_ref[column] += part
-
     def own_rows(step, carried):
         rows = [own_ref[step * UNROLL_BACK + i] for i in range(UNROLL_BACK)]
-        together([(row, jnp.minimum(row, blocks - 1)) for row in rows], True)
+        pairs = [(row, jnp.minimum(row, blocks - 1)) for row in rows]
+        batch_back(pairs, [True] * UNROLL_BACK, q_ref, k_ref, kt_ref, v_ref, do_ref, *sums)
         return carried
 
     def kept_pairs(step, carried):
         codes = [pairs_ref[step * UNROLL_BACK + i] for i in range(UNROLL_BACK)]
-        together([(code >> 10, code & 1023) for code in codes], False)
+        pairs = [(code >> 10, code & 1023) for code in codes]
+        batch_back(pairs, [None] * UNROLL_BACK, q_ref, k_ref, kt_ref, v_ref, do_ref, *sums)
         return carried
 
     lax.fori_loop(0, own_steps, own_rows, 0)
     lax.fori_loop(0, pair_steps, kept_pairs, 0)
 
     def finish(step, carried):
-        next_k, next_v, sum_q, sum_k = carried
         block = blocks - 1 - step
-        place, lanes = place_of(block, count), lanes_of(block, count)
-        earlier = jnp.maximum(block - 1, 0)
-        place_before, lanes_before = place_of(earlier, count), lanes_of(earlier, count)
-        exists = jnp.where(block > 0, 1.0, 0.0)
-        q_raw, k_raw, v_raw = (raw_ref[place, i, :, lanes].astype(f32) for i in range(3))
-        k_step = shifted(k_raw, raw_ref[place_before, 1, :, lanes_before].astype(f32) * exists) - k_raw
-        v_step = shifted(v_raw, raw_ref[place_before, 2, :, lanes_before].astype(f32) * exists) - v_raw
-        rate_k = jax.nn.sigmoid(logit_ref[place, 1:2, lanes])
-        rate_v = jax.nn.sigmoid(logit_ref[place, 2:3, lanes])
-        dq, dk, dv = dq_ref[block], dk_ref[block], dv_ref[block]
-        dq_raw, part_q = norm_back(q_raw, gain_q, dq[:HDIM] * SCORE)
-        dk_mixed, part_k = norm_back(k_raw + rate_k * k_step, gain_k, dk[:HDIM] * LN2)
-        send_k, send_v = rate_k * dk_mixed, rate_v * dv
-        draw_ref[place, 0, :, lanes] = dq_raw.astype(bf16)
-        draw_ref[place, 1, :, lanes] = (dk_mixed - send_k + shifted_back(send_k, next_k)).astype(bf16)
-        draw_ref[place, 2, :, lanes] = (dv - send_v + shifted_back(send_v, next_v)).astype(bf16)
-        dlogit_ref[place, 1:2, lanes] = (1.0 - rate_k) * jnp.sum(k_step * send_k, 0, keepdims=True)
-        dlogit_ref[place, 2:3, lanes] = (1.0 - rate_v) * jnp.sum(v_step * send_v, 0, keepdims=True)
-        cum_ref[pl.ds(place, 1), lanes] = dq[HDIM : HDIM + 1] - dk[HDIM + 3 : HDIM + 4]
-        part_q = jnp.where(is_mine(device, slot, place, count), part_q, 0.0)
-        return send_k, send_v, sum_q + part_q, sum_k + part_k
+        mine = is_mine(device, slot, place_of(block, count), count)
+        return finish_back(count, block, carried, mine, raw_ref, logit_ref, gain_ref, *sums, draw_ref, dlogit_ref, cum_ref)
 
     zero = jnp.zeros((HDIM, BLK), f32)
     _, _, sum_q, sum_k = lax.fori_loop(0, blocks, finish, (zero, zero, zero, zero))
     dgain_ref[:, 0:1] = jnp.sum(sum_q, 1, keepdims=True)
     dgain_ref[:, 1:2] = jnp.sum(sum_k, 1, keepdims=True)
-    d_log = running_sum(cum_ref[...], count, True)
-    dlogit_ref[:, 0, :] = d_log * jax.nn.sigmoid(-(logit_ref[:, 0, :] + bias_ref[slot]))
-    dlogit_ref[:, 3:, :] = jnp.zeros((count, 5, 2 * BLK), f32)
+    forget_back(count, bias_ref[slot], logit_ref, cum_ref, dlogit_ref)
 
 
 def attend_backward(device, skip, bias, raw, logits, gains, dmixed, mixed, q, k, kt, vt):
@@ -828,20 +845,18 @@
     return me
 
 
-def orders(near, far, seq):
-    x, others = seq[0], seq[1:]
-    z = others[0]
-    rest = others[1:]
-    return [
+def orders(near, far, seq, busy):
+    x, z, rest = seq[0], seq[1], seq[2:]
+    kinds = [
         [near, far, x, z] + rest,
         [near, x, far, z] + rest,
         [near, z, x, far] + rest,
-        [near, far, z, x] + rest,
-        [near, x, z] + rest + [far],
-        [near, z, far] + rest + [x],
+        [near, z, far, x] + rest,
     ]
-
-
+    return [kinds[i] for i in (EARLY_KINDS if busy else (0, 1, 2, 0, 1, 3))]
+
+
+EARLY_KINDS = (0, 1, 2, 0, 1, 3)
 PARTS = 6
 
 
@@ -849,7 +864,8 @@
     def __init__(self, base, size, order, source, own, landing, result, send, recv, local):
         self.start, self.size, self.order, self.source, self.local = base, size, order, source, local
         self.own, self.landing, self.result, self.send, self.recv = own, landing, result, send, recv
-        self.at, self.stage, self.copy, self.load = base, 0, None, None
+        self.base, self.at, self.stage, self.copy, self.load = base, base, 0, None, None
+        self.off = 0
 
     def give(self):
         there, side = partner(self.order[self.stage])
@@ -858,11 +874,12 @@
         held = self.own
         if self.stage == 0 and self.source is not None:
             held = self.source
-            mine = pl.ds(self.keep, half)
-            self.load = pltpu.make_async_copy(self.source.at[mine], self.own.at[mine], self.local)
+            self.load = pltpu.make_async_copy(
+                self.source.at[pl.ds(self.keep, half)], self.own.at[pl.ds(self.base // 2, half)], self.local
+            )
             self.load.start()
         self.copy = pltpu.make_async_remote_copy(
-            src_ref=held.at[pl.ds(self.start + (1 - side) * half, half)],
+            src_ref=held.at[pl.ds(self.start + (1 - side) * half - self.off, half)],
             dst_ref=self.landing.at[pl.ds(self.at, half)],
             send_sem=self.send.at[self.stage], recv_sem=self.recv.at[self.stage],
             device_id=there, device_id_type=MESH,
@@ -874,22 +891,22 @@
         if self.load is not None:
             self.load.wait()
             self.load = None
+            self.off = self.keep - self.base // 2
         half = self.size // 2
         step = PIECE if half % PIECE == 0 else 1
-        keep, at, own, landing = self.keep, self.at, self.own, self.landing
+        keep, at, own, landing = self.keep - self.off, self.at, self.own, self.landing
 
         def piece(i, carried):
             mine = pl.ds(keep + i * step, step)
-            theirs = landing[pl.ds(at + i * step, step)].astype(f32)
-            own[mine] = (own[mine].astype(f32) + theirs).astype(bf16)
+            own[mine] = own[mine] + landing[pl.ds(at + i * step, step)]
             return carried
 
         lax.fori_loop(0, half // step, piece, 0)
-        self.start, self.size, self.at, self.stage = keep, half, at + half, self.stage + 1
+        self.start, self.size, self.at, self.stage = self.keep, half, at + half, self.stage + 1
 
     def settle(self):
         copy = pltpu.make_async_copy(
-            self.own.at[pl.ds(self.start, self.size)], self.result.at[pl.ds(self.start, self.size)], self.local
+            self.own.at[pl.ds(self.start - self.off, self.size)], self.result.at[pl.ds(self.start, self.size)], self.local
         )
         copy.start()
         copy.wait()
@@ -929,7 +946,7 @@
 
 def sums_of(units, least, sets, source, own, landing, result, send, recv, local):
     pieces, base, sums = units // least, 0, []
-    for i, order in enumerate(orders(*sets)):
+    for i, order in enumerate(orders(*sets, source is not None)):
         size = least * ((pieces + PARTS - 1 - i) // PARTS)
         if not size:
             break
@@ -953,16 +970,84 @@
                 part.spread()
 
 
+def put_together(holders, part_ref, logit_ref, proj_ref, dsmall_ref):
+    for head, held in enumerate(holders):
+        for i in range(2):
+            start = D * (1 + i) + head * HDIM
+            if len(held) == 1:
+                proj_ref[start : start + HDIM] = part_ref[head, 0, i]
+            else:
+                proj_ref[start : start + HDIM] = total([part_ref[head, j, i].astype(f32) for j in range(len(held))]).astype(bf16)
+        dsmall_ref[8 * head : 8 * head + 8] = total([logit_ref[d, s] for d, s in held])
+
+
+def late_weights(h_ref, proj_ref, g_ref):
+    def block(i, carried):
+        grads = proj_ref[pl.ds(pl.multiple_of(i * 256, 256), 256)]
+        for j in range(3):
+            part = lax.dot_general(h_ref[:, 256 * j : 256 * j + 256], grads, (((0,), (1,)), ((), ())), preferred_element_type=f32)
+            g_ref[pl.ds(i * (D // UNIT) + j * 16, 16)] = part.astype(bf16).reshape(16, UNIT, 256)
+        return carried
+
+    lax.fori_loop(0, 9, block, 0)
+
+
+def late_rest(h_ref, proj_ref, w_ref, wsmall_ref, x_ref, gain_ref, dresid_ref, extra_ref, dsmall_ref, rows_ref, dx_ref, g_ref, gsum_ref=None):
+    low_small = dsmall_ref[...].astype(bf16)
+    for i in range(3):
+        cols = slice(256 * i, 256 * i + 256)
+        part = mm(w_ref[cols, :], proj_ref[...]) + mm(wsmall_ref[cols, :], low_small)
+        dx_ref[:, cols] = part.T
+    small = mm(low_small, h_ref[...])
+    for head in range(HEADS):
+        rows_ref[3 * head : 3 * head + 3] = small[8 * head : 8 * head + 3]
+    rows_ref[3 * HEADS :] = extra_ref[...]
+    if gsum_ref is not None:
+        rows_ref[3 * HEADS + 2 : 3 * HEADS + 4] = gsum_ref[0:2]
+    gain = gain_ref[...]
+    dgain = jnp.zeros((1, D), f32)
+    for i in range(h_ref.shape[0] // 128):
+        here = slice(128 * i, 128 * i + 128)
+        v, u = x_ref[here].astype(f32), dx_ref[here]
+        scale = lax.rsqrt(jnp.mean(v * v, 1, keepdims=True) + EPS)
+        hat, gu = v * scale, u * gain
+        dx_ref[here] = dresid_ref[here] + scale * (gu - hat * jnp.mean(hat * gu, 1, keepdims=True))
+        dgain = dgain + jnp.sum(hat * u, 0, keepdims=True)
+    rows_ref[3 * HEADS : 3 * HEADS + 1] = dgain
+    bias_rows = jnp.concatenate([dsmall_ref[8 * head : 8 * head + 1] for head in range(HEADS)], 0)
+    bias_sum = jnp.sum(bias_rows, 1, keepdims=True)
+    lane = lax.broadcasted_iota(jnp.int32, (HEADS, 128), 1)
+    row = lax.broadcasted_iota(jnp.int32, (HEADS, 128), 0)
+    rows_ref[3 * HEADS + 4 : 3 * HEADS + 5, 0:128] = jnp.sum(jnp.where(lane == row, bias_sum, 0.0), 0, keepdims=True)
+
+    used = 9 * (D // UNIT)
+    units = g_ref.shape[0]
+    for i in range(3):
+        g_ref[used + 3 * i : used + 3 * i + 3] = rows_ref[:, 256 * i : 256 * i + 256].astype(bf16).reshape(3, UNIT, 256)
+    if units > used + 9:
+        g_ref[used + 9 :] = jnp.zeros((units - used - 9, UNIT, 256), bf16)
+
+
+def give_late(sums, rest, early, stages):
+    units = 9 * (D // UNIT)
+    ahead = [part for part in sums if part.start + part.size <= units]
+    for part in ahead:
+        part.give()
+    rest()
+    for part in sums[len(ahead):]:
+        part.give()
+    step(early, stages)
+
+
 def last_kernel(count, sets, draw_ref, dlogit_ref, early_ref, h_ref, dgate_ref, w_ref, wsmall_ref, x_ref, gain_ref,
                 dresid_ref, extra_ref, late_out, early_out, dx_ref,
-                proj_ref, logit_ref, part_ref, dsmall_ref, rows_ref, dn_ref, g_ref, land_ref, e_ref, eland_ref,
+                proj_ref, logit_ref, part_ref, dsmall_ref, rows_ref, g_ref, land_ref, e_ref, eland_ref,
                 send, recv, recv_q, recv_kv, local, gsend, grecv, gsem, esend, erecv, esem):
     near, far, seq = sets
     bits = [near, far] + seq
     stages, least = len(bits), 1 << len(bits)
     me = greet_all(bits, count)
-    rows = h_ref.shape[0]
-    early = sums_of(e_ref.shape[0], least, sets, early_ref, e_ref, eland_ref, early_out, esend, erecv, esem)
+    early = sums_of(early_ref.shape[0], least, sets, early_ref, e_ref, eland_ref, early_out, esend, erecv, esem)
     for part in early:
         part.give()
 
@@ -1003,59 +1088,16 @@
             copy = push(draw_ref.at[0, pl.ds(1, 2), 0], part_ref.at[head, j], send.at[0, 0], recv_kv.at[head, j], lax.rem(me + 1, count))
             pl.when(me != d)(copy.wait_recv)
 
-    for head, held in enumerate(holders):
-        for i in range(2):
-            start = D * (1 + i) + head * HDIM
-            if len(held) == 1:
-                proj_ref[start : start + HDIM] = part_ref[head, 0, i]
-            else:
-                proj_ref[start : start + HDIM] = total([part_ref[head, j, i].astype(f32) for j in range(len(held))]).astype(bf16)
-        dsmall_ref[8 * head : 8 * head + 8] = total([logit_ref[d, s] for d, s in held])
+    put_together(holders, part_ref, logit_ref, proj_ref, dsmall_ref)
     proj_ref[3 * D :] = dgate_ref[...]
 
-    def block(i, carried):
-        grads = proj_ref[pl.ds(pl.multiple_of(i * 256, 256), 256)]
-        for j in range(3):
-            part = lax.dot_general(h_ref[:, 256 * j : 256 * j + 256], grads, (((0,), (1,)), ((), ())), preferred_element_type=f32)
-            g_ref[pl.ds(i * (D // UNIT) + j * 16, 16)] = part.astype(bf16).reshape(16, UNIT, 256)
-        return carried
-
-    lax.fori_loop(0, 9, block, 0)
-    low_small = dsmall_ref[...].astype(bf16)
-    for i in range(3):
-        cols = slice(256 * i, 256 * i + 256)
-        part = mm(w_ref[cols, :], proj_ref[...]) + mm(wsmall_ref[cols, :], low_small)
-        dn_ref[:, cols] = part.T
-    small = mm(low_small, h_ref[...])
-    for head in range(HEADS):
-        rows_ref[3 * head : 3 * head + 3] = small[8 * head : 8 * head + 3]
-    rows_ref[3 * HEADS :] = extra_ref[...]
-    gain = gain_ref[...]
-    dgain = jnp.zeros((1, D), f32)
-    for i in range(rows // 128):
-        here = slice(128 * i, 128 * i + 128)
-        v, u = x_ref[here].astype(f32), dn_ref[here]
-        scale = lax.rsqrt(jnp.mean(v * v, 1, keepdims=True) + EPS)
-        hat, gu = v * scale, u * gain
-        dx_ref[here] = dresid_ref[here] + scale * (gu - hat * jnp.mean(hat * gu, 1, keepdims=True))
-        dgain = dgain + jnp.sum(hat * u, 0, keepdims=True)
-    rows_ref[3 * HEADS : 3 * HEADS + 1] = dgain
-    bias_rows = jnp.concatenate([dsmall_ref[8 * head : 8 * head + 1] for head in range(HEADS)], 0)
-    bias_sum = jnp.sum(bias_rows, 1, keepdims=True)
-    lane = lax.broadcasted_iota(jnp.int32, (HEADS, 128), 1)
-    row = lax.broadcasted_iota(jnp.int32, (HEADS, 128), 0)
-    rows_ref[3 * HEADS + 4 : 3 * HEADS + 5, 0:128] = jnp.sum(jnp.where(lane == row, bias_sum, 0.0), 0, keepdims=True)
-
-    used = 9 * (D // UNIT)
-    units = g_ref.shape[0]
-    for i in range(3):
-        g_ref[used + 3 * i : used + 3 * i + 3] = rows_ref[:, 256 * i : 256 * i + 256].astype(bf16).reshape(3, UNIT, 256)
-    if units > used + 9:
-        g_ref[used + 9 :] = jnp.zeros((units - used - 9, UNIT, 256), bf16)
-    late = sums_of(units, least, sets, None, g_ref, land_ref, late_out, gsend, grecv, gsem)
-    for part in late:
-        part.give()
-    step(early, stages)
+    late_weights(h_ref, proj_ref, g_ref)
+    late = sums_of(g_ref.shape[0], least, sets, None, g_ref, land_ref, late_out, gsend, grecv, gsem)
+
+    def rest():
+        late_rest(h_ref, proj_ref, w_ref, wsmall_ref, x_ref, gain_ref, dresid_ref, extra_ref, dsmall_ref, rows_ref, dx_ref, g_ref)
+
+    give_late(late, rest, early, stages)
     early_left = 2 * stages - 3
     for stage in range(2 * stages):
         step(late, stages)
@@ -1086,10 +1128,9 @@
             pltpu.VMEM((HEADS, most, 2, HDIM, rows), bf16),
             pltpu.VMEM((8 * HEADS, rows), f32),
             pltpu.VMEM((SMALL, D), f32),
-            pltpu.VMEM((rows, D), f32),
             pltpu.VMEM((units,) + shape, bf16),
             pltpu.VMEM((units,) + shape, bf16),
-            pltpu.VMEM(early.shape, bf16),
+            pltpu.VMEM((early.shape[0] // 2,) + shape, bf16),
             pltpu.VMEM(early.shape, bf16),
             dma((count, 5)), dma((count,)), dma((HEADS,)), dma((HEADS, most)), dma((5,)),
             dma((PARTS, 2 * stages)), dma((PARTS, 2 * stages)), dma((PARTS,)),
@@ -1129,6 +1170,205 @@
         compiler_params=pltpu.CompilerParams(vmem_limit_bytes=32 * 2**20),
         name="unpack",
     )(*[units for units, _, _ in parts])
+
+
+def back_kernel(count, sets, skip_ref, bias_ref, dmixed_ref, logits_ref, gains_ref, wsmall_ref, gain_ref, extra_ref,
+                raw_in, full_in, q_in, k_in, kt_in, vt_in, early_ref, h_in, dgate_in, w_in, x_in, dresid_in,
+                late_out, early_out, dx_ref,
+                raw_ref, full_ref, q_ref, k_ref, kt_ref, vt_ref, do_ref, v_ref, cum_ref, dq_ref, dk_ref, dv_ref,
+                draw_ref, dlogit_ref, gsum_ref,
+                proj_ref, logit_ref, part_ref, dsmall_ref, rows_ref, h_ref, w_ref, x_ref, dresid_ref,
+                g_ref, land_ref, e_ref, eland_ref,
+                load, send, recv, recv_q, recv_kv, own, gsend, grecv, gsem, esend, erecv, esem):
+    near, far, seq = sets
+    bits = [near, far] + seq
+    stages, least = len(bits), 1 << len(bits)
+    blocks = 2 * count
+    sums = (dq_ref, dk_ref, dv_ref)
+
+    def state(slot):
+        pairs = ((full_in, full_ref), (q_in, q_ref), (k_in, k_ref), (kt_in, kt_ref), (vt_in, vt_ref))
+        return [pltpu.make_async_copy(src.at[slot], dst, load.at[i]) for i, (src, dst) in enumerate(pairs)]
+
+    other = [
+        pltpu.make_async_copy(src, dst, load.at[5 + i])
+        for i, (src, dst) in enumerate((
+            (raw_in, raw_ref), (h_in, h_ref), (dgate_in, proj_ref.at[pl.ds(3 * D, D)]), (w_in, w_ref), (x_in, x_ref), (dresid_in, dresid_ref)))
+    ]
+    for copy in state(0) + other:
+        copy.start()
+    me = greet_all(bits, count)
+    first = first_head(me, count)
+    holders = held_heads(count)
+    early = sums_of(early_ref.shape[0], least, sets, early_ref, e_ref, eland_ref, early_out, esend, erecv, esem)
+    for part in early:
+        part.give()
+    gsum_ref[...] = jnp.zeros(gsum_ref.shape, f32)
+
+    def sends(slot, k):
+        peer = lax.rem(me + k, count)
+        head = first + slot
+        order = me - holder(head, 0, count)
+        used = (head * count < HEADS * (me + 1)) & (head * count + count > HEADS * me)
+        target = proj_ref.at[pl.ds(pl.multiple_of(head * HDIM, HDIM), HDIM)]
+        items = [
+            (None, dlogit_ref.at[peer, slot], logit_ref.at[me, slot], recv.at[k, slot]),
+            (is_mine(me, slot, peer, count), draw_ref.at[peer, 0, slot], target, recv_q.at[head]),
+            (used, draw_ref.at[peer, pl.ds(1, 2), slot], part_ref.at[head, order], recv_kv.at[head, order]),
+        ]
+        return [
+            (mine, push(src, dst, send.at[k, slot, i], sem, peer) if k else pltpu.make_async_copy(src, dst, own.at[slot, i]))
+            for i, (mine, src, dst, sem) in enumerate(items)
+        ]
+
+    for slot in range(2):
+        for copy in state(slot):
+            copy.wait()
+
+        def prepare(block, carried):
+            prepare_back(count, block, dmixed_ref.at[:, slot], full_ref, vt_ref, do_ref, v_ref, *sums)
+            return carried
+
+        lax.fori_loop(0, blocks, prepare, 0)
+        step(early, stages)
+
+        def one_place(place, carried):
+            for i in range(blocks // UNROLL_BACK):
+                pairs = pairs_of_place(place, i, UNROLL_BACK, count)
+                masks = [keep_factor(skip_ref, row, column) for row, column in pairs]
+                if (i + 1) * UNROLL_BACK == blocks:
+                    pairs.append((place, place))
+                    masks[-1:] = [True, True]
+                batch_back(pairs, masks, q_ref, k_ref, kt_ref, v_ref, do_ref, *sums)
+            return carried
+
+        low, high = own_places(me, slot, count)
+        middle = (low + high) // 2
+        if slot == 0:
+            lax.fori_loop(low, high, one_place, 0)
+        else:
+            lax.fori_loop(low, middle, one_place, 0)
+            step(early, stages)
+            lax.fori_loop(middle, high, one_place, 0)
+        step(early, stages)
+        if slot == 0:
+            for copy in state(1):
+                copy.start()
+            other[0].wait()
+        raws, logits, gains = raw_ref.at[:, :, slot], logits_ref.at[:, slot], gains_ref.at[slot]
+        draws, dlogits = draw_ref.at[:, :, slot], dlogit_ref.at[:, slot]
+
+        def finish(number, carried):
+            block = blocks - 1 - number
+            mine = is_mine(me, slot, place_of(block, count), count)
+            return finish_back(count, block, carried, mine, raws, logits, gains, *sums, draws, dlogits, cum_ref)
+
+        zero = jnp.zeros((HDIM, BLK), f32)
+        _, _, sum_q, sum_k = lax.fori_loop(0, blocks, finish, (zero, zero, zero, zero))
+        lane = lax.broadcasted_iota(jnp.int32, (HDIM, D), 1)
+        channel = lax.broadcasted_iota(jnp.int32, (HDIM, D), 0)
+        here = lane == channel + (first + slot) * HDIM
+        for i, column in enumerate((sum_q, sum_k)):
+            placed = jnp.where(here, jnp.sum(column, 1, keepdims=True), 0.0)
+            gsum_ref[i : i + 1] += jnp.sum(placed, 0, keepdims=True)
+        forget_back(count, bias_ref[slot], logits, cum_ref, dlogits)
+        for k in far_first(count) + [0]:
+            for mine, copy in sends(slot, k):
+                if mine is None:
+                    copy.start()
+                else:
+                    pl.when(mine)(copy.start)
+        step(early, stages)
+
+    for _ in range(LATER):
+        step(early, stages)
+    for copy in other[1:]:
+        copy.wait()
+    for slot in range(2):
+        for k in far_first(count) + [0]:
+            for mine, copy in sends(slot, k):
+                if mine is None:
+                    copy.wait()
+                else:
+                    pl.when(mine)(copy.wait_send if k else copy.wait)
+    for head in range(HEADS):
+        source = holder(head, me, count)
+        next_one = lax.rem(me + 1, count)
+        copy = push(draw_ref.at[0, 0, 0], proj_ref.at[pl.ds(head * HDIM, HDIM)], send.at[0, 0, 0], recv_q.at[head], next_one)
+        pl.when(source != me)(copy.wait_recv)
+        for j, (d, s) in enumerate(holders[head]):
+            copy = push(draw_ref.at[0, pl.ds(1, 2), 0], part_ref.at[head, j], send.at[0, 0, 0], recv_kv.at[head, j], next_one)
+            pl.when(me != d)(copy.wait_recv)
+
+    put_together(holders, part_ref, logit_ref, proj_ref, dsmall_ref)
+    late_weights(h_ref, proj_ref, g_ref)
+    late = sums_of(g_ref.shape[0], least, sets, None, g_ref, land_ref, late_out, gsend, grecv, gsem)
+
+    def rest():
+        late_rest(h_ref, proj_ref, w_ref, wsmall_ref, x_ref, gain_ref, dresid_ref, extra_ref, dsmall_ref, rows_ref, dx_ref, g_ref, gsum_ref)
+
+    give_late(late, rest, early, stages)
+    early_left = 2 * stages - 8 - LATER
+    for stage in range(2 * stages):
+        step(late, stages)
+        if stage < early_left:
+            step(early, stages)
+
+
+LATER = 1
+
+
+def back(count, sets, skip, bias, d_mixed, logits, gains, w_small, gain, extra, raw, full, q, k, kt, vt, early, h, d_gate, w_attn, x, d_resid):
+    stages = 2 + len(sets[2])
+    units = padded(9 * (D // UNIT) + 9, 1 << stages)
+    rows = h.shape[0]
+    blocks = 2 * count
+    most = max(len(held) for held in held_heads(count))
+    vmem = pl.BlockSpec(memory_space=pltpu.VMEM)
+    smem = pl.BlockSpec(memory_space=pltpu.SMEM)
+    dma = pltpu.SemaphoreType.DMA
+    shape = (UNIT, 256)
+    held = lambda array: pltpu.VMEM(array.shape[1:], array.dtype)
+    return pl.pallas_call(
+        functools.partial(back_kernel, count, sets),
+        out_shape=[
+            jax.ShapeDtypeStruct((units,) + shape, bf16),
+            jax.ShapeDtypeStruct(early.shape, bf16),
+            jax.ShapeDtypeStruct((rows, D), f32),
+        ],
+        in_specs=[smem, smem] + [vmem] * 6 + [ANY] * 12,
+        out_specs=[ANY, ANY, vmem],
+        scratch_shapes=[
+            pltpu.VMEM(raw.shape, bf16), held(full), held(q), held(k), held(kt), held(vt),
+            pltpu.VMEM((blocks + 1, 128, BLK), bf16),
+            pltpu.VMEM((blocks, BLK, 128), bf16),
+            pltpu.VMEM((count, rows), f32),
+            pltpu.VMEM((blocks + 1, 80, BLK), f32),
+            pltpu.VMEM((blocks, 80, BLK), f32),
+            pltpu.VMEM((blocks, HDIM, BLK), f32),
+            pltpu.VMEM(raw.shape, bf16),
+            pltpu.VMEM(logits.shape, f32),
+            pltpu.VMEM((8, D), f32),
+            pltpu.VMEM((4 * D, rows), bf16),
+            pltpu.VMEM((count, 2, 8, rows), f32),
+            pltpu.VMEM((HEADS, most, 2, HDIM, rows), bf16),
+            pltpu.VMEM((8 * HEADS, rows), f32),
+            pltpu.VMEM((SMALL, D), f32),
+            pltpu.VMEM(h.shape, bf16),
+            pltpu.VMEM(w_attn.shape, bf16),
+            pltpu.VMEM(x.shape, bf16),
+            pltpu.VMEM(d_resid.shape, f32),
+            pltpu.VMEM((units,) + shape, bf16),
+            pltpu.VMEM((units,) + shape, bf16),
+            pltpu.VMEM((early.shape[0] // 2,) + shape, bf16),
+            pltpu.VMEM(early.shape, bf16),
+            dma((11,)), dma((count, 2, 3)), dma((count, 2)), dma((HEADS,)), dma((HEADS, most)), dma((2, 3)),
+            dma((PARTS, 2 * stages)), dma((PARTS, 2 * stages)), dma((PARTS,)),
+            dma((PARTS, 2 * stages)), dma((PARTS, 2 * stages)), dma((PARTS,)),
+        ],
+        compiler_params=pltpu.CompilerParams(collective_id=4, has_side_effects=True, vmem_limit_bytes=63 * 2**20),
+        name="back",
+    )(skip, bias, d_mixed, logits, gains, w_small, gain, extra, raw, full, q, k, kt, vt, early, h, d_gate, w_attn, x, d_resid)
 
 
 def rms_scale(values, gains):
@@ -1195,14 +1435,20 @@
     d_mixed_all, early = grads_out(
         count, units, d_mixed, h_first, d_gate_logit, h_second, d_gate_low, hidden_low, d_low, gated, d_branch
     )
-    d_raw, d_logits, d_gains = attend_backward(device, skip, bias, raw, logits, gains, d_mixed_all, mixed, q, k, kt, vt)
-
-    placed = jnp.zeros((HEADS, HDIM, 2), f32)
-    placed = lax.dynamic_update_slice(placed, d_gains, (head, 0, 0)).reshape(D, 2).T
-    extra = jnp.concatenate([jnp.zeros((1, D), f32), grad_gain_ffn[None], placed, jnp.zeros((SMALL - 3 * HEADS - 4, D), f32)], 0)
-    late, early, d_inputs = last(
-        count, sets, d_raw, d_logits, early, h_first, d_gate_logit, w_attn, w_small, tokens[0], gain_attn[None], d_resid, extra
-    )
+    zeros = lambda n: jnp.zeros((n, D), f32)
+    if count <= 8:
+        extra = jnp.concatenate([zeros(1), grad_gain_ffn[None], zeros(SMALL - 3 * HEADS - 2)], 0)
+        late, early, d_inputs = back(
+            count, sets, skip, bias, d_mixed_all, logits, gains, w_small, gain_attn[None], extra,
+            raw, mixed, q, k, kt, vt, early, h_first, d_gate_logit, w_attn, tokens[0], d_resid,
+        )
+    else:
+        d_raw, d_logits, d_gains = attend_backward(device, skip, bias, raw, logits, gains, d_mixed_all, mixed, q, k, kt, vt)
+        placed = lax.dynamic_update_slice(jnp.zeros((HEADS, HDIM, 2), f32), d_gains, (head, 0, 0)).reshape(D, 2).T
+        extra = jnp.concatenate([zeros(1), grad_gain_ffn[None], placed, zeros(SMALL - 3 * HEADS - 4)], 0)
+        late, early, d_inputs = last(
+            count, sets, d_raw, d_logits, early, h_first, d_gate_logit, w_attn, w_small, tokens[0], gain_attn[None], d_resid, extra
+        )
     row = 3 * HEADS
     used = 9 * (D // UNIT)
     small = late[used : used + 9].reshape(3, SMALL, 256).transpose(1, 0, 2).reshape(SMALL, D).astype(f32)

time: 461 us -> 436 us (0.946)
  Pallas kernels: 403 us -> 378 us
    pallas_call x2 -> x1, Pallas kernels: 251 us -> 227 us  [back(): pl.pallas_call(functools.partial(back_kernel, count, sets), out_shape=[ja...]
    unnamed x39 -> x37, local copies, waits for them, and re-layouts: 11.5 us -> 11.9 us
where the time goes in v5:
time: 436 us
  Pallas kernels  378 us (87%)
  matrix products  24.2 us (6%)
  local copies, waits for them, and re-layouts  22.8 us (5%)
  other arithmetic  9.57 us (2%)
    pallas_call x1, Pallas kernels, back(): pl.pallas_call(functools.partial(back_kernel, count, sets), out_shape=[ja...  227 us
    pallas_call x1, Pallas kernels, front(): pl.pallas_call(functools.partial(front_kernel, count), out_shape=[jax.Sha...  110 us
    dot_general x6, matrix products, dot(): lax.dot_general(a, b, (((i,), (j,)), ((), ())), preferred_element_type=f32)  24.2 us
    pallas_call x1, Pallas kernels, grads_out(): pl.pallas_call(functools.partial(grads_out_kernel, count), out_shape=[jax...  23.1 us
    pallas_call x4, Pallas kernels, unpack(): pl.pallas_call(functools.partial(unpack_kernel, [blocks for _, _, blocks...  18.3 us
    unnamed x37, local copies, waits for them, and re-layouts  11.9 us

profile of v5, /device:TPU:0, one launch (start us, length us, event | category | flops | bytes accessed | tf_op | source)
XLA Modules:
  0.0 435.8 jit_solution(11349564182910203306)
XLA Ops:
  0.7 1.2 dynamic_slice.6.bias_ref
  2.0 1.3 broadcast_in_dim.20.gain_ref
  5.0 1.0 stack_reshape.8
  6.0 1.0 stack_reshape.9
  7.7 109.9 %front.1 = (bf16[512,768]{1,0:T(8,128)(2,1)}, f32[768,512]{1,0:T(8,128)}, bf16[768,512]{1,0:T(8,128)(2,1)}, bf16[8,3,2,64,512]{4,3,2,1,0:T(8,128)(2,1)}, f32[8,2...) custom-call(s32[16,16]{1,0:T(8,128)} %bitcast.63, ...), custom_call_target="tpu_custom_call" | custom-call | tf_op jit(solution)/shard_map/front/pallas_call | solution.py:796
  117.6 2.2 fusion.3.gated_ref
  119.9 2.5 multiply_reduce_fusion.2
  122.7 3.4 fusion.19
  126.1 5.6 %fusion.10 = (f32[512,2048]{1,0:T(8,128)}, f32[512,2048]{1,0:T(8,128)}, bf16[512,2048]{1,0:T(8,128)(2,1)}) fusion(f32[512,4096]{1,0:T(8,128)S(1)} %fusion.19, bf16[2048,768]{1,0:T(8,128)(2,1)S(1)} %copy-done.13, bf16[1,512,768]{2,1,0:T(8,128)(2,1)S(1)} %copy-done.5), kind=kOutput, calls=%fused_computation.25 | convolution fusion | flops 1625292800 | bytes 22806528 | tf_op jit(solution)/shard_map/dot_general | solution.py:622
  131.7 4.1 add_convert_fusion.dgu_ref
  135.8 6.7 %fusion.9 = bf16[1,512,768]{2,1,0:T(8,128)(2,1)} fusion(f32[512,768]{1,0:T(8,128)S(1)} %get-tuple-element.58, bf16[512,2048]{1,0:T(8,128)(2,1)} %get-tuple-element.48.hidden_ref, bf16[2048,768]{1,0:T(8,128)(2,1)} %param.25), kind=kOutput, calls=%fused_computation.24 | convolution fusion | flops 1611399168 | bytes 7602176 | tf_op jit(solution)/shard_map/dot_general | solution.py:622
  142.5 3.6 multiply_reduce_fusion
  146.2 1.6 fusion.15
  148.7 2.3 fusion.6
  151.7 23.1 %grads_out.1 = (bf16[8,2,64,512]{3,2,1,0:T(8,128)(2,1)}, bf16[1440,16,256]{2,1,0:T(8,128)(2,1)}) custom-call(bf16[12,64,512]{2,1,0:T(8,128)(2,1)} %bitcast.58, bf16[512,768]{1,0:T(8,128)(2,1)} %get-tuple-element.29.h1_ref.h_in, bf16[768,512]{1,0:T(8,128)(2,1)} %get-tuple-element.49.dgate_ref.dgate_in, bf16[512,768]{1,0:T(8,128)(2,1)} %copy-done.4, ...), custom_call_target="tpu_custom_call" | custom-call | tf_op jit(solution)/shard_map/grads_out/pallas_call | solution.py:607
  174.8 227.0 %back.1 = (bf16[448,16,256]{2,1,0:T(8,128)(2,1)}, bf16[1440,16,256]{2,1,0:T(8,128)(2,1)}, f32[512,768]{1,0:T(8,128)}) custom-call(s32[16,16]{1,0:T(8,128)} %bitcast.64, f32[2]{0:T(128)} %dynamic_slice.6.bias_ref, bf16[8,2,64,512]{3,2,1,0:T(8,128)(2,1)} %get-tuple-element.30.dmixed_ref, f32[8,2,8,512]{3,2,1,0:T(8,128)} %get-tuple-element.31.logits_ref, ...), custom_call_target="tpu_custom_call" | custom-call | tf_op jit(solution)/shard_map/back/pallas_call | solution.py:1332
  406.6 4.3 copy-done
  411.0 1.9 unpack.5
  412.8 3.3 copy-done.1
  416.2 2.0 copy-done.2
  418.2 5.9 %unpack.4 = f32[768,3072]{1,0:T(8,128)} custom-call(bf16[448,16,256]{2,1,0:T(8,128)(2,1)S(1)} %copy-done.2, bf16[1440,16,256]{2,1,0:T(8,128)(2,1)S(1)} %copy-done.1), custom_call_target="tpu_custom_call" | custom-call | tf_op jit(solution)/shard_map/unpack/pallas_call | solution.py:1164
  424.1 2.9 unpack.7
  427.0 7.7 %unpack.6 = f32[768,4096]{1,0:T(8,128)} custom-call(bf16[1440,16,256]{2,1,0:T(8,128)(2,1)S(1)} %copy-done.1), custom_call_target="tpu_custom_call" | custom-call | tf_op jit(solution)/shard_map/unpack/pallas_call | solution.py:1164
  434.7 1.1 copy.66
  (59 shorter events, 9.2 us)
Async XLA Ops:
  7.7 112.2 %copy-start.8 = (bf16[1,512,768]{2,1,0:T(8,128)(2,1)S(1)}, bf16[1,512,768]{2,1,0:T(8,128)(2,1)}, u32[]{:S(2)}) copy-start(bf16[1,512,768]{2,1,0:T(8,128)(2,1)} %param.13) | copy-start | bytes 2359300
  7.7 114.9 %slice-start = ((s8[6291456]{0:T(1024)(128)(4,1)}), s8[2097152]{0:T(1024)(128)(4,1)S(1)}, s32[]{:S(2)}) async-start(s8[6291456]{0:T(1024)(128)(4,1)} %bitcast.49), calls=%async_computation | async-start | bytes 4194304
  117.6 5.0 %slice-start.1 = ((s8[6291456]{0:T(1024)(128)(4,1)}), s8[4194304]{0:T(1024)(128)(4,1)S(1)}, s32[]{:S(2)}) async-start(s8[6291456]{0:T(1024)(128)(4,1)} %bitcast.49), calls=%async_computation.1 | async-start | bytes 8388608
  119.9 2.5 copy-start.7
  119.9 2.5 copy-start.12
  122.6 3.5 copy-start.4
  122.6 3.5 copy-start.5
  122.6 3.5 copy-start.13
  135.8 6.7 %copy-start.3 = (bf16[512,4096]{1,0:T(8,128)(2,1)}, bf16[512,4096]{1,0:T(8,128)(2,1)S(1)}, u32[]{:S(2)}) copy-start(bf16[512,4096]{1,0:T(8,128)(2,1)S(1)} %add_convert_fusion.dgu_ref) | copy-start | bytes 12582916
  146.2 1.6 copy-start.10
  146.2 2.1 copy-start.11
  146.2 2.5 copy-start.14
  147.8 3.2 copy-start.6
  406.6 4.4 copy-start
  411.0 5.2 %copy-start.1 = (bf16[1440,16,256]{2,1,0:T(8,128)(2,1)S(1)}, bf16[1440,16,256]{2,1,0:T(8,128)(2,1)}, u32[]{:S(2)}) copy-start(bf16[1440,16,256]{2,1,0:T(8,128)(2,1)} %get-tuple-element.41.refs_1_.refs_0_) | copy-start | bytes 35389444
  416.2 2.0 copy-start.2
  427.0 7.7 %copy-start.9 = (f32[512,768]{1,0:T(8,128)S(1)}, f32[512,768]{1,0:T(8,128)}, u32[]{:S(2)}) copy-start(f32[512,768]{1,0:T(8,128)} %get-tuple-element.39) | copy-start | bytes 4718596

commit v6 on v5

--- a/solution.py
+++ b/solution.py
@@ -127,12 +127,12 @@
     cum = cum_ref[pl.ds(place, 1), lanes]
     parts = split3(cum)
     one = jnp.ones_like(cum)
-    query = q_raw * lax.rsqrt(jnp.mean(q_raw * q_raw, 0, keepdims=True) + EPS) * (gain_ref[:, 0:1] * (SCORE * LOG2E))
+    query = q_raw * lax.rsqrt(jnp.mean(q_raw * q_raw, 0, keepdims=True) + EPS) * (gain_ref[:, 1:2] * (SCORE * LOG2E))
     q_ref[block] = stack_rows(query, (*parts, one, one, one), 128).astype(bf16)
     rate_k = jax.nn.sigmoid(logit_ref[place, 1:2, lanes])
     rate_v = jax.nn.sigmoid(logit_ref[place, 2:3, lanes])
     key = k_raw + rate_k * (shifted(k_raw, carried[0]) - k_raw)
-    key = key * lax.rsqrt(jnp.mean(key * key, 0, keepdims=True) + EPS) * gain_ref[:, 1:2]
+    key = key * lax.rsqrt(jnp.mean(key * key, 0, keepdims=True) + EPS) * gain_ref[:, 2:3]
     value = v_raw + rate_v * (shifted(v_raw, carried[1]) - v_raw)
     k_ref[block] = stack_rows(key, (one, one, one, *(-c for c in parts)), 128).T.astype(bf16)
     kt_ref[block] = stack_rows(key, (one,), 80).astype(bf16)
@@ -245,7 +245,7 @@
             in_specs=[
                 pl.BlockSpec((count, 3, None, HDIM, 2 * BLK), lambda s, *_: (0, 0, s, 0, 0), pipeline_mode=mode),
                 pl.BlockSpec((count, None, 8, 2 * BLK), lambda s, *_: (0, s, 0, 0), pipeline_mode=mode),
-                by_slot(HDIM, 2),
+                by_slot(HDIM, 8),
             ],
             out_specs=[
                 by_slot(count, HDIM, 2 * BLK),
@@ -327,8 +327,8 @@
     rate_k = jax.nn.sigmoid(logit_ref[place, 1:2, lanes])
     rate_v = jax.nn.sigmoid(logit_ref[place, 2:3, lanes])
     dq, dk, dv = dq_ref[block], dk_ref[block], dv_ref[block]
-    dq_raw, part_q = norm_back(q_raw, gain_ref[:, 0:1], dq[:HDIM] * SCORE)
-    dk_mixed, part_k = norm_back(k_raw + rate_k * k_step, gain_ref[:, 1:2], dk[:HDIM] * LN2)
+    dq_raw, part_q = norm_back(q_raw, gain_ref[:, 1:2], dq[:HDIM] * SCORE)
+    dk_mixed, part_k = norm_back(k_raw + rate_k * k_step, gain_ref[:, 2:3], dk[:HDIM] * LN2)
     send_k, send_v = rate_k * dk_mixed, rate_v * dv
     draw_ref[place, 0, :, lanes] = dq_raw.astype(bf16)
     draw_ref[place, 1, :, lanes] = (dk_mixed - send_k + shifted_back(send_k, next_k)).astype(bf16)
@@ -384,8 +384,8 @@
 
     zero = jnp.zeros((HDIM, BLK), f32)
     _, _, sum_q, sum_k = lax.fori_loop(0, blocks, finish, (zero, zero, zero, zero))
-    dgain_ref[:, 0:1] = jnp.sum(sum_q, 1, keepdims=True)
-    dgain_ref[:, 1:2] = jnp.sum(sum_k, 1, keepdims=True)
+    dgain_ref[:, 1:2] = jnp.sum(sum_q, 1, keepdims=True)
+    dgain_ref[:, 2:3] = jnp.sum(sum_k, 1, keepdims=True)
     forget_back(count, bias_ref[slot], logit_ref, cum_ref, dlogit_ref)
 
 
@@ -405,7 +405,7 @@
             in_specs=[
                 raw_spec,
                 place_spec(8),
-                by_slot(HDIM, 2),
+                by_slot(HDIM, 8),
                 place_spec(HDIM),
                 by_slot(blocks, HDIM, BLK),
                 by_slot(blocks + 1, 128, BLK),
@@ -413,7 +413,7 @@
                 by_slot(blocks, 80, BLK),
                 by_slot(blocks, 80, BLK),
             ],
-            out_specs=[raw_spec, place_spec(8), by_slot(HDIM, 2)],
+            out_specs=[raw_spec, place_spec(8), by_slot(HDIM, 8)],
             scratch_shapes=[
                 pltpu.VMEM((blocks + 1, 128, BLK), bf16),
                 pltpu.VMEM((blocks, BLK, 128), bf16),
@@ -622,9 +622,9 @@
     return lax.dot_general(a, b, (((i,), (j,)), ((), ())), preferred_element_type=f32)
 
 
-def front_kernel(count, skip_ref, bias_ref, x_ref, w_ref, wsmall_ref, gain_ref, gains_ref,
+def front_kernel(count, skip_ref, bias_ref, x_ref, w_ref, wsmall_ref, gain_ref,
                  h_ref, gate_ref, att_ref, raw_out, logit_out, full_out, q_out, k_out, kt_out, vt_out,
-                 ht_ref, proj_ref, small_ref, raw_ref, logit_ref, mixed_ref, full_ref, q_ref, k_ref, kt_ref, vt_ref, cum_ref, acc_ref,
+                 ht_ref, proj_ref, small_ref, raw_ref, logit_ref, mixed_ref, full_ref, q_ref, k_ref, kt_ref, vt_ref, cum_ref, acc_ref, gains_ref,
                  send, recv, own, back_send, back_recv, back_own, keep):
     me = lax.axis_index("seq")
     barrier = pltpu.get_barrier_semaphore()
@@ -635,7 +635,7 @@
     for i in range(rows // 128):
         here = slice(128 * i, 128 * i + 128)
         v = x_ref[here].astype(f32)
-        normed = v * lax.rsqrt(jnp.mean(v * v, 1, keepdims=True) + EPS) * gain_ref[...]
+        normed = v * lax.rsqrt(jnp.mean(v * v, 1, keepdims=True) + EPS) * gain_ref[0:1]
         h_ref[here] = normed.astype(bf16)
         ht_ref[:, here] = normed.T.astype(bf16)
 
@@ -644,7 +644,11 @@
         proj_ref[pl.ds(4 * i, 4)] = block.astype(bf16).reshape(4, HDIM, rows)
         return carried
 
-    small_ref[...] = mm(wsmall_ref[...], ht_ref[...], TN).reshape(HEADS, 8, rows)
+    gains_ref[...] = gain_ref[...].T
+    small = mm(wsmall_ref[...], ht_ref[...], TN)
+    for head in range(HEADS):
+        ordered = [small[HEADS * i + head : HEADS * i + head + 1] for i in range(3)]
+        small_ref[head] = jnp.concatenate(ordered + [jnp.zeros((5, rows), f32)], 0)
     lax.fori_loop(0, 9, project, 0)
     pl.semaphore_wait(barrier, count - 1)
     first = first_head(me, count)
@@ -707,9 +711,11 @@
             pl.when(is_mine(me, slot, source, count))(copies[0].wait_recv)
             for copy in copies[1:]:
                 copy.wait_recv()
-        raws, logits, gains = raw_ref.at[:, :, slot], logit_ref.at[:, slot], gains_ref.at[slot]
+        head = first + slot
+        raws, logits = raw_ref.at[:, :, slot], logit_ref.at[:, slot]
+        gains = gains_ref.at[pl.ds(pl.multiple_of(head * HDIM, HDIM), HDIM)]
         qs, ks, kts, vts = q_ref.at[slot], k_ref.at[slot], kt_ref.at[slot], vt_ref.at[slot]
-        cum_ref[...] = log_forget_sums(logits[:, 0, :] + bias_ref[slot], count)
+        cum_ref[...] = log_forget_sums(logits[:, 0, :] + bias_ref[head], count)
 
         def prepare(block, state):
             acc_ref[block] = jnp.zeros(acc_ref.shape[1:], f32)
@@ -784,7 +790,7 @@
         copy.wait()
 
 
-def front(count, skip, bias, x, w_attn, w_small, gain, gains):
+def front(count, skip, bias, x, w_attn, w_small, gains):
     rows = x.shape[0]
     blocks = 2 * count
     vmem = pl.BlockSpec(memory_space=pltpu.VMEM)
@@ -797,7 +803,7 @@
         functools.partial(front_kernel, count),
         out_shape=[jax.ShapeDtypeStruct(s, t) for s, t in [
             ((rows, D), bf16), ((D, rows), f32), ((D, rows), bf16), (raw, bf16), (logit, f32)] + state],
-        in_specs=[smem, smem] + [vmem] * 5,
+        in_specs=[smem, smem] + [vmem] * 4,
         out_specs=[vmem] * 3 + [ANY] * 7,
         scratch_shapes=[
             pltpu.VMEM((D, rows), bf16),
@@ -809,12 +815,13 @@
         ] + [pltpu.VMEM(s, t) for s, t in state] + [
             pltpu.VMEM((count, rows), f32),
             pltpu.VMEM((blocks + 1, 80, BLK), f32),
+            pltpu.VMEM((D, 8), f32),
             dma((count, 2, 4)), dma((count, 2, 4)), dma((2, 4)),
             dma((count, 2)), dma((HEADS,)), dma((2,)), dma((2, 6)),
         ],
         compiler_params=pltpu.CompilerParams(collective_id=0, has_side_effects=True, vmem_limit_bytes=60 * 2**20),
         name="front",
-    )(skip, bias, x, w_attn, w_small, gain, gains)
+    )(skip, bias, x, w_attn, w_small, gains)
 
 
 SMALL = 48
@@ -992,19 +999,18 @@
     lax.fori_loop(0, 9, block, 0)
 
 
-def late_rest(h_ref, proj_ref, w_ref, wsmall_ref, x_ref, gain_ref, dresid_ref, extra_ref, dsmall_ref, rows_ref, dx_ref, g_ref, gsum_ref=None):
-    low_small = dsmall_ref[...].astype(bf16)
+def late_rest(h_ref, proj_ref, w_ref, wsmall_ref, x_ref, gain_ref, dresid_ref, extra_ref, dsmall_ref, rows_ref, small_ref, dx_ref, g_ref, gsum_ref=None):
+    ordered = [dsmall_ref[8 * head + i : 8 * head + i + 1] for i in range(3) for head in range(HEADS)]
+    low_small = jnp.concatenate(ordered + [jnp.zeros((SMALL - 3 * HEADS, ordered[0].shape[1]), f32)], 0).astype(bf16)
     for i in range(3):
         cols = slice(256 * i, 256 * i + 256)
         part = mm(w_ref[cols, :], proj_ref[...]) + mm(wsmall_ref[cols, :], low_small)
         dx_ref[:, cols] = part.T
-    small = mm(low_small, h_ref[...])
-    for head in range(HEADS):
-        rows_ref[3 * head : 3 * head + 3] = small[8 * head : 8 * head + 3]
-    rows_ref[3 * HEADS :] = extra_ref[...]
+    rows_ref[...] = mm(low_small, h_ref[...])
+    small_ref[...] = extra_ref[...]
     if gsum_ref is not None:
-        rows_ref[3 * HEADS + 2 : 3 * HEADS + 4] = gsum_ref[0:2]
-    gain = gain_ref[...]
+        small_ref[2:4] = gsum_ref[0:2]
+    gain = gain_ref[0:1]
     dgain = jnp.zeros((1, D), f32)
     for i in range(h_ref.shape[0] // 128):
         here = slice(128 * i, 128 * i + 128)
@@ -1013,12 +1019,12 @@
         hat, gu = v * scale, u * gain
         dx_ref[here] = dresid_ref[here] + scale * (gu - hat * jnp.mean(hat * gu, 1, keepdims=True))
         dgain = dgain + jnp.sum(hat * u, 0, keepdims=True)
-    rows_ref[3 * HEADS : 3 * HEADS + 1] = dgain
+    small_ref[0:1] = dgain
     bias_rows = jnp.concatenate([dsmall_ref[8 * head : 8 * head + 1] for head in range(HEADS)], 0)
     bias_sum = jnp.sum(bias_rows, 1, keepdims=True)
     lane = lax.broadcasted_iota(jnp.int32, (HEADS, 128), 1)
     row = lax.broadcasted_iota(jnp.int32, (HEADS, 128), 0)
-    rows_ref[3 * HEADS + 4 : 3 * HEADS + 5, 0:128] = jnp.sum(jnp.where(lane == row, bias_sum, 0.0), 0, keepdims=True)
+    small_ref[4:5, 0:128] = jnp.sum(jnp.where(lane == row, bias_sum, 0.0), 0, keepdims=True)
 
     used = 9 * (D // UNIT)
     units = g_ref.shape[0]
@@ -1026,6 +1032,37 @@
         g_ref[used + 3 * i : used + 3 * i + 3] = rows_ref[:, 256 * i : 256 * i + 256].astype(bf16).reshape(3, UNIT, 256)
     if units > used + 9:
         g_ref[used + 9 :] = jnp.zeros((units - used - 9, UNIT, 256), bf16)
+
+
+class Doubling:
+    def __init__(self, bits, own, landing, send, recv):
+        self.bits, self.own, self.landing, self.send, self.recv = bits, own, landing, send, recv
+        self.at = 0
+
+    def give(self):
+        there, _ = partner(self.bits[self.at])
+        self.copy = pltpu.make_async_remote_copy(
+            src_ref=self.own, dst_ref=self.landing.at[self.at], send_sem=self.send.at[self.at], recv_sem=self.recv.at[self.at],
+            device_id=there, device_id_type=MESH,
+        )
+        self.copy.start()
+
+    def add(self):
+        self.copy.wait()
+        self.own[...] += self.landing[self.at]
+        self.at += 1
+
+
+def finish_late(late, early, early_left, stages, small, small_out):
+    for stage in range(2 * stages):
+        if stage < stages:
+            small.give()
+        step(late, stages)
+        if stage < early_left:
+            step(early, stages)
+        if stage < stages:
+            small.add()
+    small_out[...] = small.own[...]
 
 
 def give_late(sums, rest, early, stages):
@@ -1040,8 +1077,8 @@
 
 
 def last_kernel(count, sets, draw_ref, dlogit_ref, early_ref, h_ref, dgate_ref, w_ref, wsmall_ref, x_ref, gain_ref,
-                dresid_ref, extra_ref, late_out, early_out, dx_ref,
-                proj_ref, logit_ref, part_ref, dsmall_ref, rows_ref, g_ref, land_ref, e_ref, eland_ref,
+                dresid_ref, extra_ref, late_out, early_out, dx_ref, small_out,
+                proj_ref, logit_ref, part_ref, dsmall_ref, rows_ref, small_ref, small_land, ssend, srecv, g_ref, land_ref, e_ref, eland_ref,
                 send, recv, recv_q, recv_kv, local, gsend, grecv, gsem, esend, erecv, esem):
     near, far, seq = sets
     bits = [near, far] + seq
@@ -1095,14 +1132,10 @@
     late = sums_of(g_ref.shape[0], least, sets, None, g_ref, land_ref, late_out, gsend, grecv, gsem)
 
     def rest():
-        late_rest(h_ref, proj_ref, w_ref, wsmall_ref, x_ref, gain_ref, dresid_ref, extra_ref, dsmall_ref, rows_ref, dx_ref, g_ref)
+        late_rest(h_ref, proj_ref, w_ref, wsmall_ref, x_ref, gain_ref, dresid_ref, extra_ref, dsmall_ref, rows_ref, small_ref, dx_ref, g_ref)
 
     give_late(late, rest, early, stages)
-    early_left = 2 * stages - 3
-    for stage in range(2 * stages):
-        step(late, stages)
-        if stage < early_left:
-            step(early, stages)
+    finish_late(late, early, 2 * stages - 3, stages, Doubling(bits, small_ref, small_land, ssend, srecv), small_out)
 
 
 def last(count, sets, d_raw, d_logits, early, h, d_gate, w_attn, w_small, x, gain, d_resid, extra):
@@ -1119,15 +1152,19 @@
             jax.ShapeDtypeStruct((units,) + shape, bf16),
             jax.ShapeDtypeStruct(early.shape, bf16),
             jax.ShapeDtypeStruct((rows, D), f32),
+            jax.ShapeDtypeStruct((8, D), f32),
         ],
         in_specs=[ANY] * 3 + [vmem] * 8,
-        out_specs=[ANY, ANY, vmem],
+        out_specs=[ANY, ANY, vmem, vmem],
         scratch_shapes=[
             pltpu.VMEM((4 * D, rows), bf16),
             pltpu.VMEM((count, 2, 8, rows), f32),
             pltpu.VMEM((HEADS, most, 2, HDIM, rows), bf16),
             pltpu.VMEM((8 * HEADS, rows), f32),
             pltpu.VMEM((SMALL, D), f32),
+            pltpu.VMEM((8, D), f32),
+            pltpu.VMEM((stages, 8, D), f32),
+            dma((stages,)), dma((stages,)),
             pltpu.VMEM((units,) + shape, bf16),
             pltpu.VMEM((units,) + shape, bf16),
             pltpu.VMEM((early.shape[0] // 2,) + shape, bf16),
@@ -1143,47 +1180,52 @@
 
 def unpack_kernel(parts, *refs):
     o_ref = refs[-1]
+    width = refs[0].shape[0] // (o_ref.shape[0] // UNIT)
     at = 0
     for ref, blocks in zip(refs, parts):
-        here = (pl.program_id(0) >= at) & (pl.program_id(0) < at + blocks)
-
-        @pl.when(here)
-        def _():
-            o_ref[...] = ref[...].reshape(o_ref.shape).astype(f32)
+
+        @pl.when((pl.program_id(0) >= at) & (pl.program_id(0) < at + blocks))
+        def _(ref=ref):
+            for i in range(width):
+                size = o_ref.shape[0] // UNIT
+                block = ref[size * i : size * i + size].reshape(o_ref.shape[0], 256)
+                o_ref[:, 256 * i : 256 * i + 256] = block.astype(f32)
 
         at += blocks
 
 
-def unpack(rows, *parts):
+def unpack(rows, width, *parts):
     size = rows // UNIT
     specs, at = [], 0
     for _, first, blocks in parts:
+        first, blocks = first // width, blocks // width
         index = lambda i, at=at, first=first, blocks=blocks: (first + jnp.clip(i - at, 0, blocks - 1), 0, 0)
-        specs.append(pl.BlockSpec((size, UNIT, 256), index))
+        specs.append(pl.BlockSpec((size * width, UNIT, 256), index))
         at += blocks
     return pl.pallas_call(
-        functools.partial(unpack_kernel, [blocks for _, _, blocks in parts]),
+        functools.partial(unpack_kernel, [blocks // width for _, _, blocks in parts]),
         grid=(at,),
         in_specs=specs,
-        out_specs=pl.BlockSpec((rows, 256), lambda i: (0, i)),
-        out_shape=jax.ShapeDtypeStruct((rows, 256 * at), f32),
-        compiler_params=pltpu.CompilerParams(vmem_limit_bytes=32 * 2**20),
+        out_specs=pl.BlockSpec((rows, 256 * width), lambda i: (0, i)),
+        out_shape=jax.ShapeDtypeStruct((rows, 256 * at * width), f32),
+        compiler_params=pltpu.CompilerParams(vmem_limit_bytes=62 * 2**20),
         name="unpack",
     )(*[units for units, _, _ in parts])
 
 
-def back_kernel(count, sets, skip_ref, bias_ref, dmixed_ref, logits_ref, gains_ref, wsmall_ref, gain_ref, extra_ref,
+def back_kernel(count, sets, skip_ref, bias_ref, dmixed_ref, logits_ref, wsmall_ref, gain_ref, extra_ref,
                 raw_in, full_in, q_in, k_in, kt_in, vt_in, early_ref, h_in, dgate_in, w_in, x_in, dresid_in,
-                late_out, early_out, dx_ref,
+                late_out, early_out, dx_ref, small_out,
                 raw_ref, full_ref, q_ref, k_ref, kt_ref, vt_ref, do_ref, v_ref, cum_ref, dq_ref, dk_ref, dv_ref,
-                draw_ref, dlogit_ref, gsum_ref,
-                proj_ref, logit_ref, part_ref, dsmall_ref, rows_ref, h_ref, w_ref, x_ref, dresid_ref,
+                dlogit_ref, gsum_ref, gains_ref,
+                proj_ref, logit_ref, part_ref, dsmall_ref, rows_ref, small_ref, small_land, ssend, srecv, h_ref, w_ref, x_ref, dresid_ref,
                 g_ref, land_ref, e_ref, eland_ref,
                 load, send, recv, recv_q, recv_kv, own, gsend, grecv, gsem, esend, erecv, esem):
     near, far, seq = sets
     bits = [near, far] + seq
     stages, least = len(bits), 1 << len(bits)
     blocks = 2 * count
+    draw_ref = raw_ref
     sums = (dq_ref, dk_ref, dv_ref)
 
     def state(slot):
@@ -1204,6 +1246,7 @@
     for part in early:
         part.give()
     gsum_ref[...] = jnp.zeros(gsum_ref.shape, f32)
+    gains_ref[...] = gain_ref[...].T
 
     def sends(slot, k):
         peer = lax.rem(me + k, count)
@@ -1255,7 +1298,8 @@
             for copy in state(1):
                 copy.start()
             other[0].wait()
-        raws, logits, gains = raw_ref.at[:, :, slot], logits_ref.at[:, slot], gains_ref.at[slot]
+        raws, logits = raw_ref.at[:, :, slot], logits_ref.at[:, slot]
+        gains = gains_ref.at[pl.ds(pl.multiple_of((first + slot) * HDIM, HDIM), HDIM)]
         draws, dlogits = draw_ref.at[:, :, slot], dlogit_ref.at[:, slot]
 
         def finish(number, carried):
@@ -1271,7 +1315,7 @@
         for i, column in enumerate((sum_q, sum_k)):
             placed = jnp.where(here, jnp.sum(column, 1, keepdims=True), 0.0)
             gsum_ref[i : i + 1] += jnp.sum(placed, 0, keepdims=True)
-        forget_back(count, bias_ref[slot], logits, cum_ref, dlogits)
+        forget_back(count, bias_ref[first + slot], logits, cum_ref, dlogits)
         for k in far_first(count) + [0]:
             for mine, copy in sends(slot, k):
                 if mine is None:
@@ -1305,20 +1349,16 @@
     late = sums_of(g_ref.shape[0], least, sets, None, g_ref, land_ref, late_out, gsend, grecv, gsem)
 
     def rest():
-        late_rest(h_ref, proj_ref, w_ref, wsmall_ref, x_ref, gain_ref, dresid_ref, extra_ref, dsmall_ref, rows_ref, dx_ref, g_ref, gsum_ref)
+        late_rest(h_ref, proj_ref, w_ref, wsmall_ref, x_ref, gain_ref, dresid_ref, extra_ref, dsmall_ref, rows_ref, small_ref, dx_ref, g_ref, gsum_ref)
 
     give_late(late, rest, early, stages)
-    early_left = 2 * stages - 8 - LATER
-    for stage in range(2 * stages):
-        step(late, stages)
-        if stage < early_left:
-            step(early, stages)
+    finish_late(late, early, 2 * stages - 8 - LATER, stages, Doubling(bits, small_ref, small_land, ssend, srecv), small_out)
 
 
 LATER = 1
 
 
-def back(count, sets, skip, bias, d_mixed, logits, gains, w_small, gain, extra, raw, full, q, k, kt, vt, early, h, d_gate, w_attn, x, d_resid):
+def back(count, sets, skip, bias, d_mixed, logits, w_small, gains, extra, raw, full, q, k, kt, vt, early, h, d_gate, w_attn, x, d_resid):
     stages = 2 + len(sets[2])
     units = padded(9 * (D // UNIT) + 9, 1 << stages)
     rows = h.shape[0]
@@ -1335,9 +1375,10 @@
             jax.ShapeDtypeStruct((units,) + shape, bf16),
             jax.ShapeDtypeStruct(early.shape, bf16),
             jax.ShapeDtypeStruct((rows, D), f32),
+            jax.ShapeDtypeStruct((8, D), f32),
         ],
-        in_specs=[smem, smem] + [vmem] * 6 + [ANY] * 12,
-        out_specs=[ANY, ANY, vmem],
+        in_specs=[smem, smem] + [vmem] * 5 + [ANY] * 12,
+        out_specs=[ANY, ANY, vmem, vmem],
         scratch_shapes=[
             pltpu.VMEM(raw.shape, bf16), held(full), held(q), held(k), held(kt), held(vt),
             pltpu.VMEM((blocks + 1, 128, BLK), bf16),
@@ -1346,14 +1387,17 @@
             pltpu.VMEM((blocks + 1, 80, BLK), f32),
             pltpu.VMEM((blocks, 80, BLK), f32),
             pltpu.VMEM((blocks, HDIM, BLK), f32),
-            pltpu.VMEM(raw.shape, bf16),
             pltpu.VMEM(logits.shape, f32),
             pltpu.VMEM((8, D), f32),
+            pltpu.VMEM((D, 8), f32),
             pltpu.VMEM((4 * D, rows), bf16),
             pltpu.VMEM((count, 2, 8, rows), f32),
             pltpu.VMEM((HEADS, most, 2, HDIM, rows), bf16),
             pltpu.VMEM((8 * HEADS, rows), f32),
             pltpu.VMEM((SMALL, D), f32),
+            pltpu.VMEM((8, D), f32),
+            pltpu.VMEM((stages, 8, D), f32),
+            dma((stages,)), dma((stages,)),
             pltpu.VMEM(h.shape, bf16),
             pltpu.VMEM(w_attn.shape, bf16),
             pltpu.VMEM(x.shape, bf16),
@@ -1368,7 +1412,7 @@
         ],
         compiler_params=pltpu.CompilerParams(collective_id=4, has_side_effects=True, vmem_limit_bytes=63 * 2**20),
         name="back",
-    )(skip, bias, d_mixed, logits, gains, w_small, gain, extra, raw, full, q, k, kt, vt, early, h, d_gate, w_attn, x, d_resid)
+    )(skip, bias, d_mixed, logits, w_small, gains, extra, raw, full, q, k, kt, vt, early, h, d_gate, w_attn, x, d_resid)
 
 
 def rms_scale(values, gains):
@@ -1390,16 +1434,15 @@
     device = me.astype(jnp.int32)[None]
     head = first_head(me, count)
     skip = skip_table[0]
-    gains = jnp.stack([query_gain.reshape(HEADS, HDIM), key_gain.reshape(HEADS, HDIM)], 2)
-    gains = lax.dynamic_slice_in_dim(gains, head, 2, 0)
-    bias = lax.dynamic_slice_in_dim(forget_bias, head, 2, 0)
-    w_small = jnp.pad(w_heads.reshape(D, 3, HEADS).transpose(0, 2, 1), ((0, 0), (0, 0), (0, 5))).reshape(D, HEADS * 8)
-
+    all_gains = jnp.concatenate([jnp.stack([gain_attn, query_gain, key_gain]), jnp.zeros((5, D), f32)], 0)
     if count <= 8:
         h_first, gate_logit, attended, raw, logits, mixed, q, k, kt, vt = front(
-            count, skip, bias, tokens[0], w_attn, w_small, gain_attn[None], gains
+            count, skip, forget_bias, tokens[0], w_attn, w_heads, all_gains
         )
     else:
+        gains = lax.dynamic_slice_in_dim(all_gains.T.reshape(HEADS, HDIM, 8), head, 2, 0)
+        bias = lax.dynamic_slice_in_dim(forget_bias, head, 2, 0)
+        w_small = jnp.pad(w_heads.reshape(D, 3, HEADS).transpose(0, 2, 1), ((0, 0), (0, 0), (0, 5))).reshape(D, HEADS * 8)
         h_first = rms_scale(inputs, gain_attn).astype(bf16)
         qkv = dot(w_attn[:, : 3 * D], h_first, 0, 1).astype(bf16).reshape(3, HEADS, HDIM, rows)
         gate_logit = dot(w_attn[:, 3 * D :], h_first, 0, 1)
@@ -1437,34 +1480,35 @@
     )
     zeros = lambda n: jnp.zeros((n, D), f32)
     if count <= 8:
-        extra = jnp.concatenate([zeros(1), grad_gain_ffn[None], zeros(SMALL - 3 * HEADS - 2)], 0)
-        late, early, d_inputs = back(
-            count, sets, skip, bias, d_mixed_all, logits, gains, w_small, gain_attn[None], extra,
+        extra = jnp.concatenate([zeros(1), grad_gain_ffn[None], zeros(6)], 0)
+        late, early, d_inputs, small = back(
+            count, sets, skip, forget_bias, d_mixed_all, logits, jnp.pad(w_heads, ((0, 0), (0, SMALL - 3 * HEADS))), all_gains, extra,
             raw, mixed, q, k, kt, vt, early, h_first, d_gate_logit, w_attn, tokens[0], d_resid,
         )
     else:
         d_raw, d_logits, d_gains = attend_backward(device, skip, bias, raw, logits, gains, d_mixed_all, mixed, q, k, kt, vt)
-        placed = lax.dynamic_update_slice(jnp.zeros((HEADS, HDIM, 2), f32), d_gains, (head, 0, 0)).reshape(D, 2).T
-        extra = jnp.concatenate([zeros(1), grad_gain_ffn[None], placed, zeros(SMALL - 3 * HEADS - 4)], 0)
-        late, early, d_inputs = last(
-            count, sets, d_raw, d_logits, early, h_first, d_gate_logit, w_attn, w_small, tokens[0], gain_attn[None], d_resid, extra
+        placed = lax.dynamic_update_slice(jnp.zeros((HEADS, HDIM, 2), f32), d_gains[..., 1:3], (head, 0, 0)).reshape(D, 2).T
+        extra = jnp.concatenate([zeros(1), grad_gain_ffn[None], placed, zeros(4)], 0)
+        late, early, d_inputs, small = last(
+            count, sets, d_raw, d_logits, early, h_first, d_gate_logit, w_attn,
+            jnp.pad(w_heads, ((0, 0), (0, SMALL - 3 * HEADS))), tokens[0], gain_attn[None], d_resid, extra
         )
     row = 3 * HEADS
     used = 9 * (D // UNIT)
-    small = late[used : used + 9].reshape(3, SMALL, 256).transpose(1, 0, 2).reshape(SMALL, D).astype(f32)
+    heads_rows = late[used : used + 9].reshape(3, SMALL, 256).transpose(1, 0, 2).reshape(SMALL, D).astype(f32)
     return (
         output[None].astype(bf16),
         d_inputs[None],
-        small[row],
-        unpack(D, (late, 0, 9), (early, 27, 3)),
-        small[:row].reshape(HEADS, 3, D).transpose(2, 1, 0).reshape(D, row),
-        small[row + 4, :HEADS],
-        small[row + 2],
-        small[row + 3],
-        unpack(D, (early, 24, 3)),
-        small[row + 1],
-        unpack(D, (early, 0, 16)),
-        unpack(FF, (early, 6, 3)),
+        small[0],
+        unpack(D, 3, (late, 0, 9), (early, 27, 3)),
+        heads_rows[:row].T,
+        small[4, :HEADS],
+        small[2],
+        small[3],
+        unpack(D, 1, (early, 24, 3)),
+        small[1],
+        unpack(D, 2, (early, 0, 16)),
+        unpack(FF, 1, (early, 6, 3)),
     )
 
 

time: 436 us -> 431 us (0.989)
  local copies, waits for them, and re-layouts: 22.8 us -> 10.4 us
  Pallas kernels: 378 us -> 385 us
    unnamed x37 -> x34, local copies, waits for them, and re-layouts: 11.9 us -> 3.83 us
    pallas_call x4, Pallas kernels: 18.3 us -> 23.5 us  [unpack(): pl.pallas_call(functools.partial(unpack_kernel, [blocks // width for _, _...]
where the time goes in v6:
time: 431 us; the launch traced here: 430 us
  Pallas kernels  385 us (89%)
  matrix products  24.2 us (6%)
  local copies, waits for them, and re-layouts  10.4 us (2%)
  other arithmetic  9.5 us (2%)
    pallas_call x1, Pallas kernels, back(): pl.pallas_call(functools.partial(back_kernel, count, sets), out_shape=[ja...  228 us
    pallas_call x1, Pallas kernels, front(): pl.pallas_call(functools.partial(front_kernel, count), out_shape=[jax.Sha...  110 us
    dot_general x6, matrix products, dot(): lax.dot_general(a, b, (((i,), (j,)), ((), ())), preferred_element_type=f32)  24.2 us
    pallas_call x1, Pallas kernels, grads_out(): pl.pallas_call(functools.partial(grads_out_kernel, count), out_shape=[jax...  23.7 us
    pallas_call x4, Pallas kernels, unpack(): pl.pallas_call(functools.partial(unpack_kernel, [blocks // width for _, _...  23.5 us

profile of v6, /device:TPU:0, one launch (start us, length us, event | category | flops | bytes accessed | tf_op | source)
XLA Modules:
  0.0 429.7 jit_solution(12696618281383901392)
XLA Ops:
  0.8 0.7 stack.9
  2.2 0.7 stack.11
  3.6 1.0 copy.29.wsmall_ref
  4.6 0.7 pad.12.wsmall_ref
  5.3 109.9 %front.1 = (bf16[512,768]{1,0:T(8,128)(2,1)}, f32[768,512]{1,0:T(8,128)}, bf16[768,512]{1,0:T(8,128)(2,1)}, bf16[8,3,2,64,512]{4,3,2,1,0:T(8,128)(2,1)}, f32[8,2...) custom-call(s32[16,16]{1,0:T(8,128)} %bitcast.53, ...), custom_call_target="tpu_custom_call" | custom-call | tf_op jit(solution)/shard_map/front/pallas_call | solution.py:802
  115.2 2.2 fusion.3.gated_ref
  117.5 2.5 multiply_reduce_fusion.2
  120.3 3.4 fusion.16
  123.8 5.6 %fusion.10 = (f32[512,2048]{1,0:T(8,128)}, f32[512,2048]{1,0:T(8,128)}, bf16[512,2048]{1,0:T(8,128)(2,1)}) fusion(f32[512,4096]{1,0:T(8,128)S(1)} %fusion.16, bf16[2048,768]{1,0:T(8,128)(2,1)S(1)} %copy-done.11, bf16[1,512,768]{2,1,0:T(8,128)(2,1)S(1)} %copy-done.2), kind=kOutput, calls=%fused_computation.25 | convolution fusion | flops 1625292800 | bytes 22806528 | tf_op jit(solution)/shard_map/dot_general | solution.py:622
  129.4 4.1 add_convert_fusion.dgu_ref
  133.5 6.7 %fusion.9 = bf16[1,512,768]{2,1,0:T(8,128)(2,1)} fusion(f32[512,768]{1,0:T(8,128)S(1)} %get-tuple-element.58, bf16[512,2048]{1,0:T(8,128)(2,1)} %get-tuple-element.54.hidden_ref, bf16[2048,768]{1,0:T(8,128)(2,1)} %param.25), kind=kOutput, calls=%fused_computation.24 | convolution fusion | flops 1611399168 | bytes 7602176 | tf_op jit(solution)/shard_map/dot_general | solution.py:622
  140.2 3.6 multiply_reduce_fusion
  143.9 1.6 fusion.14
  146.4 2.3 fusion.6
  149.4 23.7 %grads_out.1 = (bf16[8,2,64,512]{3,2,1,0:T(8,128)(2,1)}, bf16[1440,16,256]{2,1,0:T(8,128)(2,1)}) custom-call(bf16[12,64,512]{2,1,0:T(8,128)(2,1)} %bitcast.48, bf16[512,768]{1,0:T(8,128)(2,1)} %get-tuple-element.30.h1_ref.h_in, bf16[768,512]{1,0:T(8,128)(2,1)} %get-tuple-element.55.dgate_ref.dgate_in, bf16[512,768]{1,0:T(8,128)(2,1)} %copy-done.1, ...), custom_call_target="tpu_custom_call" | custom-call | tf_op jit(solution)/shard_map/grads_out/pallas_call | solution.py:607
  173.1 227.6 %back.1 = (bf16[448,16,256]{2,1,0:T(8,128)(2,1)}, bf16[1440,16,256]{2,1,0:T(8,128)(2,1)}, f32[512,768]{1,0:T(8,128)}, f32[8,768]{1,0:T(8,128)}) custom-call(s32[16,16]{1,0:T(8,128)} %bitcast.54, f32[12]{0:T(128)} %bias_ref.3, bf16[8,2,64,512]{3,2,1,0:T(8,128)(2,1)} %get-tuple-element.31.dmixed_ref, f32[8,2,8,512]{3,2,1,0:T(8,128)} %get-tuple-element.32.logits_ref, ...), custom_call_target="tpu_custom_call" | custom-call | tf_op jit(solution)/shard_map/back/pallas_call | solution.py:1372
  400.7 1.2 slice_bitcast_fusion
  401.9 1.5 slice_reduce_fusion
  403.4 0.9 slice.34
  405.0 3.3 unpack.5
  408.4 6.4 %unpack.4 = f32[768,3072]{1,0:T(8,128)} custom-call(bf16[448,16,256]{2,1,0:T(8,128)(2,1)} %get-tuple-element.42.refs_0_, bf16[1440,16,256]{2,1,0:T(8,128)(2,1)} %get-tuple-element.43.refs_1_.refs_0_), custom_call_target="tpu_custom_call" | custom-call | tf_op jit(solution)/shard_map/unpack/pallas_call | solution.py:1205
  414.7 4.9 %unpack.7 = f32[2048,768]{1,0:T(8,128)} custom-call(bf16[1440,16,256]{2,1,0:T(8,128)(2,1)} %get-tuple-element.43.refs_1_.refs_0_), custom_call_target="tpu_custom_call" | custom-call | tf_op jit(solution)/shard_map/unpack/pallas_call | solution.py:1205
  419.6 8.9 %unpack.6 = f32[768,4096]{1,0:T(8,128)} custom-call(bf16[1440,16,256]{2,1,0:T(8,128)(2,1)} %get-tuple-element.43.refs_1_.refs_0_), custom_call_target="tpu_custom_call" | custom-call | tf_op jit(solution)/shard_map/unpack/pallas_call | solution.py:1205
  428.5 1.1 copy.38
  (47 shorter events, 4.2 us)
Async XLA Ops:
  4.6 0.8 copy-start.6
  5.3 112.2 %copy-start.5 = (bf16[1,512,768]{2,1,0:T(8,128)(2,1)S(1)}, bf16[1,512,768]{2,1,0:T(8,128)(2,1)}, u32[]{:S(2)}) copy-start(bf16[1,512,768]{2,1,0:T(8,128)(2,1)} %param.13) | copy-start | bytes 2359300
  5.3 114.9 %slice-start = ((s8[6291456]{0:T(1024)(128)(4,1)}), s8[2097152]{0:T(1024)(128)(4,1)S(1)}, s32[]{:S(2)}) async-start(s8[6291456]{0:T(1024)(128)(4,1)} %bitcast.42), calls=%async_computation | async-start | bytes 4194304
  115.2 5.0 %slice-start.1 = ((s8[6291456]{0:T(1024)(128)(4,1)}), s8[4194304]{0:T(1024)(128)(4,1)S(1)}, s32[]{:S(2)}) async-start(s8[6291456]{0:T(1024)(128)(4,1)} %bitcast.42), calls=%async_computation.1 | async-start | bytes 8388608
  117.5 2.5 copy-start.4
  117.5 2.5 copy-start.10
  120.3 3.5 copy-start.1
  120.3 3.5 copy-start.2
  120.3 3.5 copy-start.11
  133.4 6.7 %copy-start = (bf16[512,4096]{1,0:T(8,128)(2,1)}, bf16[512,4096]{1,0:T(8,128)(2,1)S(1)}, u32[]{:S(2)}) copy-start(bf16[512,4096]{1,0:T(8,128)(2,1)S(1)} %add_convert_fusion.dgu_ref) | copy-start | bytes 12582916
  143.8 1.6 copy-start.7
  143.8 2.1 copy-start.9
  143.8 2.5 copy-start.12
  145.5 3.2 copy-start.3
  419.6 8.9 %copy-start.8 = (f32[512,768]{1,0:T(8,128)S(1)}, f32[512,768]{1,0:T(8,128)}, u32[]{:S(2)}) copy-start(f32[512,768]{1,0:T(8,128)} %get-tuple-element.40) | copy-start | bytes 4718596

commit v7 on v6

--- a/solution.py
+++ b/solution.py
@@ -211,6 +211,13 @@
     start = (first_head(device, count) + slot) * count
     low = jnp.clip(HEADS * device - start, 0, count)
     return low, jnp.clip(HEADS * device + HEADS - start, low, count)
+
+
+def slot_at(device, phase, count):
+    low, high = own_places(device, 0, count)
+    later, end = own_places(device, 1, count)
+    swap = jnp.where(end - later > high - low, 1, 0)
+    return phase + swap - 2 * phase * swap
 
 
 def pairs_of_place(place, batch, size, count):
@@ -672,14 +679,15 @@
             pltpu.make_async_copy(small_ref.at[head], logit_ref.at[me, slot], own.at[slot, 3]),
         ]
 
-    for slot in range(2):
+    for phase in range(2):
         for k in far_first(count):
             peer = lax.rem(me + k, count)
+            slot = slot_at(peer, phase, count)
             copies = out(slot, k, peer)
             pl.when(is_mine(peer, slot, me, count))(copies[0].start)
             for copy in copies[1:]:
                 copy.start()
-        for copy in own_copies(slot):
+        for copy in own_copies(slot_at(me, phase, count)):
             copy.start()
 
     def gate(i, carried):
@@ -702,7 +710,8 @@
             return push(mixed_ref.at[slot, peer], target, back_send.at[k, slot], back_recv.at[first + slot], peer)
         return pltpu.make_async_copy(mixed_ref.at[slot, peer], target, back_own.at[slot])
 
-    def one_slot(slot, carried):
+    def one_slot(phase, carried):
+        slot = slot_at(me, phase, count)
         for copy in own_copies(slot):
             copy.wait()
         for k in far_first(count):
@@ -1237,9 +1246,10 @@
         for i, (src, dst) in enumerate((
             (raw_in, raw_ref), (h_in, h_ref), (dgate_in, proj_ref.at[pl.ds(3 * D, D)]), (w_in, w_ref), (x_in, x_ref), (dresid_in, dresid_ref)))
     ]
-    for copy in state(0) + other:
+    me = lax.axis_index("seq")
+    for copy in state(slot_at(me, 0, count)) + other:
         copy.start()
-    me = greet_all(bits, count)
+    greet_all(bits, count)
     first = first_head(me, count)
     holders = held_heads(count)
     early = sums_of(early_ref.shape[0], least, sets, early_ref, e_ref, eland_ref, early_out, esend, erecv, esem)
@@ -1264,7 +1274,8 @@
             for i, (mine, src, dst, sem) in enumerate(items)
         ]
 
-    for slot in range(2):
+    for phase in range(2):
+        slot = slot_at(me, phase, count)
         for copy in state(slot):
             copy.wait()
 
@@ -1287,15 +1298,15 @@
 
         low, high = own_places(me, slot, count)
         middle = (low + high) // 2
-        if slot == 0:
+        if phase == 0:
             lax.fori_loop(low, high, one_place, 0)
         else:
             lax.fori_loop(low, middle, one_place, 0)
             step(early, stages)
             lax.fori_loop(middle, high, one_place, 0)
         step(early, stages)
-        if slot == 0:
-            for copy in state(1):
+        if phase == 0:
+            for copy in state(slot_at(me, 1, count)):
                 copy.start()
             other[0].wait()
         raws, logits = raw_ref.at[:, :, slot], logits_ref.at[:, slot]

time: 431 us -> 425 us (0.986)
  Pallas kernels: 385 us -> 379 us
    pallas_call x1, Pallas kernels: 110 us -> 102 us  [front(): pl.pallas_call(functools.partial(front_kernel, count), out_shape=[jax.Sha...]
where the time goes in v7:
time: 425 us; the launch traced here: 424 us
  Pallas kernels  379 us (89%)
  matrix products  24.2 us (6%)
  local copies, waits for them, and re-layouts  10.4 us (2%)
  other arithmetic  9.5 us (2%)
    pallas_call x1, Pallas kernels, back(): pl.pallas_call(functools.partial(back_kernel, count, sets), out_shape=[ja...  227 us
    pallas_call x1, Pallas kernels, front(): pl.pallas_call(functools.partial(front_kernel, count), out_shape=[jax.Sha...  102 us
    pallas_call x1, Pallas kernels, grads_out(): pl.pallas_call(functools.partial(grads_out_kernel, count), out_shape=[jax...  26.8 us
    dot_general x6, matrix products, dot(): lax.dot_general(a, b, (((i,), (j,)), ((), ())), preferred_element_type=f32)  24.2 us
    pallas_call x4, Pallas kernels, unpack(): pl.pallas_call(functools.partial(unpack_kernel, [blocks // width for _, _...  23.5 us

profile of v7, /device:TPU:0, one launch (start us, length us, event | category | flops | bytes accessed | tf_op | source)
XLA Modules:
  0.0 424.1 jit_solution(11912616908916873252)
XLA Ops:
  0.8 0.7 stack.9
  1.5 0.7 stack.10
  3.6 1.0 copy.29.wsmall_ref
  4.6 0.7 pad.12.wsmall_ref
  5.3 101.8 %front.1 = (bf16[512,768]{1,0:T(8,128)(2,1)}, f32[768,512]{1,0:T(8,128)}, bf16[768,512]{1,0:T(8,128)(2,1)}, bf16[8,3,2,64,512]{4,3,2,1,0:T(8,128)(2,1)}, f32[8,2...) custom-call(s32[16,16]{1,0:T(8,128)} %bitcast.53, ...), custom_call_target="tpu_custom_call" | custom-call | tf_op jit(solution)/shard_map/front/pallas_call | solution.py:811
  107.2 2.2 fusion.3.gated_ref
  109.4 2.5 multiply_reduce_fusion.2
  112.2 3.4 fusion.16
  115.7 5.6 %fusion.10 = (f32[512,2048]{1,0:T(8,128)}, f32[512,2048]{1,0:T(8,128)}, bf16[512,2048]{1,0:T(8,128)(2,1)}) fusion(f32[512,4096]{1,0:T(8,128)S(1)} %fusion.16, bf16[2048,768]{1,0:T(8,128)(2,1)S(1)} %copy-done.11, bf16[1,512,768]{2,1,0:T(8,128)(2,1)S(1)} %copy-done.2), kind=kOutput, calls=%fused_computation.25 | convolution fusion | flops 1625292800 | bytes 22806528 | tf_op jit(solution)/shard_map/dot_general | solution.py:629
  121.3 4.1 add_convert_fusion.dgu_ref
  125.4 6.7 %fusion.9 = bf16[1,512,768]{2,1,0:T(8,128)(2,1)} fusion(f32[512,768]{1,0:T(8,128)S(1)} %get-tuple-element.58, bf16[512,2048]{1,0:T(8,128)(2,1)} %get-tuple-element.54.hidden_ref, bf16[2048,768]{1,0:T(8,128)(2,1)} %param.25), kind=kOutput, calls=%fused_computation.24 | convolution fusion | flops 1611399168 | bytes 7602176 | tf_op jit(solution)/shard_map/dot_general | solution.py:629
  132.1 3.6 multiply_reduce_fusion
  135.8 1.6 fusion.14
  138.3 2.3 fusion.6
  141.3 26.8 %grads_out.1 = (bf16[8,2,64,512]{3,2,1,0:T(8,128)(2,1)}, bf16[1440,16,256]{2,1,0:T(8,128)(2,1)}) custom-call(bf16[12,64,512]{2,1,0:T(8,128)(2,1)} %bitcast.48, bf16[512,768]{1,0:T(8,128)(2,1)} %get-tuple-element.30.h1_ref.h_in, bf16[768,512]{1,0:T(8,128)(2,1)} %get-tuple-element.55.dgate_ref.dgate_in, bf16[512,768]{1,0:T(8,128)(2,1)} %copy-done.1, ...), custom_call_target="tpu_custom_call" | custom-call | tf_op jit(solution)/shard_map/grads_out/pallas_call | solution.py:614
  168.1 226.9 %back.1 = (bf16[448,16,256]{2,1,0:T(8,128)(2,1)}, bf16[1440,16,256]{2,1,0:T(8,128)(2,1)}, f32[512,768]{1,0:T(8,128)}, f32[8,768]{1,0:T(8,128)}) custom-call(s32[16,16]{1,0:T(8,128)} %bitcast.54, f32[12]{0:T(128)} %bias_ref.3, bf16[8,2,64,512]{3,2,1,0:T(8,128)(2,1)} %get-tuple-element.31.dmixed_ref, f32[8,2,8,512]{3,2,1,0:T(8,128)} %get-tuple-element.32.logits_ref, ...), custom_call_target="tpu_custom_call" | custom-call | tf_op jit(solution)/shard_map/back/pallas_call | solution.py:1383
  395.1 1.2 slice_bitcast_fusion
  396.3 1.5 slice_reduce_fusion
  397.8 0.9 slice.34
  399.5 3.3 unpack.5
  402.8 6.4 %unpack.4 = f32[768,3072]{1,0:T(8,128)} custom-call(bf16[448,16,256]{2,1,0:T(8,128)(2,1)} %get-tuple-element.42.refs_0_, bf16[1440,16,256]{2,1,0:T(8,128)(2,1)} %get-tuple-element.43.refs_1_.refs_0_), custom_call_target="tpu_custom_call" | custom-call | tf_op jit(solution)/shard_map/unpack/pallas_call | solution.py:1214
  409.1 4.9 %unpack.7 = f32[2048,768]{1,0:T(8,128)} custom-call(bf16[1440,16,256]{2,1,0:T(8,128)(2,1)} %get-tuple-element.43.refs_1_.refs_0_), custom_call_target="tpu_custom_call" | custom-call | tf_op jit(solution)/shard_map/unpack/pallas_call | solution.py:1214
  414.0 8.9 %unpack.6 = f32[768,4096]{1,0:T(8,128)} custom-call(bf16[1440,16,256]{2,1,0:T(8,128)(2,1)} %get-tuple-element.43.refs_1_.refs_0_), custom_call_target="tpu_custom_call" | custom-call | tf_op jit(solution)/shard_map/unpack/pallas_call | solution.py:1214
  423.0 1.1 copy.38
  (47 shorter events, 4.2 us)
Async XLA Ops:
  4.6 0.8 copy-start.6
  5.3 104.1 %copy-start.5 = (bf16[1,512,768]{2,1,0:T(8,128)(2,1)S(1)}, bf16[1,512,768]{2,1,0:T(8,128)(2,1)}, u32[]{:S(2)}) copy-start(bf16[1,512,768]{2,1,0:T(8,128)(2,1)} %param.13) | copy-start | bytes 2359300
  5.3 106.8 %slice-start = ((s8[6291456]{0:T(1024)(128)(4,1)}), s8[2097152]{0:T(1024)(128)(4,1)S(1)}, s32[]{:S(2)}) async-start(s8[6291456]{0:T(1024)(128)(4,1)} %bitcast.42), calls=%async_computation | async-start | bytes 4194304
  107.2 5.0 %slice-start.1 = ((s8[6291456]{0:T(1024)(128)(4,1)}), s8[4194304]{0:T(1024)(128)(4,1)S(1)}, s32[]{:S(2)}) async-start(s8[6291456]{0:T(1024)(128)(4,1)} %bitcast.42), calls=%async_computation.1 | async-start | bytes 8388608
  109.4 2.5 copy-start.4
  109.4 2.5 copy-start.10
  112.2 3.5 copy-start.1
  112.2 3.5 copy-start.2
  112.2 3.5 copy-start.11
  125.4 6.7 %copy-start = (bf16[512,4096]{1,0:T(8,128)(2,1)}, bf16[512,4096]{1,0:T(8,128)(2,1)S(1)}, u32[]{:S(2)}) copy-start(bf16[512,4096]{1,0:T(8,128)(2,1)S(1)} %add_convert_fusion.dgu_ref) | copy-start | bytes 12582916
  135.7 1.6 copy-start.7
  135.7 2.1 copy-start.9
  135.8 2.5 copy-start.12
  137.4 3.2 copy-start.3
  414.0 8.9 %copy-start.8 = (f32[512,768]{1,0:T(8,128)S(1)}, f32[512,768]{1,0:T(8,128)}, u32[]{:S(2)}) copy-start(f32[512,768]{1,0:T(8,128)} %get-tuple-element.40) | copy-start | bytes 4718596

commit v8 on v7

--- a/solution.py
+++ b/solution.py
@@ -872,7 +872,7 @@
     return [kinds[i] for i in (EARLY_KINDS if busy else (0, 1, 2, 0, 1, 3))]
 
 
-EARLY_KINDS = (0, 1, 2, 0, 1, 3)
+EARLY_KINDS = (0, 1, 3, 0, 1, 2)
 PARTS = 6
 
 
@@ -997,7 +997,7 @@
         dsmall_ref[8 * head : 8 * head + 8] = total([logit_ref[d, s] for d, s in held])
 
 
-def late_weights(h_ref, proj_ref, g_ref):
+def late_weights(h_ref, proj_ref, g_ref, low, high):
     def block(i, carried):
         grads = proj_ref[pl.ds(pl.multiple_of(i * 256, 256), 256)]
         for j in range(3):
@@ -1005,7 +1005,7 @@
             g_ref[pl.ds(i * (D // UNIT) + j * 16, 16)] = part.astype(bf16).reshape(16, UNIT, 256)
         return carried
 
-    lax.fori_loop(0, 9, block, 0)
+    lax.fori_loop(low, high, block, 0)
 
 
 def late_rest(h_ref, proj_ref, w_ref, wsmall_ref, x_ref, gain_ref, dresid_ref, extra_ref, dsmall_ref, rows_ref, small_ref, dx_ref, g_ref, gsum_ref=None):
@@ -1074,11 +1074,15 @@
     small_out[...] = small.own[...]
 
 
-def give_late(sums, rest, early, stages):
-    units = 9 * (D // UNIT)
-    ahead = [part for part in sums if part.start + part.size <= units]
+def give_late(sums, weights, rest, early, stages):
+    block, blocks, given = D // UNIT, 9, 0
+    ahead = [part for part in sums if part.start + part.size <= blocks * block]
     for part in ahead:
+        needed = -(-(part.start + part.size) // block)
+        weights(given, needed)
+        given = needed
         part.give()
+    weights(given, blocks)
     rest()
     for part in sums[len(ahead):]:
         part.give()
@@ -1137,13 +1141,12 @@
     put_together(holders, part_ref, logit_ref, proj_ref, dsmall_ref)
     proj_ref[3 * D :] = dgate_ref[...]
 
-    late_weights(h_ref, proj_ref, g_ref)
     late = sums_of(g_ref.shape[0], least, sets, None, g_ref, land_ref, late_out, gsend, grecv, gsem)
 
     def rest():
         late_rest(h_ref, proj_ref, w_ref, wsmall_ref, x_ref, gain_ref, dresid_ref, extra_ref, dsmall_ref, rows_ref, small_ref, dx_ref, g_ref)
 
-    give_late(late, rest, early, stages)
+    give_late(late, functools.partial(late_weights, h_ref, proj_ref, g_ref), rest, early, stages)
     finish_late(late, early, 2 * stages - 3, stages, Doubling(bits, small_ref, small_land, ssend, srecv), small_out)
 
 
@@ -1356,13 +1359,12 @@
             pl.when(me != d)(copy.wait_recv)
 
     put_together(holders, part_ref, logit_ref, proj_ref, dsmall_ref)
-    late_weights(h_ref, proj_ref, g_ref)
     late = sums_of(g_ref.shape[0], least, sets, None, g_ref, land_ref, late_out, gsend, grecv, gsem)
 
     def rest():
         late_rest(h_ref, proj_ref, w_ref, wsmall_ref, x_ref, gain_ref, dresid_ref, extra_ref, dsmall_ref, rows_ref, small_ref, dx_ref, g_ref, gsum_ref)
 
-    give_late(late, rest, early, stages)
+    give_late(late, functools.partial(late_weights, h_ref, proj_ref, g_ref), rest, early, stages)
     finish_late(late, early, 2 * stages - 8 - LATER, stages, Doubling(bits, small_ref, small_land, ssend, srecv), small_out)
 
 

time: 425 us -> 432 us (1.016); the launches traced: 424 us -> 424 us
  no operation moved by 1% of the time
where the time goes in v8:
time: 432 us; the launch traced here: 424 us
  Pallas kernels  378 us (88%)
  matrix products  24.3 us (6%)
  local copies, waits for them, and re-layouts  10.4 us (2%)
  other arithmetic  9.5 us (2%)
    pallas_call x1, Pallas kernels, back(): pl.pallas_call(functools.partial(back_kernel, count, sets), out_shape=[ja...  226 us
    pallas_call x1, Pallas kernels, front(): pl.pallas_call(functools.partial(front_kernel, count), out_shape=[jax.Sha...  102 us
    pallas_call x1, Pallas kernels, grads_out(): pl.pallas_call(functools.partial(grads_out_kernel, count), out_shape=[jax...  26.9 us
    dot_general x6, matrix products, dot(): lax.dot_general(a, b, (((i,), (j,)), ((), ())), preferred_element_type=f32)  24.3 us
    pallas_call x4, Pallas kernels, unpack(): pl.pallas_call(functools.partial(unpack_kernel, [blocks // width for _, _...  23.5 us

profile of v8, /device:TPU:0, one launch (start us, length us, event | category | flops | bytes accessed | tf_op | source)
XLA Modules:
  0.0 423.9 jit_solution(15635843822149843078)
XLA Ops:
  0.8 0.7 stack.9
  1.5 0.7 stack.10
  3.6 1.0 copy.29.wsmall_ref
  4.6 0.7 pad.12.wsmall_ref
  5.3 101.8 %front.1 = (bf16[512,768]{1,0:T(8,128)(2,1)}, f32[768,512]{1,0:T(8,128)}, bf16[768,512]{1,0:T(8,128)(2,1)}, bf16[8,3,2,64,512]{4,3,2,1,0:T(8,128)(2,1)}, f32[8,2...) custom-call(s32[16,16]{1,0:T(8,128)} %bitcast.53, ...), custom_call_target="tpu_custom_call" | custom-call | tf_op jit(solution)/shard_map/front/pallas_call | solution.py:811
  107.1 2.2 fusion.3.gated_ref
  109.4 2.5 multiply_reduce_fusion.2
  112.2 3.4 fusion.16
  115.7 5.7 %fusion.10 = (f32[512,2048]{1,0:T(8,128)}, f32[512,2048]{1,0:T(8,128)}, bf16[512,2048]{1,0:T(8,128)(2,1)}) fusion(f32[512,4096]{1,0:T(8,128)S(1)} %fusion.16, bf16[2048,768]{1,0:T(8,128)(2,1)S(1)} %copy-done.11, bf16[1,512,768]{2,1,0:T(8,128)(2,1)S(1)} %copy-done.2), kind=kOutput, calls=%fused_computation.25 | convolution fusion | flops 1625292800 | bytes 22806528 | tf_op jit(solution)/shard_map/dot_general | solution.py:629
  121.4 4.1 add_convert_fusion.dgu_ref
  125.5 6.7 %fusion.9 = bf16[1,512,768]{2,1,0:T(8,128)(2,1)} fusion(f32[512,768]{1,0:T(8,128)S(1)} %get-tuple-element.58, bf16[512,2048]{1,0:T(8,128)(2,1)} %get-tuple-element.54.hidden_ref, bf16[2048,768]{1,0:T(8,128)(2,1)} %param.25), kind=kOutput, calls=%fused_computation.24 | convolution fusion | flops 1611399168 | bytes 7602176 | tf_op jit(solution)/shard_map/dot_general | solution.py:629
  132.2 3.6 multiply_reduce_fusion
  135.9 1.6 fusion.14
  138.4 2.3 fusion.6
  141.4 26.9 %grads_out.1 = (bf16[8,2,64,512]{3,2,1,0:T(8,128)(2,1)}, bf16[1440,16,256]{2,1,0:T(8,128)(2,1)}) custom-call(bf16[12,64,512]{2,1,0:T(8,128)(2,1)} %bitcast.48, bf16[512,768]{1,0:T(8,128)(2,1)} %get-tuple-element.30.h1_ref.h_in, bf16[768,512]{1,0:T(8,128)(2,1)} %get-tuple-element.55.dgate_ref.dgate_in, bf16[512,768]{1,0:T(8,128)(2,1)} %copy-done.1, ...), custom_call_target="tpu_custom_call" | custom-call | tf_op jit(solution)/shard_map/grads_out/pallas_call | solution.py:614
  168.4 226.0 %back.1 = (bf16[448,16,256]{2,1,0:T(8,128)(2,1)}, bf16[1440,16,256]{2,1,0:T(8,128)(2,1)}, f32[512,768]{1,0:T(8,128)}, f32[8,768]{1,0:T(8,128)}) custom-call(s32[16,16]{1,0:T(8,128)} %bitcast.54, f32[12]{0:T(128)} %bias_ref.3, bf16[8,2,64,512]{3,2,1,0:T(8,128)(2,1)} %get-tuple-element.31.dmixed_ref, f32[8,2,8,512]{3,2,1,0:T(8,128)} %get-tuple-element.32.logits_ref, ...), custom_call_target="tpu_custom_call" | custom-call | tf_op jit(solution)/shard_map/back/pallas_call | solution.py:1385
  394.4 1.2 slice_bitcast_fusion
  395.6 1.5 slice_reduce_fusion
  397.1 0.9 slice.34
  398.8 3.3 unpack.5
  402.1 6.4 %unpack.4 = f32[768,3072]{1,0:T(8,128)} custom-call(bf16[448,16,256]{2,1,0:T(8,128)(2,1)} %get-tuple-element.42.refs_0_, bf16[1440,16,256]{2,1,0:T(8,128)(2,1)} %get-tuple-element.43.refs_1_.refs_0_), custom_call_target="tpu_custom_call" | custom-call | tf_op jit(solution)/shard_map/unpack/pallas_call | solution.py:1217
  408.5 4.9 %unpack.7 = f32[2048,768]{1,0:T(8,128)} custom-call(bf16[1440,16,256]{2,1,0:T(8,128)(2,1)} %get-tuple-element.43.refs_1_.refs_0_), custom_call_target="tpu_custom_call" | custom-call | tf_op jit(solution)/shard_map/unpack/pallas_call | solution.py:1217
  413.4 8.9 %unpack.6 = f32[768,4096]{1,0:T(8,128)} custom-call(bf16[1440,16,256]{2,1,0:T(8,128)(2,1)} %get-tuple-element.43.refs_1_.refs_0_), custom_call_target="tpu_custom_call" | custom-call | tf_op jit(solution)/shard_map/unpack/pallas_call | solution.py:1217
  422.3 1.1 copy.38
  (47 shorter events, 4.2 us)
Async XLA Ops:
  4.6 0.8 copy-start.6
  5.3 104.1 %copy-start.5 = (bf16[1,512,768]{2,1,0:T(8,128)(2,1)S(1)}, bf16[1,512,768]{2,1,0:T(8,128)(2,1)}, u32[]{:S(2)}) copy-start(bf16[1,512,768]{2,1,0:T(8,128)(2,1)} %param.13) | copy-start | bytes 2359300
  5.3 106.8 %slice-start = ((s8[6291456]{0:T(1024)(128)(4,1)}), s8[2097152]{0:T(1024)(128)(4,1)S(1)}, s32[]{:S(2)}) async-start(s8[6291456]{0:T(1024)(128)(4,1)} %bitcast.42), calls=%async_computation | async-start | bytes 4194304
  107.1 5.0 %slice-start.1 = ((s8[6291456]{0:T(1024)(128)(4,1)}), s8[4194304]{0:T(1024)(128)(4,1)S(1)}, s32[]{:S(2)}) async-start(s8[6291456]{0:T(1024)(128)(4,1)} %bitcast.42), calls=%async_computation.1 | async-start | bytes 8388608
  109.4 2.5 copy-start.4
  109.4 2.5 copy-start.10
  112.2 3.5 copy-start.1
  112.2 3.5 copy-start.2
  112.2 3.5 copy-start.11
  125.5 6.7 %copy-start = (bf16[512,4096]{1,0:T(8,128)(2,1)}, bf16[512,4096]{1,0:T(8,128)(2,1)S(1)}, u32[]{:S(2)}) copy-start(bf16[512,4096]{1,0:T(8,128)(2,1)S(1)} %add_convert_fusion.dgu_ref) | copy-start | bytes 12582916
  135.9 1.6 copy-start.7
  135.9 2.1 copy-start.9
  135.9 2.5 copy-start.12
  137.5 3.2 copy-start.3
  413.4 8.9 %copy-start.8 = (f32[512,768]{1,0:T(8,128)S(1)}, f32[512,768]{1,0:T(8,128)}, u32[]{:S(2)}) copy-start(f32[512,768]{1,0:T(8,128)} %get-tuple-element.40) | copy-start | bytes 4718596
